TPU v7x, 256 devices: a whole 4x4x8 slice. The times are simulated.
256 devices in a mesh: chan: 128 (over y, z, x_lo, core), tm: 2 (over x_hi).
Axes of the slice: x: 4 (x_hi: 2, x_lo: 2; x = x_hi * 2 + x_lo), y: 4, z: 8, core: 2. Of those that a mesh axis runs over, the one named last changes fastest.
Arguments:
- traces: float32 [4, 1024, 768], P('tm', 'chan'), may hold values from -6 to 6
- lengths: int32 [4], replicated, may hold values from 1 to 768, 2304 in all
- mask: int32 [1024], P('chan'), may hold values 0 or 1
Outputs:
- correlations: float32 [1024, 1024, 256], P(('chan', 'tm'))
Inputs may be any that keep to these rules, and one draw needn't show every extreme that they name: `lengths`: live samples of each sub-window; together they hold 2304 samples and the longest holds exactly 768.
All inputs are finite; a program needn't handle non-finite values. No bound on the sum of `mask` on one device may be relied on, other than what follows from the above.
Results may differ from a plain program's by a relative error of at most 0.0043.
Values may be sent and summed in bfloat16 or wider, within the bound.
No kernel may reach another device: no remote copies, remote signals or barrier semaphores. Data moves between devices by JAX's collectives and lax.ppermute only.
A program may use at most 128 MiB of HBM per device.

v0:
```python
import math

import jax
import jax.numpy as jnp
from jax import lax
from jax.sharding import PartitionSpec as P

NFFT = 1024
LAG = 128
F = 512


def dft_table(seg_len, nfft, nfreq):
    sample_idx = jnp.arange(seg_len, dtype=jnp.int32)
    freq_idx = jnp.arange(nfreq, dtype=jnp.int32)
    product = jnp.mod(sample_idx[:, None] * freq_idx[None, :], nfft).astype(jnp.float32)
    theta = product * (2.0 * math.pi / nfft)
    return jnp.concatenate([jnp.cos(theta), -jnp.sin(theta)], axis=1)


def lag_table(nfft, nfreq, max_lag, sub_total):
    freq_idx = jnp.arange(nfreq, dtype=jnp.int32)
    lag_idx = jnp.arange(2 * max_lag, dtype=jnp.int32) - max_lag
    product = jnp.mod(freq_idx[:, None] * lag_idx[None, :], nfft).astype(jnp.float32)
    phase = product * (2.0 * math.pi / nfft)
    weight = jnp.where(freq_idx == 0, 1.0, 2.0).astype(jnp.float32)[:, None] / math.sqrt(
        nfreq * sub_total
    )
    return jnp.concatenate([weight * jnp.cos(phase), -weight * jnp.sin(phase)], axis=0).astype(
        jnp.bfloat16
    )


def whiten_spectra(traces, lengths, mask):
    seg_len = traces.shape[2]
    live = (jnp.arange(seg_len, dtype=jnp.int32)[None, :] < lengths[:, None]).astype(jnp.float32)
    counted = lengths.astype(jnp.float32)
    average = jnp.sum(traces * live[:, None, :], axis=-1) / counted[:, None]
    centred = (traces - average[:, :, None]) * live[:, None, :]
    table = dft_table(seg_len, NFFT, F)
    spectrum = jnp.dot(
        centred.reshape(-1, seg_len),
        table,
        precision=lax.Precision.HIGHEST,
        preferred_element_type=jnp.float32,
    )
    spectrum = spectrum.reshape(traces.shape[0], traces.shape[1], 2 * F)
    power = spectrum[..., :F] ** 2 + spectrum[..., F:] ** 2
    level = jnp.mean(power, axis=-1, keepdims=True)
    factor = 1.0 / jnp.sqrt(power + 0.01 * level + 1e-06)
    factor = jnp.concatenate([factor, factor], axis=-1)
    return (spectrum * factor * mask.astype(jnp.float32)[None, :, None]).astype(jnp.bfloat16)


def cross_spectrum(own_spec, other_spec):
    nfreq = own_spec.shape[-1] // 2
    own_re = own_spec[..., :nfreq]
    own_im = own_spec[..., nfreq:]
    other_re = other_spec[..., :nfreq]
    other_im = other_spec[..., nfreq:]
    real_part = jnp.einsum(
        "kif,kjf->ijf", own_re, other_re, preferred_element_type=jnp.float32
    ) + jnp.einsum("kif,kjf->ijf", own_im, other_im, preferred_element_type=jnp.float32)
    imag_part = jnp.einsum(
        "kif,kjf->ijf", own_im, other_re, preferred_element_type=jnp.float32
    ) - jnp.einsum("kif,kjf->ijf", own_re, other_im, preferred_element_type=jnp.float32)
    return jnp.concatenate([real_part, imag_part], axis=-1).astype(jnp.bfloat16)


def place_lags(running, own_spec, incoming, begin_col, lag_matrix):
    column_count = incoming.shape[1]
    slab_cols = 128

    def one_slab(slab, offset, current):
        half_spectra = cross_spectrum(own_spec, slab)
        lag_values = jnp.dot(
            half_spectra.reshape(-1, half_spectra.shape[-1]),
            lag_matrix,
            preferred_element_type=jnp.float32,
        )
        lag_values = lag_values.reshape(own_spec.shape[1], slab.shape[1], lag_matrix.shape[1])
        return lax.dynamic_update_slice(
            current, lag_values, (jnp.int32(0), jnp.asarray(offset, jnp.int32), jnp.int32(0))
        )

    def loop_body(slab_index, current):
        slab = lax.dynamic_slice_in_dim(incoming, slab_index * slab_cols, slab_cols, 1)
        return one_slab(slab, begin_col + slab_index * slab_cols, current)

    return lax.fori_loop(0, column_count // slab_cols, loop_body, running)


def local(traces, lengths, mask):
    sub_count = traces.shape[0]
    own_rows = traces.shape[1]
    time_groups = lax.axis_size("tm")
    local_lengths = lax.dynamic_slice_in_dim(lengths, lax.axis_index("tm") * sub_count, sub_count)
    spectra = whiten_spectra(traces, local_lengths, mask)
    lag_matrix = lag_table(NFFT, F, LAG, sub_count * time_groups)
    channel_total = own_rows * lax.axis_size("chan")
    empty_lags = jnp.zeros((own_rows, channel_total, 2 * LAG), jnp.float32)
    partial_lags = place_lags(
        empty_lags,
        spectra,
        lax.all_gather(spectra, "chan", axis=1, tiled=True),
        jnp.int32(0),
        lag_matrix,
    )
    return lax.psum_scatter(partial_lags, "tm", scatter_dimension=0, tiled=True)


def solution(mesh):
    placed = (P("tm", "chan", None), P(), P("chan"))
    return jax.shard_map(
        local, mesh=mesh, in_specs=placed, out_specs=P(("chan", "tm"), None, None), check_vma=False
    )
```

profile of v0, /device:TPU:1, one launch (start us, length us, event | category | flops | bytes accessed | tf_op | source)
XLA Modules:
  0.0 562.4 jit_solution(10639168242448990964)
XLA Ops:
  6.5 6.2 %sine_negate_fusion = (f32[768,512]{1,0:T(8,128)S(1)}, f32[768,512]{1,0:T(8,128)S(1)}) fusion(), kind=kLoop, calls=%fused_computation.23 | loop fusion | flops 5898240 | bytes 3145728 | tf_op jit(solution)/shard_map/neg | solution.py:18
  15.8 2.3 multiply_convert_fusion.1
  19.0 216.1 %all-gather.2.cloned.1.call-done = bf16[2,1024,1024]{2,1,0:T(8,128)(2,1)} async-done(((bf16[2,8,1024]{2,1,0:T(8,128)(2,1)}), bf16[2,1024,1024]{2,1,0:T(8,128)(2,1)}) %all-gather.2.cloned.1.call-update) | async-done | bytes 4194320 | tf_op jit(solution)/shard_map/all_gather | solution.py:105
  235.1 3.9 broadcast_in_dim.8
  239.0 211.6 %while.13 = (s32[]{:T(128)}, f32[8,1024,256]{2,1,0:T(8,128)}, bf16[2,1024,1024]{2,1,0:T(8,128)(2,1)}, bf16[2,8,1024]{2,1,0:T(8,128)(2,1)S(1)}, bf16[1024,256]{1,...) while((s32[]{:T(128)}, f32[8,1024,256]{2,1,0:T(8,128)}, ...), condition=%wide.region_3.4_spmd, body=%wide.region_2.3_spmd.sunk | while | flops 551550976 | bytes 44761288 | solution.py:90
  240.8 2.1 fusion.82
  244.9 2.1 fusion.79
  247.0 2.9 copy.22
  249.9 2.1 fusion.81
  252.0 3.0 copy.26
  255.0 2.1 fusion.80
  257.2 2.9 copy.25
  260.1 3.7 fusion.83
  267.2 2.1 fusion.82
  271.3 2.1 fusion.79
  273.4 2.9 copy.22
  276.3 2.1 fusion.81
  278.5 3.0 copy.26
  283.6 2.9 copy.25
  286.5 3.7 fusion.83
  293.7 2.1 fusion.82
  297.7 2.1 fusion.79
  299.9 2.9 copy.22
  302.8 2.1 fusion.81
  304.9 3.0 copy.26
  310.0 2.9 copy.25
  313.0 3.7 fusion.83
  320.1 2.1 fusion.82
  324.2 2.1 fusion.79
  326.3 2.9 copy.22
  329.3 2.1 fusion.81
  331.4 3.0 copy.26
  334.4 2.1 fusion.80
  336.5 2.9 copy.25
  339.4 3.7 fusion.83
  346.6 2.1 fusion.82
  350.6 2.1 fusion.79
  352.8 2.9 copy.22
  355.7 2.1 fusion.81
  357.8 3.0 copy.26
  362.9 2.9 copy.25
  365.9 3.7 fusion.83
  373.0 2.1 fusion.82
  377.1 2.1 fusion.79
  379.2 2.9 copy.22
  384.3 3.0 copy.26
  387.3 2.1 fusion.80
  389.4 2.9 copy.25
  392.3 3.7 fusion.83
  399.5 2.1 fusion.82
  403.5 2.1 fusion.79
  405.7 2.9 copy.22
  410.7 3.0 copy.26
  413.7 2.1 fusion.80
  415.8 2.9 copy.25
  418.8 3.7 fusion.83
  425.9 2.1 fusion.82
  430.0 2.1 fusion.79
  432.1 2.9 copy.22
  435.1 2.1 fusion.81
  437.2 3.0 copy.26
  442.3 2.9 copy.25
  445.2 3.7 fusion.83
  450.6 104.9 %reduce-scatter.2.cloned.1.call-done = f32[4,1024,256]{2,1,0:T(8,128)} async-done(((f32[8,1024,256]{2,1,0:T(8,128)}), f32[4,1024,256]{2,1,0:T(8,128)}) %reduce-scatter.2.cloned.1.call-update) | async-done | bytes 4194320 | tf_op jit(solution)/shard_map/reduce_scatter | solution.py:109
  (111 shorter events, 59.7 us)
Async XLA Ops:
  6.5 6.2 %copy-start.4 = (s32[8]{0:T(128)S(1)}, s32[8]{0:T(128)}, u32[]{:S(2)}) copy-start(s32[8]{0:T(128)} %param.7) | copy-start | bytes 100
  6.5 6.2 %copy-start.3 = (s32[4]{0:T(128)S(1)}, s32[4]{0:T(128)}, u32[]{:S(2)}) copy-start(s32[4]{0:T(128)} %param.6) | copy-start | bytes 52
  6.5 6.4 %copy-start.2 = (f32[2,8,768]{2,1,0:T(8,128)S(1)}, f32[2,8,768]{2,1,0:T(8,128)}, u32[]{:S(2)}) copy-start(f32[2,8,768]{2,1,0:T(8,128)} %param.5) | copy-start | bytes 147460
  6.5 228.5 %all-gather.2.cloned.1.call-start = ((), (), s32[]{:S(2)}) async-start(), calls=%async_computation.1 | async-start | bytes 4227072 | tf_op jit(solution)/shard_map/all_gather | solution.py:105
  15.6 539.9 %reduce-scatter.2.cloned.1.call-start = ((), (), s32[]{:S(2)}) async-start(), calls=%async_computation.2 | async-start | bytes 12582912 | tf_op jit(solution)/shard_map/reduce_scatter | solution.py:109
  19.0 220.0 %copy-start = (bf16[2,8,1024]{2,1,0:T(8,128)(2,1)S(1)}, bf16[2,8,1024]{2,1,0:T(8,128)(2,1)}, u32[]{:S(2)}) copy-start(bf16[2,8,1024]{2,1,0:T(8,128)(2,1)} %fusion.28) | copy-start | bytes 98308
  260.1 3.7 copy-start.1
  286.5 3.7 copy-start.1
  313.0 3.7 copy-start.1
  339.4 3.7 copy-start.1
  365.9 3.7 copy-start.1
  392.3 3.7 copy-start.1
  418.8 3.7 copy-start.1
  445.2 3.7 copy-start.1
Sparse Core Ops, SparseCore 0:
  15.7 219.3 all-gather.1
  450.8 104.7 reduce-scatter.1
where the time goes:
time: 563 us; the launch traced here: 562 us
  waiting for transfers between devices  321 us (57%)
  local copies, waits for them, and re-layouts  104 us (18%)
  matrix products  83.3 us (15%)
  other arithmetic  39.8 us (7%)
  between operations  13.5 us (2%)
    all_gather x1, waiting for transfers between devices, local(): lax.all_gather(spectra, 'chan', axis=1, tiled=True)  216 us
    reduce_scatter x1, waiting for transfers between devices, local(): return lax.psum_scatter(partial_lags, 'tm', scatter_dimension=0, tiled=True)  105 us
    add x8, other arithmetic, cross_spectrum(): jnp.einsum('kif,kjf->ijf', own_re, other_re, preferred_element_type=jnp.f...  29.3 us
    dot_general x8, local copies, waits for them, and re-layouts, cross_spectrum(): jnp.einsum('kif,kjf->ijf', own_im, other_re, preferred_element_type=jnp.f...  24 us
    dot_general x8, local copies, waits for them, and re-layouts, cross_spectrum(): jnp.einsum('kif,kjf->ijf', own_im, other_im, preferred_element_type=jnp.f...  23.5 us
    dot_general x8, local copies, waits for them, and re-layouts, cross_spectrum(): jnp.einsum('kif,kjf->ijf', own_re, other_re, preferred_element_type=jnp.f...  23.4 us
    dot_general x8, matrix products, cross_spectrum(): jnp.einsum('kif,kjf->ijf', own_re, other_im, preferred_element_type=jnp.f...  17 us
    dot_general x8, matrix products, cross_spectrum(): jnp.einsum('kif,kjf->ijf', own_re, other_re, preferred_element_type=jnp.f...  17 us
  transfers between devices with their start and end apart: 2, of which 2 were waited for; matrix products, arithmetic and copies ran while one was open for 1% of the time, Pallas kernels for 0%

commit v1 on v0

v1 whole, which is shorter than its diff:
```python
import math

import jax
import jax.numpy as jnp
import ml_dtypes
import numpy as np
from jax import lax
from jax.experimental import pallas as pl
from jax.experimental.pallas import tpu as pltpu
from jax.sharding import Mesh
from jax.sharding import PartitionSpec as P

NFFT = 1024
LAG = 128
F = 512
SEG = 768
SUBWIN = 4
NY, NZ, NX = 4, 8, 4
AXES = ("y", "z", "xl", "core", "tm")
VMEM_LIMIT = 60 * 2**20


def dft_tables():
    product = np.mod(np.arange(SEG)[:, None] * np.arange(F)[None, :], NFFT)
    theta = product * (2.0 * math.pi / NFFT)
    table = np.concatenate([np.cos(theta), -np.sin(theta)], axis=1)
    high = table.astype(ml_dtypes.bfloat16)
    low = (table - high.astype(np.float64)).astype(ml_dtypes.bfloat16)
    return high, low


def lag_table():
    product = np.mod(np.arange(F)[:, None] * (np.arange(2 * LAG) - LAG)[None, :], NFFT)
    phase = product * (2.0 * math.pi / NFFT)
    weight = np.where(np.arange(F) == 0, 1.0, 2.0)[:, None] / math.sqrt(F * SUBWIN)
    table = np.concatenate([weight * np.cos(phase), -weight * np.sin(phase)], axis=0)
    return table.astype(np.float32).astype(ml_dtypes.bfloat16)


def device_index(y, z, x, core):
    return (((y * NZ + z) * 2 + x % 2) * 2 + core) * 2 + x // 2


def permute(value, partner):
    pairs = []
    for y in range(NY):
        for z in range(NZ):
            for x in range(NX):
                for core in range(2):
                    pairs.append((device_index(y, z, x, core), device_index(*partner(y, z, x, core))))
    return lax.ppermute(value, AXES, pairs)


def along_z(d):
    return lambda y, z, x, core: (y, z ^ d, x, core)


def along_first(d):
    return lambda y, z, x, core: (y ^ d, z, x, core) if core == 0 else (y, z, x ^ d, core)


def along_second(d):
    return lambda y, z, x, core: (y, z, x ^ d, core) if core == 0 else (y ^ d, z, x, core)


def other_core(y, z, x, core):
    return (y, z, x, 1 - core)


def other_group(y, z, x, core):
    return (y, z, x ^ 2, core)


def whiten_kernel(lengths_ref, mask_ref, traces_ref, high_ref, low_ref, out_ref):
    tm = lax.axis_index("tm")
    x = traces_ref[...].reshape(16, SEG)
    row = lax.broadcasted_iota(jnp.int32, (16, 1), 0)
    length = jnp.where(row < 8, lengths_ref[2 * tm], lengths_ref[2 * tm + 1])
    usable = jnp.zeros((16, 1), jnp.float32)
    for c in range(8):
        usable = jnp.where(row % 8 == c, mask_ref[c].astype(jnp.float32), usable)
    live = lax.broadcasted_iota(jnp.int32, (16, SEG), 1) < length
    average = jnp.sum(jnp.where(live, x, 0.0), axis=1, keepdims=True) / length.astype(jnp.float32)
    centred = jnp.where(live, x - average, 0.0)
    part0 = centred.astype(jnp.bfloat16)
    rest = centred - part0.astype(jnp.float32)
    part1 = rest.astype(jnp.bfloat16)
    part2 = (rest - part1.astype(jnp.float32)).astype(jnp.bfloat16)
    parts = jnp.concatenate([part0, part1, part2], axis=0)
    by_high = jnp.dot(parts, high_ref[...], preferred_element_type=jnp.float32)
    by_low = jnp.dot(parts[:32], low_ref[...], preferred_element_type=jnp.float32)
    spectrum = by_high[:16] + (by_high[16:32] + by_low[:16] + (by_high[32:] + by_low[16:]))
    re, im = spectrum[:, :F], spectrum[:, F:]
    power = re * re + im * im
    level = jnp.mean(power, axis=1, keepdims=True)
    factor = usable / jnp.sqrt(power + 0.01 * level + 1e-06)
    for k in range(2):
        rows = slice(8 * k, 8 * k + 8)
        out_ref[:, 2 * k * F : (2 * k + 1) * F] = (re * factor)[rows].astype(jnp.bfloat16)
        out_ref[:, (2 * k + 1) * F : (2 * k + 2) * F] = (im * factor)[rows].astype(jnp.bfloat16)


def whiten(traces, lengths, mask):
    high, low = dft_tables()
    smem = pl.BlockSpec(memory_space=pltpu.SMEM)
    vmem = pl.BlockSpec(memory_space=pltpu.VMEM)
    return pl.pallas_call(
        whiten_kernel,
        in_specs=[smem, smem, vmem, vmem, vmem],
        out_specs=vmem,
        out_shape=jax.ShapeDtypeStruct((8, 4 * F), jnp.bfloat16),
        compiler_params=pltpu.CompilerParams(vmem_limit_bytes=VMEM_LIMIT),
        name="whiten",
    )(lengths, mask, traces, jnp.asarray(high), jnp.asarray(low))


def fold_kernel(own_ref, other_ref, lag_ref, out_ref, columns):
    tm = lax.axis_index("tm")
    own = own_ref[...].astype(jnp.float32)
    other = other_ref[...].astype(jnp.float32)
    rows = jnp.concatenate([own, other], axis=0)
    rows = jnp.where(tm == 0, jnp.concatenate([rows[0:4], rows[8:12]], axis=0), jnp.concatenate([rows[4:8], rows[12:16]], axis=0))
    columns[...] = rows.T
    step = 64

    @pl.loop(0, F, step=step)
    def _(begin):
        re_at = pl.ds(pl.multiple_of(begin, step), step)
        im_at = pl.ds(pl.multiple_of(begin + F, step), step)
        cos = lag_ref[re_at, :].astype(jnp.float32)
        sin = lag_ref[im_at, :].astype(jnp.float32)
        for group in range(2):
            for i in range(4):
                a_re = columns[re_at, 4 * group + i : 4 * group + i + 1]
                a_im = columns[im_at, 4 * group + i : 4 * group + i + 1]
                lanes = slice(2 * LAG * i, 2 * LAG * (i + 1))
                out_ref[group, 0, re_at, lanes] = (a_re * cos + a_im * sin).astype(jnp.bfloat16)
                out_ref[group, 0, im_at, lanes] = (a_im * cos - a_re * sin).astype(jnp.bfloat16)


def fold(own, other):
    folded = pl.pallas_call(
        fold_kernel,
        grid=(2,),
        in_specs=[
            pl.BlockSpec((8, 2 * F), lambda k: (0, k)),
            pl.BlockSpec((8, 2 * F), lambda k: (0, k)),
            pl.BlockSpec((2 * F, 2 * LAG), lambda k: (0, 0)),
        ],
        out_specs=pl.BlockSpec((2, 1, 2 * F, 8 * LAG), lambda k: (0, k, 0, 0)),
        out_shape=jax.ShapeDtypeStruct((2, 2, 2 * F, 8 * LAG), jnp.bfloat16),
        scratch_shapes=[pltpu.VMEM((2 * F, 8), jnp.float32)],
        compiler_params=pltpu.CompilerParams(vmem_limit_bytes=VMEM_LIMIT),
        name="fold",
    )(own, other, jnp.asarray(lag_table()))
    return folded.reshape(8 * F, 8 * LAG)


def correlate_kernel(*refs):
    mine, theirs, folded, out_ref = refs[0:4], refs[4:8], refs[8], refs[9]
    y, z, xl, core = (lax.axis_index(name) for name in ("y", "z", "xl", "core"))
    half = 4 * F

    def store(values, slot, e, kind):
        for g in range(NZ):
            out_ref[0, y ^ slot, z ^ g, xl ^ e, kind] = values[8 * g : 8 * g + 8]

    def product(first, second):
        return jnp.dot(first, folded[:half, :], preferred_element_type=jnp.float32) + jnp.dot(
            second, folded[half:, :], preferred_element_type=jnp.float32
        )

    def x_chunks(chunks):
        for e in range(2):
            values = product(chunks[e][...], chunks[e + 2][...])
            for slot in range(4):
                store(values[64 * slot : 64 * slot + 64], slot, e, 0)

    def y_chunks(chunks):
        for e in range(2):
            first = jnp.concatenate([chunks[b][64 * e : 64 * e + 64, :] for b in range(4)], axis=0)
            second = jnp.concatenate([chunks[b][64 * e + 128 : 64 * e + 192, :] for b in range(4)], axis=0)
            values = product(first, second)
            for slot in range(4):
                store(values[64 * slot : 64 * slot + 64], slot, e, 1)

    @pl.when(core == 0)
    def _():
        x_chunks(mine)
        y_chunks(theirs)

    @pl.when(core == 1)
    def _():
        y_chunks(mine)
        x_chunks(theirs)


def correlate(mine, theirs, folded):
    whole = pl.BlockSpec((256, 4 * F), lambda i: (0, 0))
    out = pl.pallas_call(
        correlate_kernel,
        grid=(4,),
        in_specs=[whole] * 8 + [pl.BlockSpec((8 * F, 2 * LAG), lambda i: (0, i))],
        out_specs=pl.BlockSpec((1, NY, NZ, 2, 2, 8, 2 * LAG), lambda i: (i, 0, 0, 0, 0, 0, 0)),
        out_shape=jax.ShapeDtypeStruct((4, NY, NZ, 2, 2, 8, 2 * LAG), jnp.float32),
        compiler_params=pltpu.CompilerParams(vmem_limit_bytes=VMEM_LIMIT),
        name="correlate",
    )(*mine, *theirs, folded)
    return out.reshape(4, NY * NZ * 4 * 8, 2 * LAG)


def local(traces, lengths, mask):
    own = whiten(traces, lengths, mask)
    other = permute(own, other_group)
    folded = fold(own, other)
    ring = jnp.concatenate([own] + [permute(own, along_z(d)) for d in range(1, 8)], axis=0)
    plane = jnp.concatenate([ring] + [permute(ring, along_first(d)) for d in range(1, 4)], axis=0)
    mine = [plane] + [permute(plane, along_second(d)) for d in range(1, 4)]
    theirs = [permute(chunk, other_core) for chunk in mine]
    return correlate(mine, theirs, folded)


def solution(mesh):
    finer = Mesh(mesh.devices.reshape(NY, NZ, 2, 2, 2), AXES)
    chan = ("y", "z", "xl", "core")
    return jax.shard_map(
        local,
        mesh=finer,
        in_specs=(P("tm", chan, None), P(), P(chan)),
        out_specs=P(AXES, None, None),
        check_vma=False,
    )
```

time: 563 us -> 117 us (0.21)
  waiting for transfers between devices: 321 us -> 23.6 us
  local copies, waits for them, and re-layouts: 104 us -> 1.5 us
  matrix products: 83.3 us -> 0 us
  starting transfers between devices: 0.22 us -> 66.6 us
  other arithmetic: 39.8 us -> 0 us
  Pallas kernels: 0 us -> 25 us
  between operations: 13.5 us -> 0.14 us
    all_gather x1 -> x0, waiting for transfers between devices: 216 us -> none  [local(): lax.all_gather(spectra, 'chan', axis=1, tiled=True)]
    reduce_scatter x1 -> x0, waiting for transfers between devices: 105 us -> none  [local(): return lax.psum_scatter(partial_lags, 'tm', scatter_dimension=0, tiled=True)]
    dot_general x32 -> x0, local copies, waits for them, and re-layouts: 86.3 us -> none  [the longest x8 24 us: cross_spectrum(): jnp.einsum('kif,kjf->ijf', own_im, other_re, preferred_element_type=jnp.f...]
    dot_general x41 -> x0, matrix products: 83.3 us -> none  [the longest x8 17 us: cross_spectrum(): jnp.einsum('kif,kjf->ijf', own_re, other_im, preferred_element_type=jnp.f...]
    ppermute x0 -> x18, starting transfers between devices: none -> 66.6 us  [permute(): return lax.ppermute(value, AXES, pairs)]
    add x8 -> x0, other arithmetic: 29.3 us -> none  [cross_spectrum(): jnp.einsum('kif,kjf->ijf', own_re, other_re, preferred_element_type=jnp.f...]
    pallas_call x0 -> x3, Pallas kernels: none -> 25 us  [the longest x1 14.6 us: correlate(): pl.pallas_call(correlate_kernel, grid=(4,), in_specs=[whole] * 8 + [pl.Bl...]
    ppermute x0 -> x18, waiting for transfers between devices: none -> 23.6 us  [permute(): return lax.ppermute(value, AXES, pairs)]
  transfers between devices with their start and end apart: 2 -> 18, of which waited for: 2 -> 8; matrix products, arithmetic and copies ran while one was open for 1% -> 1% of each run, Pallas kernels for 0% -> 6%
where the time goes in v1:
time: 117 us
  starting transfers between devices  66.6 us (57%)
  Pallas kernels  25 us (21%)
  waiting for transfers between devices  23.6 us (20%)
  local copies, waits for them, and re-layouts  1.5 us (1%)
    ppermute x18, starting transfers between devices, permute(): return lax.ppermute(value, AXES, pairs)  66.6 us
    ppermute x18, waiting for transfers between devices, permute(): return lax.ppermute(value, AXES, pairs)  23.6 us
    pallas_call x1, Pallas kernels, correlate(): pl.pallas_call(correlate_kernel, grid=(4,), in_specs=[whole] * 8 + [pl.Bl...  14.6 us
    pallas_call x1, Pallas kernels, fold(): pl.pallas_call(fold_kernel, grid=(2,), in_specs=[pl.BlockSpec((8, 2 * F),...  7.06 us
    pallas_call x1, Pallas kernels, whiten(): pl.pallas_call(whiten_kernel, in_specs=[smem, smem, vmem, vmem, vmem], ou...  3.31 us
  transfers between devices with their start and end apart: 18, of which 8 were waited for; matrix products, arithmetic and copies ran while one was open for 1% of the time, Pallas kernels for 6%

profile of v1, /device:TPU:1, one launch (start us, length us, event | category | flops | bytes accessed | tf_op | source)
XLA Modules:
  0.0 116.9 jit_solution(1696743185237888182)
XLA Ops:
  0.0 3.3 %whiten.1.own_ref = bf16[8,2048]{1,0:T(8,128)(2,1)} custom-call(s32[4]{0:T(128)} %lengths_ref.1, s32[8]{0:T(128)} %mask_ref.1, f32[2,8,768]{2,1,0:T(8,128)} %traces_ref.1, bf16[768,1024]{1,0:T(8,128)(2,1)} %constant.6.clone.high_ref, bf16[768,1024]{1,0:T(8,128)(2,1)} %constant.7.clone.low_ref), custom_call_target="tpu_custom_call" | custom-call | tf_op jit(solution)/shard_map/whiten/pallas_call | solution.py:107
  3.3 6.4 %collective-permute-start.6 = (bf16[8,2048]{1,0:T(8,128)(2,1)}, bf16[8,2048]{1,0:T(8,128)(2,1)S(1)}, u32[]{:S(2)}, u32[]{:S(2)}) collective-permute-start(bf16[8,2048]{1,0:T(8,128)(2,1)} %whiten.1.own_ref), channel_id=1, source_target_pairs={{0,56},{2,58},{4,60},{6,62},{1,57},{3,59},{5,61},{7,63},{8,48},{10... | collective-permute-start | bytes 98312 | tf_op jit(solution)/shard_map/ppermute | solution.py:51
  9.7 0.4 collective-permute-start.5
  10.2 3.6 %collective-permute-start.4 = (bf16[8,2048]{1,0:T(8,128)(2,1)}, bf16[8,2048]{1,0:T(8,128)(2,1)S(1)}, u32[]{:S(2)}, u32[]{:S(2)}) collective-permute-start(bf16[8,2048]{1,0:T(8,128)(2,1)} %whiten.1.own_ref), channel_id=1, source_target_pairs={{0,40},{2,42},{4,44},{6,46},{1,41},{3,43},{5,45},{7,47},{8,32},{10... | collective-permute-start | bytes 98312 | tf_op jit(solution)/shard_map/ppermute | solution.py:51
  13.7 1.8 %collective-permute-start.3 = (bf16[8,2048]{1,0:T(8,128)(2,1)}, bf16[8,2048]{1,0:T(8,128)(2,1)S(1)}, u32[]{:S(2)}, u32[]{:S(2)}) collective-permute-start(bf16[8,2048]{1,0:T(8,128)(2,1)} %whiten.1.own_ref), channel_id=1, source_target_pairs={{0,32},{2,34},{4,36},{6,38},{1,33},{3,35},{5,37},{7,39},{8,40},{10... | collective-permute-start | bytes 98312 | tf_op jit(solution)/shard_map/ppermute | solution.py:51
  15.5 0.3 collective-permute-start
  15.8 0.8 constant_dynamic-update-slice_fusion.7
  16.6 1.9 %collective-permute-done = bf16[8,2048]{1,0:T(8,128)(2,1)S(1)} collective-permute-done((bf16[8,2048]{1,0:T(8,128)(2,1)}, bf16[8,2048]{1,0:T(8,128)(2,1)S(1)}, u32[]{:S(2)}, u32[]{:S(2)}) %collective-permute-start) | collective-permute-done | bytes 32800 | tf_op jit(solution)/shard_map/ppermute | solution.py:51
  18.5 1.0 collective-permute-start.1
  19.6 3.3 %collective-permute-done.1 = bf16[8,2048]{1,0:T(8,128)(2,1)S(1)} collective-permute-done((bf16[8,2048]{1,0:T(8,128)(2,1)}, bf16[8,2048]{1,0:T(8,128)(2,1)S(1)}, u32[]{:S(2)}, u32[]{:S(2)}) %collective-permute-start.1) | collective-permute-done | bytes 32800 | tf_op jit(solution)/shard_map/ppermute | solution.py:51
  22.9 1.6 %collective-permute-start.2 = (bf16[8,2048]{1,0:T(8,128)(2,1)}, bf16[8,2048]{1,0:T(8,128)(2,1)S(1)}, u32[]{:S(2)}, u32[]{:S(2)}) collective-permute-start(bf16[8,2048]{1,0:T(8,128)(2,1)} %whiten.1.own_ref), channel_id=1, source_target_pairs={{0,24},{2,26},{4,28},{6,30},{1,25},{3,27},{5,29},{7,31},{8,16},{10... | collective-permute-start | bytes 98312 | tf_op jit(solution)/shard_map/ppermute | solution.py:51
  24.6 3.1 %collective-permute-done.2 = bf16[8,2048]{1,0:T(8,128)(2,1)S(1)} collective-permute-done((bf16[8,2048]{1,0:T(8,128)(2,1)}, bf16[8,2048]{1,0:T(8,128)(2,1)S(1)}, u32[]{:S(2)}, u32[]{:S(2)}) %collective-permute-start.2) | collective-permute-done | bytes 32800 | tf_op jit(solution)/shard_map/ppermute | solution.py:51
  27.7 0.0 collective-permute-done.3
  27.7 0.0 collective-permute-done.4
  27.8 0.0 collective-permute-done.5
  27.8 0.0 collective-permute-done.6
  27.8 1.3 %collective-permute-start.7 = (bf16[64,2048]{1,0:T(8,128)(2,1)S(1)}, bf16[64,2048]{1,0:T(8,128)(2,1)S(1)}, u32[]{:S(2)}, u32[]{:S(2)}) collective-permute-start(bf16[64,2048]{1,0:T(8,128)(2,1)S(1)} %get-tuple-element.5), channel_id=1, source_target_pairs={{0,64},{2,6},{4,68},{6,2},{1,65},{3,7},{5,69},{7,3},{8,72},{10,14}... | collective-permute-start | bytes 786440 | tf_op jit(solution)/shard_map/ppermute | solution.py:51
  29.1 2.4 %collective-permute-start.8 = (bf16[64,2048]{1,0:T(8,128)(2,1)S(1)}, bf16[64,2048]{1,0:T(8,128)(2,1)S(1)}, u32[]{:S(2)}, u32[]{:S(2)}) collective-permute-start(bf16[64,2048]{1,0:T(8,128)(2,1)S(1)} %get-tuple-element.5), channel_id=1, source_target_pairs={{0,128},{2,3},{4,132},{6,7},{1,129},{3,2},{5,133},{7,6},{8,136},{1... | collective-permute-start | bytes 786440 | tf_op jit(solution)/shard_map/ppermute | solution.py:51
  31.6 0.2 collective-permute-start.9
  31.8 1.4 %collective-permute-done.7 = bf16[64,2048]{1,0:T(8,128)(2,1)S(1)} collective-permute-done((bf16[64,2048]{1,0:T(8,128)(2,1)S(1)}, bf16[64,2048]{1,0:T(8,128)(2,1)S(1)}, u32[]{:S(2)}, u32[]{:S(2)}) %collective-permute-start.7) | collective-permute-done | bytes 262176 | tf_op jit(solution)/shard_map/ppermute | solution.py:51
  33.1 5.1 %collective-permute-done.8 = bf16[64,2048]{1,0:T(8,128)(2,1)S(1)} collective-permute-done((bf16[64,2048]{1,0:T(8,128)(2,1)S(1)}, bf16[64,2048]{1,0:T(8,128)(2,1)S(1)}, u32[]{:S(2)}, u32[]{:S(2)}) %collective-permute-start.8) | collective-permute-done | bytes 262176 | tf_op jit(solution)/shard_map/ppermute | solution.py:51
  38.2 2.6 %collective-permute-done.9 = bf16[64,2048]{1,0:T(8,128)(2,1)S(1)} collective-permute-done((bf16[64,2048]{1,0:T(8,128)(2,1)S(1)}, bf16[64,2048]{1,0:T(8,128)(2,1)S(1)}, u32[]{:S(2)}, u32[]{:S(2)}) %collective-permute-start.9) | collective-permute-done | bytes 262176 | tf_op jit(solution)/shard_map/ppermute | solution.py:51
  40.8 0.0 copy-start
  40.8 3.1 %collective-permute-start.12 = (bf16[256,2048]{1,0:T(8,128)(2,1)S(1)}, bf16[256,2048]{1,0:T(8,128)(2,1)S(1)}, u32[]{:S(2)}, u32[]{:S(2)}) collective-permute-start(bf16[256,2048]{1,0:T(8,128)(2,1)S(1)} %constant_dynamic-update-slice_fusion.8.refs_0_), channel_id=1, source_target_pairs={{0,5},{2,194},{4,1},{6,198},{1,4},{3,195},{5,0},{7,199},{8,13},{10... | collective-permute-start | bytes 3145736 | tf_op jit(solution)/shard_map/ppermute | solution.py:51
  43.9 0.2 collective-permute-start.11
  44.1 0.5 collective-permute-start.10
  44.6 20.6 %collective-permute-start.13 = (bf16[256,2048]{1,0:T(8,128)(2,1)S(1)}, bf16[256,2048]{1,0:T(8,128)(2,1)}, u32[]{:S(2)}, u32[]{:S(2)}) collective-permute-start(bf16[256,2048]{1,0:T(8,128)(2,1)S(1)} %constant_dynamic-update-slice_fusion.8.refs_0_), channel_id=1, source_target_pairs={{0,2},{2,0},{4,6},{6,4},{1,3},{3,1},{5,7},{7,5},{8,10},{10,8},{12,... | collective-permute-start | bytes 3145736 | tf_op jit(solution)/shard_map/ppermute | solution.py:51
  65.2 4.3 %collective-permute-done.12.refs_3_ = bf16[256,2048]{1,0:T(8,128)(2,1)S(1)} collective-permute-done((bf16[256,2048]{1,0:T(8,128)(2,1)S(1)}, bf16[256,2048]{1,0:T(8,128)(2,1)S(1)}, u32[]{:S(2)}, u32[]{:S(2)}) %collective-permute-start.12) | collective-permute-done | bytes 1048608 | tf_op jit(solution)/shard_map/ppermute | solution.py:51
  69.5 0.0 copy-start.1
  69.5 18.8 %collective-permute-start.16 = (bf16[256,2048]{1,0:T(8,128)(2,1)S(1)}, bf16[256,2048]{1,0:T(8,128)(2,1)}, u32[]{:S(2)}, u32[]{:S(2)}) collective-permute-start(bf16[256,2048]{1,0:T(8,128)(2,1)S(1)} %collective-permute-done.12.refs_3_), channel_id=1, source_target_pairs={{0,2},{2,0},{4,6},{6,4},{1,3},{3,1},{5,7},{7,5},{8,10},{10,8},{12,... | collective-permute-start | bytes 3145736 | tf_op jit(solution)/shard_map/ppermute | solution.py:51
  88.3 0.0 collective-permute-done.11.refs_2_
  88.3 0.0 copy-start.2
  88.3 0.1 collective-permute-start.15
  88.4 0.0 collective-permute-done.10.refs_1_
  88.4 1.0 collective-permute-start.14
  89.4 3.2 %collective-permute-start.17 = (bf16[8,2048]{1,0:T(8,128)(2,1)}, bf16[8,2048]{1,0:T(8,128)(2,1)S(1)}, u32[]{:S(2)}, u32[]{:S(2)}) collective-permute-start(bf16[8,2048]{1,0:T(8,128)(2,1)} %whiten.1.own_ref), channel_id=1, source_target_pairs={{0,1},{2,3},{4,5},{6,7},{1,0},{3,2},{5,4},{7,6},{8,9},{10,11},{12,... | collective-permute-start | bytes 98312 | tf_op jit(solution)/shard_map/ppermute | solution.py:51
  92.6 1.9 %collective-permute-done.17.other_ref = bf16[8,2048]{1,0:T(8,128)(2,1)S(1)} collective-permute-done((bf16[8,2048]{1,0:T(8,128)(2,1)}, bf16[8,2048]{1,0:T(8,128)(2,1)S(1)}, u32[]{:S(2)}, u32[]{:S(2)}) %collective-permute-start.17) | collective-permute-done | bytes 32800 | tf_op jit(solution)/shard_map/ppermute | solution.py:51
  94.6 0.0 copy-start.3
  94.6 0.6 copy-done.3
  95.2 7.1 %fold.1 = bf16[2,2,1024,1024]{3,2,1,0:T(8,128)(2,1)} custom-call(bf16[8,2048]{1,0:T(8,128)(2,1)} %whiten.1.own_ref, bf16[8,2048]{1,0:T(8,128)(2,1)} %copy-done.3, bf16[1024,256]{1,0:T(8,128)(2,1)} %constant.8.clone.lag_ref), custom_call_target="tpu_custom_call" | custom-call | tf_op jit(solution)/shard_map/fold/pallas_call | solution.py:142
  102.2 0.0 copy-done
  102.2 0.0 copy-done.1
  102.2 0.0 copy-done.2
  102.2 0.0 collective-permute-done.13.refs_4_
  102.3 0.0 collective-permute-done.16.refs_7_
  102.3 0.0 collective-permute-done.15.refs_6_
  102.3 0.0 collective-permute-done.14.refs_5_
  102.3 14.6 %correlate.1 = f32[4,4,8,2,2,8,256]{6,5,4,3,2,1,0:T(8,128)} custom-call(bf16[256,2048]{1,0:T(8,128)(2,1)} %copy-done, bf16[256,2048]{1,0:T(8,128)(2,1)} %collective-permute-done.10.refs_1_, bf16[256,2048]{1,0:T(8,128)(2,1)} %copy-done.2, bf16[256,2048]{1,0:T(8,128)(2,1)} %copy-done.1, bf16[256,2048]{1,0:T(8,128)(2,1)} %collective-permute-done.13.refs_4_, ...), custom_call_target="tpu_custom_call" | custom-call | tf_op jit(solution)/shard_map/correlate/pallas_call | solution.py:200
  (10 shorter events, 0.1 us)
Async XLA Ops:
  3.3 24.5 %collective-permute-start.6 = (bf16[8,2048]{1,0:T(8,128)(2,1)}, bf16[8,2048]{1,0:T(8,128)(2,1)S(1)}, u32[]{:S(2)}, u32[]{:S(2)}) collective-permute-start(bf16[8,2048]{1,0:T(8,128)(2,1)} %whiten.1.own_ref), channel_id=1, source_target_pairs={{0,56},{2,58},{4,60},{6,62},{1,57},{3,59},{5,61},{7,63},{8,48},{10... | collective-permute-start | bytes 98312 | tf_op jit(solution)/shard_map/ppermute | solution.py:51
  9.7 18.0 %collective-permute-start.5 = (bf16[8,2048]{1,0:T(8,128)(2,1)}, bf16[8,2048]{1,0:T(8,128)(2,1)S(1)}, u32[]{:S(2)}, u32[]{:S(2)}) collective-permute-start(bf16[8,2048]{1,0:T(8,128)(2,1)} %whiten.1.own_ref), channel_id=1, source_target_pairs={{0,48},{2,50},{4,52},{6,54},{1,49},{3,51},{5,53},{7,55},{8,56},{10... | collective-permute-start | bytes 98312 | tf_op jit(solution)/shard_map/ppermute | solution.py:51
  10.2 17.6 %collective-permute-start.4 = (bf16[8,2048]{1,0:T(8,128)(2,1)}, bf16[8,2048]{1,0:T(8,128)(2,1)S(1)}, u32[]{:S(2)}, u32[]{:S(2)}) collective-permute-start(bf16[8,2048]{1,0:T(8,128)(2,1)} %whiten.1.own_ref), channel_id=1, source_target_pairs={{0,40},{2,42},{4,44},{6,46},{1,41},{3,43},{5,45},{7,47},{8,32},{10... | collective-permute-start | bytes 98312 | tf_op jit(solution)/shard_map/ppermute | solution.py:51
  13.7 14.0 %collective-permute-start.3 = (bf16[8,2048]{1,0:T(8,128)(2,1)}, bf16[8,2048]{1,0:T(8,128)(2,1)S(1)}, u32[]{:S(2)}, u32[]{:S(2)}) collective-permute-start(bf16[8,2048]{1,0:T(8,128)(2,1)} %whiten.1.own_ref), channel_id=1, source_target_pairs={{0,32},{2,34},{4,36},{6,38},{1,33},{3,35},{5,37},{7,39},{8,40},{10... | collective-permute-start | bytes 98312 | tf_op jit(solution)/shard_map/ppermute | solution.py:51
  15.5 3.0 %collective-permute-start = (bf16[8,2048]{1,0:T(8,128)(2,1)}, bf16[8,2048]{1,0:T(8,128)(2,1)S(1)}, u32[]{:S(2)}, u32[]{:S(2)}) collective-permute-start(bf16[8,2048]{1,0:T(8,128)(2,1)} %whiten.1.own_ref), channel_id=1, source_target_pairs={{0,8},{2,10},{4,12},{6,14},{1,9},{3,11},{5,13},{7,15},{8,0},{10,2}... | collective-permute-start | bytes 98312 | tf_op jit(solution)/shard_map/ppermute | solution.py:51
  18.5 4.4 %collective-permute-start.1 = (bf16[8,2048]{1,0:T(8,128)(2,1)}, bf16[8,2048]{1,0:T(8,128)(2,1)S(1)}, u32[]{:S(2)}, u32[]{:S(2)}) collective-permute-start(bf16[8,2048]{1,0:T(8,128)(2,1)} %whiten.1.own_ref), channel_id=1, source_target_pairs={{0,16},{2,18},{4,20},{6,22},{1,17},{3,19},{5,21},{7,23},{8,24},{10... | collective-permute-start | bytes 98312 | tf_op jit(solution)/shard_map/ppermute | solution.py:51
  22.9 4.8 %collective-permute-start.2 = (bf16[8,2048]{1,0:T(8,128)(2,1)}, bf16[8,2048]{1,0:T(8,128)(2,1)S(1)}, u32[]{:S(2)}, u32[]{:S(2)}) collective-permute-start(bf16[8,2048]{1,0:T(8,128)(2,1)} %whiten.1.own_ref), channel_id=1, source_target_pairs={{0,24},{2,26},{4,28},{6,30},{1,25},{3,27},{5,29},{7,31},{8,16},{10... | collective-permute-start | bytes 98312 | tf_op jit(solution)/shard_map/ppermute | solution.py:51
  27.8 5.3 %collective-permute-start.7 = (bf16[64,2048]{1,0:T(8,128)(2,1)S(1)}, bf16[64,2048]{1,0:T(8,128)(2,1)S(1)}, u32[]{:S(2)}, u32[]{:S(2)}) collective-permute-start(bf16[64,2048]{1,0:T(8,128)(2,1)S(1)} %get-tuple-element.5), channel_id=1, source_target_pairs={{0,64},{2,6},{4,68},{6,2},{1,65},{3,7},{5,69},{7,3},{8,72},{10,14}... | collective-permute-start | bytes 786440 | tf_op jit(solution)/shard_map/ppermute | solution.py:51
  29.1 9.1 %collective-permute-start.8 = (bf16[64,2048]{1,0:T(8,128)(2,1)S(1)}, bf16[64,2048]{1,0:T(8,128)(2,1)S(1)}, u32[]{:S(2)}, u32[]{:S(2)}) collective-permute-start(bf16[64,2048]{1,0:T(8,128)(2,1)S(1)} %get-tuple-element.5), channel_id=1, source_target_pairs={{0,128},{2,3},{4,132},{6,7},{1,129},{3,2},{5,133},{7,6},{8,136},{1... | collective-permute-start | bytes 786440 | tf_op jit(solution)/shard_map/ppermute | solution.py:51
  31.6 9.2 %collective-permute-start.9 = (bf16[64,2048]{1,0:T(8,128)(2,1)S(1)}, bf16[64,2048]{1,0:T(8,128)(2,1)S(1)}, u32[]{:S(2)}, u32[]{:S(2)}) collective-permute-start(bf16[64,2048]{1,0:T(8,128)(2,1)S(1)} %get-tuple-element.5), channel_id=1, source_target_pairs={{0,192},{2,7},{4,196},{6,3},{1,193},{3,6},{5,197},{7,2},{8,200},{1... | collective-permute-start | bytes 786440 | tf_op jit(solution)/shard_map/ppermute | solution.py:51
  40.8 61.4 %copy-start = (bf16[256,2048]{1,0:T(8,128)(2,1)}, bf16[256,2048]{1,0:T(8,128)(2,1)S(1)}, u32[]{:S(2)}) copy-start(bf16[256,2048]{1,0:T(8,128)(2,1)S(1)} %constant_dynamic-update-slice_fusion.8.refs_0_) | copy-start | bytes 3145732
  40.8 28.7 %collective-permute-start.12 = (bf16[256,2048]{1,0:T(8,128)(2,1)S(1)}, bf16[256,2048]{1,0:T(8,128)(2,1)S(1)}, u32[]{:S(2)}, u32[]{:S(2)}) collective-permute-start(bf16[256,2048]{1,0:T(8,128)(2,1)S(1)} %constant_dynamic-update-slice_fusion.8.refs_0_), channel_id=1, source_target_pairs={{0,5},{2,194},{4,1},{6,198},{1,4},{3,195},{5,0},{7,199},{8,13},{10... | collective-permute-start | bytes 3145736 | tf_op jit(solution)/shard_map/ppermute | solution.py:51
  43.9 44.4 %collective-permute-start.11 = (bf16[256,2048]{1,0:T(8,128)(2,1)S(1)}, bf16[256,2048]{1,0:T(8,128)(2,1)S(1)}, u32[]{:S(2)}, u32[]{:S(2)}) collective-permute-start(bf16[256,2048]{1,0:T(8,128)(2,1)S(1)} %constant_dynamic-update-slice_fusion.8.refs_0_), channel_id=1, source_target_pairs={{0,1},{2,130},{4,5},{6,134},{1,0},{3,131},{5,4},{7,135},{8,9},{10,... | collective-permute-start | bytes 3145736 | tf_op jit(solution)/shard_map/ppermute | solution.py:51
  44.1 44.3 %collective-permute-start.10 = (bf16[256,2048]{1,0:T(8,128)(2,1)S(1)}, bf16[256,2048]{1,0:T(8,128)(2,1)}, u32[]{:S(2)}, u32[]{:S(2)}) collective-permute-start(bf16[256,2048]{1,0:T(8,128)(2,1)S(1)} %constant_dynamic-update-slice_fusion.8.refs_0_), channel_id=1, source_target_pairs={{0,4},{2,66},{4,0},{6,70},{1,5},{3,67},{5,1},{7,71},{8,12},{10,74}... | collective-permute-start | bytes 3145736 | tf_op jit(solution)/shard_map/ppermute | solution.py:51
  44.6 57.6 %collective-permute-start.13 = (bf16[256,2048]{1,0:T(8,128)(2,1)S(1)}, bf16[256,2048]{1,0:T(8,128)(2,1)}, u32[]{:S(2)}, u32[]{:S(2)}) collective-permute-start(bf16[256,2048]{1,0:T(8,128)(2,1)S(1)} %constant_dynamic-update-slice_fusion.8.refs_0_), channel_id=1, source_target_pairs={{0,2},{2,0},{4,6},{6,4},{1,3},{3,1},{5,7},{7,5},{8,10},{10,8},{12,... | collective-permute-start | bytes 3145736 | tf_op jit(solution)/shard_map/ppermute | solution.py:51
  69.5 32.7 %copy-start.1 = (bf16[256,2048]{1,0:T(8,128)(2,1)}, bf16[256,2048]{1,0:T(8,128)(2,1)S(1)}, u32[]{:S(2)}) copy-start(bf16[256,2048]{1,0:T(8,128)(2,1)S(1)} %collective-permute-done.12.refs_3_) | copy-start | bytes 3145732
  69.5 32.7 %collective-permute-start.16 = (bf16[256,2048]{1,0:T(8,128)(2,1)S(1)}, bf16[256,2048]{1,0:T(8,128)(2,1)}, u32[]{:S(2)}, u32[]{:S(2)}) collective-permute-start(bf16[256,2048]{1,0:T(8,128)(2,1)S(1)} %collective-permute-done.12.refs_3_), channel_id=1, source_target_pairs={{0,2},{2,0},{4,6},{6,4},{1,3},{3,1},{5,7},{7,5},{8,10},{10,8},{12,... | collective-permute-start | bytes 3145736 | tf_op jit(solution)/shard_map/ppermute | solution.py:51
  88.3 13.9 %copy-start.2 = (bf16[256,2048]{1,0:T(8,128)(2,1)}, bf16[256,2048]{1,0:T(8,128)(2,1)S(1)}, u32[]{:S(2)}) copy-start(bf16[256,2048]{1,0:T(8,128)(2,1)S(1)} %collective-permute-done.11.refs_2_) | copy-start | bytes 3145732
  88.3 14.0 %collective-permute-start.15 = (bf16[256,2048]{1,0:T(8,128)(2,1)S(1)}, bf16[256,2048]{1,0:T(8,128)(2,1)}, u32[]{:S(2)}, u32[]{:S(2)}) collective-permute-start(bf16[256,2048]{1,0:T(8,128)(2,1)S(1)} %collective-permute-done.11.refs_2_), channel_id=1, source_target_pairs={{0,2},{2,0},{4,6},{6,4},{1,3},{3,1},{5,7},{7,5},{8,10},{10,8},{12,... | collective-permute-start | bytes 3145736 | tf_op jit(solution)/shard_map/ppermute | solution.py:51
  88.4 13.9 %collective-permute-start.14 = (bf16[256,2048]{1,0:T(8,128)(2,1)}, bf16[256,2048]{1,0:T(8,128)(2,1)}, u32[]{:S(2)}, u32[]{:S(2)}) collective-permute-start(bf16[256,2048]{1,0:T(8,128)(2,1)} %collective-permute-done.10.refs_1_), channel_id=1, source_target_pairs={{0,2},{2,0},{4,6},{6,4},{1,3},{3,1},{5,7},{7,5},{8,10},{10,8},{12,... | collective-permute-start | bytes 3145736 | tf_op jit(solution)/shard_map/ppermute | solution.py:51
  89.4 5.2 %collective-permute-start.17 = (bf16[8,2048]{1,0:T(8,128)(2,1)}, bf16[8,2048]{1,0:T(8,128)(2,1)S(1)}, u32[]{:S(2)}, u32[]{:S(2)}) collective-permute-start(bf16[8,2048]{1,0:T(8,128)(2,1)} %whiten.1.own_ref), channel_id=1, source_target_pairs={{0,1},{2,3},{4,5},{6,7},{1,0},{3,2},{5,4},{7,6},{8,9},{10,11},{12,... | collective-permute-start | bytes 98312 | tf_op jit(solution)/shard_map/ppermute | solution.py:51
  94.6 0.6 copy-start.3

commit v2 on v1

v2 whole, which is shorter than its diff:
```python
import functools
import math

import jax
import jax.numpy as jnp
import ml_dtypes
import numpy as np
from jax import lax
from jax.experimental import pallas as pl
from jax.experimental.pallas import tpu as pltpu
from jax.sharding import Mesh
from jax.sharding import PartitionSpec as P

NFFT = 1024
LAG = 128
F = 512
SEG = 768
SUBWIN = 4
NY, NZ, NX = 4, 8, 4
AXES = ("y", "z", "xl", "core", "tm")


def dft_tables():
    product = np.mod(np.arange(SEG)[:, None] * np.arange(F)[None, :], NFFT)
    theta = product * (2.0 * math.pi / NFFT)
    table = np.concatenate([np.cos(theta), -np.sin(theta)], axis=1)
    high = table.astype(ml_dtypes.bfloat16)
    low = (table - high.astype(np.float64)).astype(ml_dtypes.bfloat16)
    return high, low


def lag_table():
    product = np.mod(np.arange(F)[:, None] * (np.arange(2 * LAG) - LAG)[None, :], NFFT)
    phase = product * (2.0 * math.pi / NFFT)
    weight = np.where(np.arange(F) == 0, 1.0, 2.0)[:, None] / math.sqrt(F * SUBWIN)
    table = np.concatenate([weight * np.cos(phase), -weight * np.sin(phase)], axis=0)
    return table.astype(np.float32).astype(ml_dtypes.bfloat16)


def device_index(y, z, x, core):
    return (((y * NZ + z) * 2 + x % 2) * 2 + core) * 2 + x // 2


def permute(value, partner):
    pairs = []
    for y in range(NY):
        for z in range(NZ):
            for x in range(NX):
                for core in range(2):
                    pairs.append((device_index(y, z, x, core), device_index(*partner(y, z, x, core))))
    return lax.ppermute(value, AXES, pairs)


def along_z(d):
    return lambda y, z, x, core: (y, z ^ d, x, core)


def along_first(d):
    return lambda y, z, x, core: (y ^ d, z, x, core) if core == 0 else (y, z, x ^ d, core)


def along_second(d):
    return lambda y, z, x, core: (y, z, x ^ d, core) if core == 0 else (y ^ d, z, x, core)


def other_core(y, z, x, core):
    return (y, z, x, 1 - core)


def other_group(y, z, x, core):
    return (y, z, x ^ 2, core)


def whiten_kernel(lengths_ref, mask_ref, traces_ref, high_ref, low_ref, out_ref):
    tm = lax.axis_index("tm")
    x = traces_ref[...].reshape(16, SEG)
    row = lax.broadcasted_iota(jnp.int32, (16, 1), 0)
    length = jnp.where(row < 8, lengths_ref[2 * tm], lengths_ref[2 * tm + 1])
    usable = jnp.zeros((16, 1), jnp.float32)
    for c in range(8):
        usable = jnp.where(row % 8 == c, mask_ref[c].astype(jnp.float32), usable)
    live = lax.broadcasted_iota(jnp.int32, (16, SEG), 1) < length
    average = jnp.sum(jnp.where(live, x, 0.0), axis=1, keepdims=True) / length.astype(jnp.float32)
    centred = jnp.where(live, x - average, 0.0)
    part0 = centred.astype(jnp.bfloat16)
    rest = centred - part0.astype(jnp.float32)
    part1 = rest.astype(jnp.bfloat16)
    part2 = (rest - part1.astype(jnp.float32)).astype(jnp.bfloat16)
    parts = jnp.concatenate([part0, part1, part2], axis=0)
    by_high = jnp.dot(parts, high_ref[...], preferred_element_type=jnp.float32)
    by_low = jnp.dot(parts[:32], low_ref[...], preferred_element_type=jnp.float32)
    spectrum = by_high[:16] + (by_high[16:32] + by_low[:16] + (by_high[32:] + by_low[16:]))
    re, im = spectrum[:, :F], spectrum[:, F:]
    power = re * re + im * im
    level = jnp.mean(power, axis=1, keepdims=True)
    factor = usable / jnp.sqrt(power + 0.01 * level + 1e-06)
    for k in range(2):
        rows = slice(8 * k, 8 * k + 8)
        out_ref[:, 2 * k * F : (2 * k + 1) * F] = (re * factor)[rows].astype(jnp.bfloat16)
        out_ref[:, (2 * k + 1) * F : (2 * k + 2) * F] = (im * factor)[rows].astype(jnp.bfloat16)


def whiten(traces, lengths, mask):
    high, low = dft_tables()
    smem = pl.BlockSpec(memory_space=pltpu.SMEM)
    vmem = pl.BlockSpec(memory_space=pltpu.VMEM)
    return pl.pallas_call(
        whiten_kernel,
        in_specs=[smem, smem, vmem, vmem, vmem],
        out_specs=vmem,
        out_shape=jax.ShapeDtypeStruct((8, 4 * F), jnp.bfloat16),
        compiler_params=pltpu.CompilerParams(vmem_limit_bytes=60 * 2**20),
        name="whiten",
    )(lengths, mask, traces, jnp.asarray(high), jnp.asarray(low))


def fold_kernel(own_ref, other_ref, lag_ref, out_ref, rows):
    i = pl.program_id(0)
    rows[0] = own_ref[...].astype(jnp.float32)
    rows[1] = other_ref[...].astype(jnp.float32)
    mine = 4 * lax.axis_index("tm") + i
    step = 32

    @pl.loop(0, 2 * LAG, step=step)
    def _(begin):
        at = pl.ds(pl.multiple_of(begin, step), step)
        cos = lag_ref[at, :F].astype(jnp.float32)
        sin = lag_ref[at, F:].astype(jnp.float32)
        for group in range(2):
            for k in range(2):
                to = 2 * F * (2 * group + k)
                a_re = rows[group, pl.ds(mine, 1), 2 * k * F : (2 * k + 1) * F]
                a_im = rows[group, pl.ds(mine, 1), (2 * k + 1) * F : (2 * k + 2) * F]
                out_ref[at, to : to + F] = (a_re * cos + a_im * sin).astype(jnp.bfloat16)
                out_ref[at, to + F : to + 2 * F] = (a_im * cos - a_re * sin).astype(jnp.bfloat16)


def fold(own, other):
    whole = pl.BlockSpec((8, 4 * F), lambda i: (0, 0))
    return pl.pallas_call(
        fold_kernel,
        grid=(4,),
        in_specs=[whole, whole, pl.BlockSpec((2 * LAG, 2 * F), lambda i: (0, 0))],
        out_specs=pl.BlockSpec((2 * LAG, 8 * F), lambda i: (i, 0)),
        out_shape=jax.ShapeDtypeStruct((8 * LAG, 8 * F), jnp.bfloat16),
        scratch_shapes=[pltpu.VMEM((2, 8, 4 * F), jnp.float32)],
        cost_estimate=pl.CostEstimate(flops=2**20, bytes_accessed=2**10, transcendentals=0),
        compiler_params=pltpu.CompilerParams(vmem_limit_bytes=16 * 2**20),
        name="fold",
    )(own, other, jnp.asarray(np.ascontiguousarray(lag_table().T)))


def select(part, x, y):
    if part == 0:
        return [y[0][:128, :]], [y[0][128:, :]]
    if part == 1:
        return [x[0][...], y[0][:128, :], y[1][:128, :]], [x[1][...], y[0][128:, :], y[1][128:, :]]
    return [x[0][...], y[1][...]], [x[1][...], x[2][...], y[2][...]]


def places_of(part, y, xl):
    if part == 0:
        return [(y, xl ^ e, 1) for e in range(2)]
    if part == 1:
        return [(y ^ b, xl ^ 1, 0) for b in range(4)] + [(y ^ b, xl ^ e, 1) for b in (1, 3) for e in range(2)]
    return [(y ^ b, xl, 0) for b in range(4)] + [(y ^ 2, xl ^ e, 1) for e in range(2)]


def part_kernel(part, count, *refs):
    mine, theirs = refs[0:count], refs[count : 2 * count]
    folded, out_ref, blocks, stored = refs[2 * count], *refs[-3:]
    y, z, xl, core = (lax.axis_index(name) for name in ("y", "z", "xl", "core"))
    half = 4 * F
    places = places_of(part, y, xl)

    def stores(i):
        return [
            pltpu.make_async_copy(blocks.at[i, n], out_ref.at[i, to_y, :, to_xl, to_core], stored.at[i, n])
            for n, (to_y, to_xl, to_core) in enumerate(places)
        ]

    def product(rows, columns):
        rows = rows[0] if len(rows) == 1 else jnp.concatenate(rows, axis=0)
        return lax.dot_general(rows, columns, (((1,), (1,)), ((), ())), preferred_element_type=jnp.float32)

    def compute(i, x_chunks, y_chunks):
        at = pl.ds(pl.multiple_of(2 * LAG * i, 2 * LAG), 2 * LAG)
        first, second = select(part, x_chunks, y_chunks)
        values = product(first, folded[at, :half]) + product(second, folded[at, half:])
        for n in range(len(places)):
            for g in range(NZ):
                blocks[i, n, z ^ g] = values[64 * n + 8 * g : 64 * n + 8 * g + 8]

    @pl.loop(0, 4)
    def _(i):
        @pl.when(core == 0)
        def _():
            compute(i, mine, theirs)

        @pl.when(core == 1)
        def _():
            compute(i, theirs, mine)

        for copy in stores(i):
            copy.start()

    @pl.loop(0, 4)
    def _(i):
        for copy in stores(i):
            copy.wait()


def correlate_part(part, mine, theirs, folded, out):
    count, blocks = len(mine), len(places_of(part, 0, 0))
    vmem = pl.BlockSpec(memory_space=pltpu.VMEM)
    hbm = pl.BlockSpec(memory_space=pltpu.HBM)
    operands = [*mine, *theirs, folded] + ([] if out is None else [out])
    return pl.pallas_call(
        functools.partial(part_kernel, part, count),
        in_specs=[vmem] * (2 * count + 1) + ([] if out is None else [hbm]),
        out_specs=hbm,
        out_shape=jax.ShapeDtypeStruct((4, NY, NZ, 2, 2, 8, 2 * LAG), jnp.float32),
        scratch_shapes=[
            pltpu.VMEM((4, blocks, NZ, 8, 2 * LAG), jnp.float32),
            pltpu.SemaphoreType.DMA((4, blocks)),
        ],
        input_output_aliases={} if out is None else {2 * count + 1: 0},
        cost_estimate=pl.CostEstimate(flops=2**20, bytes_accessed=2**10, transcendentals=0),
        compiler_params=pltpu.CompilerParams(vmem_limit_bytes=24 * 2**20),
        name="correlate",
    )(*operands)


def local(traces, lengths, mask):
    own = whiten(traces, lengths, mask)
    other = permute(own, other_group)
    ring = jnp.concatenate([own, permute(own, along_z(1))], axis=0)
    ring = jnp.concatenate([ring] + [permute(ring, along_z(d)) for d in (2, 4, 6)], axis=0)
    ring, own, other = lax.optimization_barrier((ring, own, other))
    plane = jnp.concatenate([ring] + [permute(ring, along_first(d)) for d in range(1, 4)], axis=0)
    folded = fold(own, other)
    plane, folded = lax.optimization_barrier((plane, folded))
    chunk1, chunk3 = permute(plane, along_second(1)), permute(plane, along_second(3))
    plane_too = permute(plane, other_core)
    out = correlate_part(0, [plane], [plane_too], folded, None)
    chunk1, chunk3, out, folded = lax.optimization_barrier((chunk1, chunk3, out, folded))
    top, bottom = permute(chunk3[:128], along_second(1)), permute(chunk1[128:], along_second(3))
    mine = [chunk1, chunk3]
    out = correlate_part(1, mine, [permute(chunk, other_core) for chunk in mine], folded, out)
    top, bottom, out = lax.optimization_barrier((top, bottom, out))
    theirs = [plane_too, permute(top, other_core), permute(bottom, other_core)]
    out = correlate_part(2, [plane, top, bottom], theirs, folded, out)
    return out.reshape(4, NY * NZ * 4 * 8, 2 * LAG)


def solution(mesh):
    finer = Mesh(mesh.devices.reshape(NY, NZ, 2, 2, 2), AXES)
    chan = ("y", "z", "xl", "core")
    return jax.shard_map(
        local,
        mesh=finer,
        in_specs=(P("tm", chan, None), P(), P(chan)),
        out_specs=P(AXES, None, None),
        check_vma=False,
    )
```

time: 117 us -> 76.3 us (0.65)
  starting transfers between devices: 66.6 us -> 24.9 us
  Pallas kernels: 25 us -> 21 us
  waiting for transfers between devices: 23.6 us -> 27.3 us
    ppermute x18 -> x17, starting transfers between devices: 66.6 us -> 24.9 us  [permute(): return lax.ppermute(value, AXES, pairs)]
    pallas_call x2 -> x4, Pallas kernels: 21.7 us -> 17.6 us  [the longest x3 15.3 us: correlate_part(): pl.pallas_call(functools.partial(part_kernel, part, count), in_specs=[vme...]
    ppermute x18 -> x17, waiting for transfers between devices: 23.6 us -> 27.3 us  [permute(): return lax.ppermute(value, AXES, pairs)]
  transfers between devices with their start and end apart: 18 -> 17, of which waited for: 8 -> 11; matrix products, arithmetic and copies ran while one was open for 1% -> 2% of each run, Pallas kernels for 6% -> 16%
where the time goes in v2:
time: 76.3 us; the launch traced here: 76 us
  waiting for transfers between devices  27.3 us (36%)
  starting transfers between devices  24.9 us (33%)
  Pallas kernels  21 us (28%)
  local copies, waits for them, and re-layouts  1.66 us (2%)
  other arithmetic  0.83 us (1%)
    ppermute x17, waiting for transfers between devices, permute(): return lax.ppermute(value, AXES, pairs)  27.3 us
    ppermute x17, starting transfers between devices, permute(): return lax.ppermute(value, AXES, pairs)  24.9 us
    pallas_call x3, Pallas kernels, correlate_part(): pl.pallas_call(functools.partial(part_kernel, part, count), in_specs=[vme...  15.3 us
    pallas_call x1, Pallas kernels, whiten(): pl.pallas_call(whiten_kernel, in_specs=[smem, smem, vmem, vmem, vmem], ou...  3.36 us
    pallas_call x1, Pallas kernels, fold(): pl.pallas_call(fold_kernel, grid=(4,), in_specs=[whole, whole, pl.BlockSp...  2.28 us
    unnamed x8, local copies, waits for them, and re-layouts  1.57 us
  transfers between devices with their start and end apart: 17, of which 11 were waited for; matrix products, arithmetic and copies ran while one was open for 2% of the time, Pallas kernels for 16%

profile of v2, /device:TPU:1, one launch (start us, length us, event | category | flops | bytes accessed | tf_op | source)
XLA Modules:
  0.0 76.0 jit_solution(5126135745563780224)
XLA Ops:
  0.0 0.0 copy-start.1
  0.0 3.4 %whiten.1.own_ref = bf16[8,2048]{1,0:T(8,128)(2,1)} custom-call(s32[4]{0:T(128)} %lengths_ref.1, s32[8]{0:T(128)} %mask_ref.1, f32[2,8,768]{2,1,0:T(8,128)} %traces_ref.1, bf16[768,1024]{1,0:T(8,128)(2,1)} %constant.6.clone.high_ref, bf16[768,1024]{1,0:T(8,128)(2,1)} %constant.7.clone.low_ref), custom_call_target="tpu_custom_call" | custom-call | tf_op jit(solution)/shard_map/whiten/pallas_call | solution.py:107
  3.4 2.5 %collective-permute-start = (bf16[8,2048]{1,0:T(8,128)(2,1)}, bf16[8,2048]{1,0:T(8,128)(2,1)S(1)}, u32[]{:S(2)}, u32[]{:S(2)}) collective-permute-start(bf16[8,2048]{1,0:T(8,128)(2,1)} %whiten.1.own_ref), channel_id=1, source_target_pairs={{0,8},{2,10},{4,12},{6,14},{1,9},{3,11},{5,13},{7,15},{8,0},{10,2}... | collective-permute-start | bytes 98312 | tf_op jit(solution)/shard_map/ppermute | solution.py:51
  5.8 2.7 %collective-permute-start.4 = (bf16[8,2048]{1,0:T(8,128)(2,1)}, bf16[8,2048]{1,0:T(8,128)(2,1)S(1)}, u32[]{:S(2)}, u32[]{:S(2)}) collective-permute-start(bf16[8,2048]{1,0:T(8,128)(2,1)} %whiten.1.own_ref), channel_id=1, source_target_pairs={{0,1},{2,3},{4,5},{6,7},{1,0},{3,2},{5,4},{7,6},{8,9},{10,11},{12,... | collective-permute-start | bytes 98312 | tf_op jit(solution)/shard_map/ppermute | solution.py:51
  8.6 0.8 %constant_dynamic-update-slice_fusion.4 = bf16[64,2048]{1,0:T(8,128)(2,1)S(1)} fusion(bf16[8,2048]{1,0:T(8,128)(2,1)} %whiten.1.own_ref), kind=kLoop, calls=%fused_computation.6 | loop fusion | bytes 65536
  9.4 0.0 collective-permute-done
  9.4 0.8 %pad_maximum_fusion.1 = bf16[16,2048]{1,0:T(8,128)(2,1)S(1)} fusion(bf16[8,2048]{1,0:T(8,128)(2,1)S(1)} %collective-permute-done, bf16[8,2048]{1,0:T(8,128)(2,1)} %whiten.1.own_ref), kind=kLoop, calls=%fused_computation.1 | loop fusion | flops 131072 | bytes 131072 | tf_op jit(solution)/shard_map/concatenate | solution.py:237
  10.1 3.0 %collective-permute-start.1 = (bf16[16,2048]{1,0:T(8,128)(2,1)S(1)}, bf16[16,2048]{1,0:T(8,128)(2,1)S(1)}, u32[]{:S(2)}, u32[]{:S(2)}) collective-permute-start(bf16[16,2048]{1,0:T(8,128)(2,1)S(1)} %pad_maximum_fusion.1), channel_id=1, source_target_pairs={{0,16},{2,18},{4,20},{6,22},{1,17},{3,19},{5,21},{7,23},{8,24},{10... | collective-permute-start | bytes 196616 | tf_op jit(solution)/shard_map/ppermute | solution.py:51
  13.1 4.2 %collective-permute-start.2 = (bf16[16,2048]{1,0:T(8,128)(2,1)S(1)}, bf16[16,2048]{1,0:T(8,128)(2,1)S(1)}, u32[]{:S(2)}, u32[]{:S(2)}) collective-permute-start(bf16[16,2048]{1,0:T(8,128)(2,1)S(1)} %pad_maximum_fusion.1), channel_id=1, source_target_pairs={{0,32},{2,34},{4,36},{6,38},{1,33},{3,35},{5,37},{7,39},{8,40},{10... | collective-permute-start | bytes 196616 | tf_op jit(solution)/shard_map/ppermute | solution.py:51
  17.3 0.0 collective-permute-start.3
  17.4 0.0 collective-permute-done.1
  17.4 3.0 %collective-permute-done.2 = bf16[16,2048]{1,0:T(8,128)(2,1)S(1)} collective-permute-done((bf16[16,2048]{1,0:T(8,128)(2,1)S(1)}, bf16[16,2048]{1,0:T(8,128)(2,1)S(1)}, u32[]{:S(2)}, u32[]{:S(2)}) %collective-permute-start.2) | collective-permute-done | bytes 65568 | tf_op jit(solution)/shard_map/ppermute | solution.py:51
  20.4 2.9 %collective-permute-done.3 = bf16[16,2048]{1,0:T(8,128)(2,1)S(1)} collective-permute-done((bf16[16,2048]{1,0:T(8,128)(2,1)S(1)}, bf16[16,2048]{1,0:T(8,128)(2,1)S(1)}, u32[]{:S(2)}, u32[]{:S(2)}) %collective-permute-start.3) | collective-permute-done | bytes 65568 | tf_op jit(solution)/shard_map/ppermute | solution.py:51
  23.3 0.0 collective-permute-done.4.other_ref
  23.3 0.4 collective-permute-start.5
  23.7 1.7 %collective-permute-start.6 = (bf16[64,2048]{1,0:T(8,128)(2,1)S(1)}, bf16[64,2048]{1,0:T(8,128)(2,1)S(1)}, u32[]{:S(2)}, u32[]{:S(2)}) collective-permute-start(bf16[64,2048]{1,0:T(8,128)(2,1)S(1)} %constant_dynamic-update-slice_fusion), channel_id=1, source_target_pairs={{0,128},{2,3},{4,132},{6,7},{1,129},{3,2},{5,133},{7,6},{8,136},{1... | collective-permute-start | bytes 786440 | tf_op jit(solution)/shard_map/ppermute | solution.py:51
  25.4 1.8 %collective-permute-start.7 = (bf16[64,2048]{1,0:T(8,128)(2,1)S(1)}, bf16[64,2048]{1,0:T(8,128)(2,1)S(1)}, u32[]{:S(2)}, u32[]{:S(2)}) collective-permute-start(bf16[64,2048]{1,0:T(8,128)(2,1)S(1)} %constant_dynamic-update-slice_fusion), channel_id=1, source_target_pairs={{0,192},{2,7},{4,196},{6,3},{1,193},{3,6},{5,197},{7,2},{8,200},{1... | collective-permute-start | bytes 786440 | tf_op jit(solution)/shard_map/ppermute | solution.py:51
  27.2 0.0 copy-done.1
  27.2 0.0 copy-start
  27.2 0.8 copy-done
  28.0 2.3 %fold.1.refs_2_.refs_4_.refs_6_ = bf16[1024,4096]{1,0:T(8,128)(2,1)S(1)} custom-call(bf16[8,2048]{1,0:T(8,128)(2,1)S(1)} %copy-done, bf16[8,2048]{1,0:T(8,128)(2,1)S(1)} %collective-permute-done.4.other_ref, bf16[256,1024]{1,0:T(8,128)(2,1)S(1)} %copy-done.1), custom_call_target="tpu_custom_call" | custom-call | flops 1048576 | bytes 1024 | tf_op jit(solution)/shard_map/fold/pallas_call | solution.py:140
  30.3 0.0 collective-permute-done.5
  30.3 1.8 %collective-permute-done.6 = bf16[64,2048]{1,0:T(8,128)(2,1)S(1)} collective-permute-done((bf16[64,2048]{1,0:T(8,128)(2,1)S(1)}, bf16[64,2048]{1,0:T(8,128)(2,1)S(1)}, u32[]{:S(2)}, u32[]{:S(2)}) %collective-permute-start.6) | collective-permute-done | bytes 262176 | tf_op jit(solution)/shard_map/ppermute | solution.py:51
  32.1 2.9 %collective-permute-done.7 = bf16[64,2048]{1,0:T(8,128)(2,1)S(1)} collective-permute-done((bf16[64,2048]{1,0:T(8,128)(2,1)S(1)}, bf16[64,2048]{1,0:T(8,128)(2,1)S(1)}, u32[]{:S(2)}, u32[]{:S(2)}) %collective-permute-start.7) | collective-permute-done | bytes 262176 | tf_op jit(solution)/shard_map/ppermute | solution.py:51
  34.9 0.1 pad_maximum_fusion.refs_0_
  35.0 5.2 %collective-permute-start.10 = (bf16[256,2048]{1,0:T(8,128)(2,1)S(1)}, bf16[256,2048]{1,0:T(8,128)(2,1)S(1)}, u32[]{:S(2)}, u32[]{:S(2)}) collective-permute-start(bf16[256,2048]{1,0:T(8,128)(2,1)S(1)} %pad_maximum_fusion.refs_0_), channel_id=1, source_target_pairs={{0,2},{2,0},{4,6},{6,4},{1,3},{3,1},{5,7},{7,5},{8,10},{10,8},{12,... | collective-permute-start | bytes 3145736 | tf_op jit(solution)/shard_map/ppermute | solution.py:51
  40.2 0.0 collective-permute-start.8
  40.2 0.0 collective-permute-start.9
  40.2 2.3 %collective-permute-done.10.refs_1_.refs_3_ = bf16[256,2048]{1,0:T(8,128)(2,1)S(1)} collective-permute-done((bf16[256,2048]{1,0:T(8,128)(2,1)S(1)}, bf16[256,2048]{1,0:T(8,128)(2,1)S(1)}, u32[]{:S(2)}, u32[]{:S(2)}) %collective-permute-start.10) | collective-permute-done | bytes 1048608 | tf_op jit(solution)/shard_map/ppermute | solution.py:51
  42.5 4.0 %correlate.3.refs_5_ = f32[4,4,8,2,2,8,256]{6,5,4,3,2,1,0:T(8,128)} custom-call(bf16[256,2048]{1,0:T(8,128)(2,1)S(1)} %pad_maximum_fusion.refs_0_, bf16[256,2048]{1,0:T(8,128)(2,1)S(1)} %collective-permute-done.10.refs_1_.refs_3_, bf16[1024,4096]{1,0:T(8,128)(2,1)S(1)} %fold.1.refs_2_.refs_4_.refs_6_), custom_call_target="tpu_custom_call" | custom-call | flops 1048576 | bytes 1024 | tf_op jit(solution)/shard_map/correlate/pallas_call | solution.py:218
  46.5 7.7 %collective-permute-done.8.refs_0_ = bf16[256,2048]{1,0:T(8,128)(2,1)S(1)} collective-permute-done((bf16[256,2048]{1,0:T(8,128)(2,1)S(1)}, bf16[256,2048]{1,0:T(8,128)(2,1)S(1)}, u32[]{:S(2)}, u32[]{:S(2)}) %collective-permute-start.8) | collective-permute-done | bytes 1048608 | tf_op jit(solution)/shard_map/ppermute | solution.py:51
  54.2 1.2 %collective-permute-done.9.refs_1_ = bf16[256,2048]{1,0:T(8,128)(2,1)S(1)} collective-permute-done((bf16[256,2048]{1,0:T(8,128)(2,1)S(1)}, bf16[256,2048]{1,0:T(8,128)(2,1)S(1)}, u32[]{:S(2)}, u32[]{:S(2)}) %collective-permute-start.9) | collective-permute-done | bytes 1048608 | tf_op jit(solution)/shard_map/ppermute | solution.py:51
  55.4 1.7 %collective-permute-start.13 = (bf16[256,2048]{1,0:T(8,128)(2,1)S(1)}, bf16[256,2048]{1,0:T(8,128)(2,1)S(1)}, u32[]{:S(2)}, u32[]{:S(2)}) collective-permute-start(bf16[256,2048]{1,0:T(8,128)(2,1)S(1)} %collective-permute-done.8.refs_0_), channel_id=1, source_target_pairs={{0,2},{2,0},{4,6},{6,4},{1,3},{3,1},{5,7},{7,5},{8,10},{10,8},{12,... | collective-permute-start | bytes 3145736 | tf_op jit(solution)/shard_map/ppermute | solution.py:51
  57.1 0.0 collective-permute-start.14
  57.2 0.1 collective-permute-start.11
  57.3 0.3 collective-permute-start.12
  57.6 1.8 %collective-permute-done.13.refs_2_ = bf16[256,2048]{1,0:T(8,128)(2,1)S(1)} collective-permute-done((bf16[256,2048]{1,0:T(8,128)(2,1)S(1)}, bf16[256,2048]{1,0:T(8,128)(2,1)S(1)}, u32[]{:S(2)}, u32[]{:S(2)}) %collective-permute-start.13) | collective-permute-done | bytes 1048608 | tf_op jit(solution)/shard_map/ppermute | solution.py:51
  59.4 1.5 %collective-permute-done.14.refs_3_ = bf16[256,2048]{1,0:T(8,128)(2,1)S(1)} collective-permute-done((bf16[256,2048]{1,0:T(8,128)(2,1)S(1)}, bf16[256,2048]{1,0:T(8,128)(2,1)S(1)}, u32[]{:S(2)}, u32[]{:S(2)}) %collective-permute-start.14) | collective-permute-done | bytes 1048608 | tf_op jit(solution)/shard_map/ppermute | solution.py:51
  60.9 6.3 %correlate.4.refs_7_ = f32[4,4,8,2,2,8,256]{6,5,4,3,2,1,0:T(8,128)} custom-call(bf16[256,2048]{1,0:T(8,128)(2,1)S(1)} %collective-permute-done.8.refs_0_, bf16[256,2048]{1,0:T(8,128)(2,1)S(1)} %collective-permute-done.9.refs_1_, bf16[256,2048]{1,0:T(8,128)(2,1)S(1)} %collective-permute-done.13.refs_2_, ...), custom_call_target="tpu_custom_call", output_to_operand_aliasing={{}: (5, {})} | custom-call | flops 1048576 | bytes 1024 | tf_op jit(solution)/shard_map/correlate/pallas_call | solution.py:218
  67.2 0.0 collective-permute-done.11.refs_1_
  67.2 0.0 collective-permute-done.12.refs_2_
  67.2 1.3 %collective-permute-start.15 = (bf16[128,2048]{1,0:T(8,128)(2,1)S(1)}, bf16[128,2048]{1,0:T(8,128)(2,1)S(1)}, u32[]{:S(2)}, u32[]{:S(2)}) collective-permute-start(bf16[128,2048]{1,0:T(8,128)(2,1)S(1)} %collective-permute-done.11.refs_1_), channel_id=1, source_target_pairs={{0,2},{2,0},{4,6},{6,4},{1,3},{3,1},{5,7},{7,5},{8,10},{10,8},{12,... | collective-permute-start | bytes 1572872 | tf_op jit(solution)/shard_map/ppermute | solution.py:51
  68.5 0.0 collective-permute-start.16
  68.5 1.5 %collective-permute-done.15.refs_4_ = bf16[128,2048]{1,0:T(8,128)(2,1)S(1)} collective-permute-done((bf16[128,2048]{1,0:T(8,128)(2,1)S(1)}, bf16[128,2048]{1,0:T(8,128)(2,1)S(1)}, u32[]{:S(2)}, u32[]{:S(2)}) %collective-permute-start.15) | collective-permute-done | bytes 524320 | tf_op jit(solution)/shard_map/ppermute | solution.py:51
  70.0 0.7 collective-permute-done.16.refs_5_
  70.8 5.1 %correlate.5 = f32[4,4,8,2,2,8,256]{6,5,4,3,2,1,0:T(8,128)} custom-call(bf16[256,2048]{1,0:T(8,128)(2,1)S(1)} %pad_maximum_fusion.refs_0_, bf16[128,2048]{1,0:T(8,128)(2,1)S(1)} %collective-permute-done.11.refs_1_, bf16[128,2048]{1,0:T(8,128)(2,1)S(1)} %collective-permute-done.12.refs_2_, ...), custom_call_target="tpu_custom_call", output_to_operand_aliasing={{}: (7, {})} | custom-call | flops 1048576 | bytes 1024 | tf_op jit(solution)/shard_map/correlate/pallas_call | solution.py:218
  (6 shorter events, 0.1 us)
Async XLA Ops:
  0.0 27.2 %copy-start.1 = (bf16[256,1024]{1,0:T(8,128)(2,1)S(1)}, bf16[256,1024]{1,0:T(8,128)(2,1)}, u32[]{:S(2)}) copy-start(bf16[256,1024]{1,0:T(8,128)(2,1)} %constant.8.clone.lag_ref) | copy-start | bytes 1572868
  3.4 6.0 %collective-permute-start = (bf16[8,2048]{1,0:T(8,128)(2,1)}, bf16[8,2048]{1,0:T(8,128)(2,1)S(1)}, u32[]{:S(2)}, u32[]{:S(2)}) collective-permute-start(bf16[8,2048]{1,0:T(8,128)(2,1)} %whiten.1.own_ref), channel_id=1, source_target_pairs={{0,8},{2,10},{4,12},{6,14},{1,9},{3,11},{5,13},{7,15},{8,0},{10,2}... | collective-permute-start | bytes 98312 | tf_op jit(solution)/shard_map/ppermute | solution.py:51
  5.8 17.4 %collective-permute-start.4 = (bf16[8,2048]{1,0:T(8,128)(2,1)}, bf16[8,2048]{1,0:T(8,128)(2,1)S(1)}, u32[]{:S(2)}, u32[]{:S(2)}) collective-permute-start(bf16[8,2048]{1,0:T(8,128)(2,1)} %whiten.1.own_ref), channel_id=1, source_target_pairs={{0,1},{2,3},{4,5},{6,7},{1,0},{3,2},{5,4},{7,6},{8,9},{10,11},{12,... | collective-permute-start | bytes 98312 | tf_op jit(solution)/shard_map/ppermute | solution.py:51
  10.1 7.2 %collective-permute-start.1 = (bf16[16,2048]{1,0:T(8,128)(2,1)S(1)}, bf16[16,2048]{1,0:T(8,128)(2,1)S(1)}, u32[]{:S(2)}, u32[]{:S(2)}) collective-permute-start(bf16[16,2048]{1,0:T(8,128)(2,1)S(1)} %pad_maximum_fusion.1), channel_id=1, source_target_pairs={{0,16},{2,18},{4,20},{6,22},{1,17},{3,19},{5,21},{7,23},{8,24},{10... | collective-permute-start | bytes 196616 | tf_op jit(solution)/shard_map/ppermute | solution.py:51
  13.1 7.3 %collective-permute-start.2 = (bf16[16,2048]{1,0:T(8,128)(2,1)S(1)}, bf16[16,2048]{1,0:T(8,128)(2,1)S(1)}, u32[]{:S(2)}, u32[]{:S(2)}) collective-permute-start(bf16[16,2048]{1,0:T(8,128)(2,1)S(1)} %pad_maximum_fusion.1), channel_id=1, source_target_pairs={{0,32},{2,34},{4,36},{6,38},{1,33},{3,35},{5,37},{7,39},{8,40},{10... | collective-permute-start | bytes 196616 | tf_op jit(solution)/shard_map/ppermute | solution.py:51
  17.3 5.9 %collective-permute-start.3 = (bf16[16,2048]{1,0:T(8,128)(2,1)S(1)}, bf16[16,2048]{1,0:T(8,128)(2,1)S(1)}, u32[]{:S(2)}, u32[]{:S(2)}) collective-permute-start(bf16[16,2048]{1,0:T(8,128)(2,1)S(1)} %pad_maximum_fusion.1), channel_id=1, source_target_pairs={{0,48},{2,50},{4,52},{6,54},{1,49},{3,51},{5,53},{7,55},{8,56},{10... | collective-permute-start | bytes 196616 | tf_op jit(solution)/shard_map/ppermute | solution.py:51
  23.3 7.0 %collective-permute-start.5 = (bf16[64,2048]{1,0:T(8,128)(2,1)S(1)}, bf16[64,2048]{1,0:T(8,128)(2,1)S(1)}, u32[]{:S(2)}, u32[]{:S(2)}) collective-permute-start(bf16[64,2048]{1,0:T(8,128)(2,1)S(1)} %constant_dynamic-update-slice_fusion), channel_id=1, source_target_pairs={{0,64},{2,6},{4,68},{6,2},{1,65},{3,7},{5,69},{7,3},{8,72},{10,14}... | collective-permute-start | bytes 786440 | tf_op jit(solution)/shard_map/ppermute | solution.py:51
  23.7 8.4 %collective-permute-start.6 = (bf16[64,2048]{1,0:T(8,128)(2,1)S(1)}, bf16[64,2048]{1,0:T(8,128)(2,1)S(1)}, u32[]{:S(2)}, u32[]{:S(2)}) collective-permute-start(bf16[64,2048]{1,0:T(8,128)(2,1)S(1)} %constant_dynamic-update-slice_fusion), channel_id=1, source_target_pairs={{0,128},{2,3},{4,132},{6,7},{1,129},{3,2},{5,133},{7,6},{8,136},{1... | collective-permute-start | bytes 786440 | tf_op jit(solution)/shard_map/ppermute | solution.py:51
  25.4 9.5 %collective-permute-start.7 = (bf16[64,2048]{1,0:T(8,128)(2,1)S(1)}, bf16[64,2048]{1,0:T(8,128)(2,1)S(1)}, u32[]{:S(2)}, u32[]{:S(2)}) collective-permute-start(bf16[64,2048]{1,0:T(8,128)(2,1)S(1)} %constant_dynamic-update-slice_fusion), channel_id=1, source_target_pairs={{0,192},{2,7},{4,196},{6,3},{1,193},{3,6},{5,197},{7,2},{8,200},{1... | collective-permute-start | bytes 786440 | tf_op jit(solution)/shard_map/ppermute | solution.py:51
  27.2 0.8 copy-start
  35.0 7.5 %collective-permute-start.10 = (bf16[256,2048]{1,0:T(8,128)(2,1)S(1)}, bf16[256,2048]{1,0:T(8,128)(2,1)S(1)}, u32[]{:S(2)}, u32[]{:S(2)}) collective-permute-start(bf16[256,2048]{1,0:T(8,128)(2,1)S(1)} %pad_maximum_fusion.refs_0_), channel_id=1, source_target_pairs={{0,2},{2,0},{4,6},{6,4},{1,3},{3,1},{5,7},{7,5},{8,10},{10,8},{12,... | collective-permute-start | bytes 3145736 | tf_op jit(solution)/shard_map/ppermute | solution.py:51
  40.2 13.9 %collective-permute-start.8 = (bf16[256,2048]{1,0:T(8,128)(2,1)S(1)}, bf16[256,2048]{1,0:T(8,128)(2,1)S(1)}, u32[]{:S(2)}, u32[]{:S(2)}) collective-permute-start(bf16[256,2048]{1,0:T(8,128)(2,1)S(1)} %pad_maximum_fusion.refs_0_), channel_id=1, source_target_pairs={{0,4},{2,66},{4,0},{6,70},{1,5},{3,67},{5,1},{7,71},{8,12},{10,74}... | collective-permute-start | bytes 3145736 | tf_op jit(solution)/shard_map/ppermute | solution.py:51
  40.2 15.2 %collective-permute-start.9 = (bf16[256,2048]{1,0:T(8,128)(2,1)S(1)}, bf16[256,2048]{1,0:T(8,128)(2,1)S(1)}, u32[]{:S(2)}, u32[]{:S(2)}) collective-permute-start(bf16[256,2048]{1,0:T(8,128)(2,1)S(1)} %pad_maximum_fusion.refs_0_), channel_id=1, source_target_pairs={{0,5},{2,194},{4,1},{6,198},{1,4},{3,195},{5,0},{7,199},{8,13},{10... | collective-permute-start | bytes 3145736 | tf_op jit(solution)/shard_map/ppermute | solution.py:51
  55.4 4.0 %collective-permute-start.13 = (bf16[256,2048]{1,0:T(8,128)(2,1)S(1)}, bf16[256,2048]{1,0:T(8,128)(2,1)S(1)}, u32[]{:S(2)}, u32[]{:S(2)}) collective-permute-start(bf16[256,2048]{1,0:T(8,128)(2,1)S(1)} %collective-permute-done.8.refs_0_), channel_id=1, source_target_pairs={{0,2},{2,0},{4,6},{6,4},{1,3},{3,1},{5,7},{7,5},{8,10},{10,8},{12,... | collective-permute-start | bytes 3145736 | tf_op jit(solution)/shard_map/ppermute | solution.py:51
  57.1 3.8 %collective-permute-start.14 = (bf16[256,2048]{1,0:T(8,128)(2,1)S(1)}, bf16[256,2048]{1,0:T(8,128)(2,1)S(1)}, u32[]{:S(2)}, u32[]{:S(2)}) collective-permute-start(bf16[256,2048]{1,0:T(8,128)(2,1)S(1)} %collective-permute-done.9.refs_1_), channel_id=1, source_target_pairs={{0,2},{2,0},{4,6},{6,4},{1,3},{3,1},{5,7},{7,5},{8,10},{10,8},{12,... | collective-permute-start | bytes 3145736 | tf_op jit(solution)/shard_map/ppermute | solution.py:51
  57.2 10.0 %collective-permute-start.11 = (bf16[128,2048]{1,0:T(8,128)(2,1)S(1)}, bf16[128,2048]{1,0:T(8,128)(2,1)S(1)}, u32[]{:S(2)}, u32[]{:S(2)}) collective-permute-start(bf16[128,2048]{1,0:T(8,128)(2,1)S(1)} %slice.6), channel_id=1, source_target_pairs={{0,4},{2,66},{4,0},{6,70},{1,5},{3,67},{5,1},{7,71},{8,12},{10,74}... | collective-permute-start | bytes 1572872 | tf_op jit(solution)/shard_map/ppermute | solution.py:51
  57.3 9.9 %collective-permute-start.12 = (bf16[128,2048]{1,0:T(8,128)(2,1)S(1)}, bf16[128,2048]{1,0:T(8,128)(2,1)S(1)}, u32[]{:S(2)}, u32[]{:S(2)}) collective-permute-start(bf16[128,2048]{1,0:T(8,128)(2,1)S(1)} %slice.7), channel_id=1, source_target_pairs={{0,5},{2,194},{4,1},{6,198},{1,4},{3,195},{5,0},{7,199},{8,13},{10... | collective-permute-start | bytes 1572872 | tf_op jit(solution)/shard_map/ppermute | solution.py:51
  67.2 2.8 %collective-permute-start.15 = (bf16[128,2048]{1,0:T(8,128)(2,1)S(1)}, bf16[128,2048]{1,0:T(8,128)(2,1)S(1)}, u32[]{:S(2)}, u32[]{:S(2)}) collective-permute-start(bf16[128,2048]{1,0:T(8,128)(2,1)S(1)} %collective-permute-done.11.refs_1_), channel_id=1, source_target_pairs={{0,2},{2,0},{4,6},{6,4},{1,3},{3,1},{5,7},{7,5},{8,10},{10,8},{12,... | collective-permute-start | bytes 1572872 | tf_op jit(solution)/shard_map/ppermute | solution.py:51
  68.5 2.3 %collective-permute-start.16 = (bf16[128,2048]{1,0:T(8,128)(2,1)S(1)}, bf16[128,2048]{1,0:T(8,128)(2,1)S(1)}, u32[]{:S(2)}, u32[]{:S(2)}) collective-permute-start(bf16[128,2048]{1,0:T(8,128)(2,1)S(1)} %collective-permute-done.12.refs_2_), channel_id=1, source_target_pairs={{0,2},{2,0},{4,6},{6,4},{1,3},{3,1},{5,7},{7,5},{8,10},{10,8},{12,... | collective-permute-start | bytes 1572872 | tf_op jit(solution)/shard_map/ppermute | solution.py:51

commit v3 on v2

v3 whole, which is shorter than its diff:
```python
import functools
import math

import jax
import jax.numpy as jnp
import ml_dtypes
import numpy as np
from jax import lax
from jax.experimental import pallas as pl
from jax.experimental.pallas import tpu as pltpu
from jax.sharding import Mesh
from jax.sharding import PartitionSpec as P

NFFT = 1024
LAG = 128
F = 512
SEG = 768
SUBWIN = 4
NY, NZ, NX = 4, 8, 4
AXES = ("y", "z", "xl", "core", "tm")


def dft_tables():
    product = np.mod(np.arange(SEG)[:, None] * np.arange(F)[None, :], NFFT)
    theta = product * (2.0 * math.pi / NFFT)
    table = np.concatenate([np.cos(theta), -np.sin(theta)], axis=1)
    high = table.astype(ml_dtypes.bfloat16)
    low = (table - high.astype(np.float64)).astype(ml_dtypes.bfloat16)
    return high, low


def lag_table():
    product = np.mod(np.arange(F)[:, None] * (np.arange(2 * LAG) - LAG)[None, :], NFFT)
    phase = product * (2.0 * math.pi / NFFT)
    weight = np.where(np.arange(F) == 0, 1.0, 2.0)[:, None] / math.sqrt(F * SUBWIN)
    table = np.concatenate([weight * np.cos(phase), -weight * np.sin(phase)], axis=0)
    return table.astype(np.float32).astype(ml_dtypes.bfloat16)


def device_index(y, z, x, core):
    return (((y * NZ + z) * 2 + x % 2) * 2 + core) * 2 + x // 2


def permute(value, partner):
    pairs = []
    for y in range(NY):
        for z in range(NZ):
            for x in range(NX):
                for core in range(2):
                    pairs.append((device_index(y, z, x, core), device_index(*partner(y, z, x, core))))
    return lax.ppermute(value, AXES, pairs)


def along_z(d):
    return lambda y, z, x, core: (y, z ^ d, x, core)


def along_first(d):
    return lambda y, z, x, core: (y ^ d, z, x, core) if core == 0 else (y, z, x ^ d, core)


def along_second(d):
    return lambda y, z, x, core: (y, z, x ^ d, core) if core == 0 else (y ^ d, z, x, core)


def other_core(y, z, x, core):
    return (y, z, x, 1 - core)


def other_group(y, z, x, core):
    return (y, z, x ^ 2, core)


def touch_kernel(high_ref, low_ref, out_ref):
    out_ref[...] = high_ref[0:16, 0:128] + low_ref[0:16, 0:128]


def touch(tables):
    vmem = pl.BlockSpec(memory_space=pltpu.VMEM)
    return pl.pallas_call(
        touch_kernel,
        in_specs=[vmem, vmem],
        out_specs=vmem,
        out_shape=jax.ShapeDtypeStruct((16, 128), jnp.bfloat16),
        cost_estimate=pl.CostEstimate(flops=2**10, bytes_accessed=2**10, transcendentals=0),
        compiler_params=pltpu.CompilerParams(vmem_limit_bytes=16 * 2**20),
        name="touch",
    )(*tables)


def whiten_kernel(lengths_ref, own_mask_ref, near_mask_ref, own_ref, near_ref, high_ref, low_ref, touched_ref, pair_ref, out_ref):
    del touched_ref
    tm = lax.axis_index("tm")
    x = jnp.concatenate([own_ref[...].reshape(16, SEG), near_ref[...].reshape(16, SEG)], axis=0)
    row = lax.broadcasted_iota(jnp.int32, (32, 1), 0)
    length = jnp.where(row % 16 < 8, lengths_ref[2 * tm], lengths_ref[2 * tm + 1])
    usable = jnp.zeros((32, 1), jnp.float32)
    for c in range(8):
        mask = jnp.where(row < 16, own_mask_ref[c], near_mask_ref[c])
        usable = jnp.where(row % 8 == c, mask.astype(jnp.float32), usable)
    live = lax.broadcasted_iota(jnp.int32, (32, SEG), 1) < length
    average = jnp.sum(jnp.where(live, x, 0.0), axis=1, keepdims=True) / length.astype(jnp.float32)
    centred = jnp.where(live, x - average, 0.0)
    part0 = centred.astype(jnp.bfloat16)
    rest = centred - part0.astype(jnp.float32)
    part1 = rest.astype(jnp.bfloat16)
    part2 = (rest - part1.astype(jnp.float32)).astype(jnp.bfloat16)
    parts = jnp.concatenate([part0, part1, part2], axis=0)
    by_high = jnp.dot(parts, high_ref[...], preferred_element_type=jnp.float32)
    by_low = jnp.dot(parts[:64], low_ref[...], preferred_element_type=jnp.float32)
    spectrum = by_high[:32] + (by_high[32:64] + by_low[:32] + (by_high[64:] + by_low[32:]))
    re, im = spectrum[:, :F], spectrum[:, F:]
    power = re * re + im * im
    level = jnp.mean(power, axis=1, keepdims=True)
    factor = usable / jnp.sqrt(power + 0.01 * level + 1e-06)
    white = [re * factor, im * factor]
    for k in range(2):
        for part in range(2):
            lanes = slice((2 * k + part) * F, (2 * k + part + 1) * F)
            own = white[part][8 * k : 8 * k + 8]
            pair_ref[:, lanes] = jnp.concatenate([own, white[part][16 + 8 * k : 24 + 8 * k]], axis=0).astype(jnp.bfloat16)
            out_ref[:, lanes] = own.astype(jnp.bfloat16)


def whiten(lengths, own_mask, near_mask, own, near, tables, touched):
    smem = pl.BlockSpec(memory_space=pltpu.SMEM)
    vmem = pl.BlockSpec(memory_space=pltpu.VMEM)
    return pl.pallas_call(
        whiten_kernel,
        in_specs=[smem, smem, smem, vmem, vmem, vmem, vmem, vmem],
        out_specs=[vmem, vmem],
        out_shape=[jax.ShapeDtypeStruct((rows, 4 * F), jnp.bfloat16) for rows in (16, 8)],
        compiler_params=pltpu.CompilerParams(vmem_limit_bytes=16 * 2**20),
        name="whiten",
    )(lengths, own_mask, near_mask, own, near, *tables, touched)


def fold_kernel(own_ref, other_ref, lag_ref, out_ref, rows):
    i = pl.program_id(0)
    rows[0] = own_ref[...].astype(jnp.float32)
    rows[1] = other_ref[...].astype(jnp.float32)
    mine = 4 * lax.axis_index("tm") + i
    step = 32

    @pl.loop(0, 2 * LAG, step=step)
    def _(begin):
        at = pl.ds(pl.multiple_of(begin, step), step)
        cos = lag_ref[at, :F].astype(jnp.float32)
        sin = lag_ref[at, F:].astype(jnp.float32)
        for group in range(2):
            for k in range(2):
                to = 2 * F * (2 * group + k)
                a_re = rows[group, pl.ds(mine, 1), 2 * k * F : (2 * k + 1) * F]
                a_im = rows[group, pl.ds(mine, 1), (2 * k + 1) * F : (2 * k + 2) * F]
                out_ref[at, to : to + F] = (a_re * cos + a_im * sin).astype(jnp.bfloat16)
                out_ref[at, to + F : to + 2 * F] = (a_im * cos - a_re * sin).astype(jnp.bfloat16)


def fold(own, other):
    whole = pl.BlockSpec((8, 4 * F), lambda i: (0, 0))
    return pl.pallas_call(
        fold_kernel,
        grid=(4,),
        in_specs=[whole, whole, pl.BlockSpec((2 * LAG, 2 * F), lambda i: (0, 0))],
        out_specs=pl.BlockSpec((2 * LAG, 8 * F), lambda i: (i, 0)),
        out_shape=jax.ShapeDtypeStruct((8 * LAG, 8 * F), jnp.bfloat16),
        scratch_shapes=[pltpu.VMEM((2, 8, 4 * F), jnp.float32)],
        cost_estimate=pl.CostEstimate(flops=2**20, bytes_accessed=2**10, transcendentals=0),
        compiler_params=pltpu.CompilerParams(vmem_limit_bytes=16 * 2**20),
        name="fold",
    )(own, other, jnp.asarray(np.ascontiguousarray(lag_table().T)))


ALL, TOP, BOTTOM = slice(0, 256), slice(0, 128), slice(128, 256)
NEAR = {
    0: ([(0, ALL)], [(1, ALL)], [(b, 1) for b in range(4)]),
    1: ([(0, TOP), (1, TOP)], [(0, BOTTOM), (1, BOTTOM)], [(1, 0), (1, 1), (3, 0), (3, 1)]),
}
FAR = {
    0: ([(0, ALL)], [(1, TOP), (2, TOP)], [(b, 0) for b in range(4)]),
    1: ([(0, TOP), (1, TOP)], [(0, BOTTOM), (2, TOP)], [(0, 0), (0, 1), (2, 0), (2, 1)]),
}


def part_kernel(work, count, *refs):
    chunks, folded, out_ref, blocks, stored = refs[:count], refs[count], *refs[-3:]
    y, z, xl, core = (lax.axis_index(name) for name in ("y", "z", "xl", "core"))
    half = 4 * F

    def rows_of(mine, pieces):
        rows = [mine[p][at, :] for p, at in pieces]
        return rows[0] if len(rows) == 1 else jnp.concatenate(rows, axis=0)

    def product(rows, columns):
        return lax.dot_general(rows, columns, (((1,), (1,)), ((), ())), preferred_element_type=jnp.float32)

    def run(kind, operands, job):
        first, second, offsets = job
        mine = [chunks[p] for p in operands]
        copies = []
        for i in range(4):
            at = slice(2 * LAG * i, 2 * LAG * (i + 1))
            values = product(rows_of(mine, first), folded[at, :half]) + product(rows_of(mine, second), folded[at, half:])
            for n, (dy, dxl) in enumerate(offsets):
                for g in range(NZ):
                    blocks[i, n, z ^ g] = values[64 * n + 8 * g : 64 * n + 8 * g + 8]
                copy = pltpu.make_async_copy(blocks.at[i, n], out_ref.at[i, y ^ dy, :, xl ^ dxl, kind], stored.at[i, n])
                copy.start()
                copies.append(copy)
        for copy in copies:
            copy.wait()

    for to_core in range(2):

        @pl.when(core == to_core)
        def _():
            run(*work[to_core])


def correlate_part(work, chunks, folded, out):
    count = len(chunks)
    blocks = max(len(job[2]) for _, _, job in work)
    vmem = pl.BlockSpec(memory_space=pltpu.VMEM)
    hbm = pl.BlockSpec(memory_space=pltpu.HBM)
    operands = [*chunks, folded] + ([] if out is None else [out])
    return pl.pallas_call(
        functools.partial(part_kernel, work, count),
        in_specs=[vmem] * (count + 1) + ([] if out is None else [hbm]),
        out_specs=hbm,
        out_shape=jax.ShapeDtypeStruct((4, NY, NZ, 2, 2, 8, 2 * LAG), jnp.float32),
        scratch_shapes=[
            pltpu.VMEM((4, blocks, NZ, 8, 2 * LAG), jnp.float32),
            pltpu.SemaphoreType.DMA((4, blocks)),
        ],
        input_output_aliases={} if out is None else {count + 1: 0},
        cost_estimate=pl.CostEstimate(flops=2**20, bytes_accessed=2**10, transcendentals=0),
        compiler_params=pltpu.CompilerParams(vmem_limit_bytes=24 * 2**20),
        name="correlate",
    )(*operands)


def of_own_class(part, chunks, folded, out):
    return correlate_part([(k, range(len(chunks)), part[k]) for k in (0, 1)], chunks, folded, out)


def of_other_class(part, chunks, folded, out):
    return correlate_part([(k, range(len(chunks)), part[k]) for k in (1, 0)], chunks, folded, out)


def local(traces, lengths, mask):
    near_traces, near_mask = permute(traces, along_z(1)), permute(mask, along_z(1))
    tables = [jnp.asarray(table) for table in dft_tables()]
    near_traces, near_mask, touched = lax.optimization_barrier((near_traces, near_mask, touch(tables)))
    pair, own = whiten(lengths, mask, near_mask, traces, near_traces, tables, touched)
    ring = jnp.concatenate([pair] + [permute(pair, along_z(d)) for d in (2, 4, 6)], axis=0)
    ring, own = lax.optimization_barrier((ring, own))
    other = permute(own, other_group)
    plane = jnp.concatenate([ring] + [permute(ring, along_first(d)) for d in range(1, 4)], axis=0)
    plane, own, other = lax.optimization_barrier((plane, own, other))
    near = [permute(plane, along_second(1)), permute(plane, along_second(3))]
    folded = fold(own, other)
    near[0], near[1], plane, folded = lax.optimization_barrier((near[0], near[1], plane, folded))
    top, bottom = permute(near[1][:128], along_second(1)), permute(near[0][128:], along_second(3))
    near_too = [permute(chunk, other_core) for chunk in near]
    plane_too = permute(plane, other_core)
    out = of_own_class(NEAR, near, folded, None)
    out = of_other_class(NEAR, near_too, folded, out)
    top, bottom, plane_too, out = lax.optimization_barrier((top, bottom, plane_too, out))
    top_too, bottom_too = permute(top, other_core), permute(bottom, other_core)
    out = of_own_class(FAR, [plane, top, bottom], folded, out)
    out = of_other_class(FAR, [plane_too, top_too, bottom_too], folded, out)
    return out.reshape(4, NY * NZ * 4 * 8, 2 * LAG)


def solution(mesh):
    finer = Mesh(mesh.devices.reshape(NY, NZ, 2, 2, 2), AXES)
    chan = ("y", "z", "xl", "core")
    return jax.shard_map(
        local,
        mesh=finer,
        in_specs=(P("tm", chan, None), P(), P(chan)),
        out_specs=P(AXES, None, None),
        check_vma=False,
    )
```

time: 76.3 us -> 71.9 us (0.942)
  Pallas kernels: 21 us -> 16.8 us
  local copies, waits for them, and re-layouts: 1.66 us -> 3.68 us
    pallas_call x4 -> x6, Pallas kernels: 18.7 us -> 14.5 us  [the longest x4 13.2 us: correlate_part(): pl.pallas_call(functools.partial(part_kernel, work, count), in_specs=[vme...]
    unnamed x8 -> x12, local copies, waits for them, and re-layouts: 1.57 us -> 3.59 us
    ppermute x17 -> x18, waiting for transfers between devices: 27.3 us -> 26.6 us  [permute(): return lax.ppermute(value, AXES, pairs)]
    ppermute x17 -> x18, starting transfers between devices: 24.9 us -> 24.2 us  [permute(): return lax.ppermute(value, AXES, pairs)]
  transfers between devices with their start and end apart: 17 -> 18, of which waited for: 11 -> 10; matrix products, arithmetic and copies ran while one was open for 2% -> 0% of each run, Pallas kernels for 16% -> 17%
where the time goes in v3:
time: 71.9 us; the launch traced here: 71.7 us
  waiting for transfers between devices  26.6 us (37%)
  starting transfers between devices  24.2 us (34%)
  Pallas kernels  16.8 us (23%)
  local copies, waits for them, and re-layouts  3.68 us (5%)
    ppermute x18, waiting for transfers between devices, permute(): return lax.ppermute(value, AXES, pairs)  26.6 us
    ppermute x18, starting transfers between devices, permute(): return lax.ppermute(value, AXES, pairs)  24.2 us
    pallas_call x4, Pallas kernels, correlate_part(): pl.pallas_call(functools.partial(part_kernel, work, count), in_specs=[vme...  13.2 us
    unnamed x12, local copies, waits for them, and re-layouts  3.59 us
    pallas_call x1, Pallas kernels, fold(): pl.pallas_call(fold_kernel, grid=(4,), in_specs=[whole, whole, pl.BlockSp...  2.28 us
  transfers between devices with their start and end apart: 18, of which 10 were waited for; matrix products, arithmetic and copies ran while one was open for 0% of the time, Pallas kernels for 17%

profile of v3, /device:TPU:1, one launch (start us, length us, event | category | flops | bytes accessed | tf_op | source)
XLA Modules:
  0.0 71.7 jit_solution(15204601275208913097)
XLA Ops:
  0.0 2.5 %collective-permute-start = (f32[2,8,768]{2,1,0:T(8,128)}, f32[2,8,768]{2,1,0:T(8,128)S(1)}, u32[]{:S(2)}, u32[]{:S(2)}) collective-permute-start(f32[2,8,768]{2,1,0:T(8,128)} %own_ref.1), channel_id=1, source_target_pairs={{0,8},{2,10},{4,12},{6,14},{1,9},{3,11},{5,13},{7,15},{8,0},{10,2}... | collective-permute-start | bytes 147464 | tf_op jit(solution)/shard_map/ppermute | solution.py:51
  2.5 0.0 collective-permute-start.1
  2.5 0.0 copy-start
  2.5 1.4 %copy-done = bf16[768,1024]{1,0:T(8,128)(2,1)S(1)} copy-done((bf16[768,1024]{1,0:T(8,128)(2,1)S(1)}, bf16[768,1024]{1,0:T(8,128)(2,1)}, u32[]{:S(2)}) %copy-start) | copy-done | bytes 1572888
  3.9 0.0 copy-start.1
  3.9 1.4 %copy-done.1 = bf16[768,1024]{1,0:T(8,128)(2,1)S(1)} copy-done((bf16[768,1024]{1,0:T(8,128)(2,1)S(1)}, bf16[768,1024]{1,0:T(8,128)(2,1)}, u32[]{:S(2)}) %copy-start.1) | copy-done | bytes 1572888
  5.3 0.0 copy-start.3
  5.3 0.0 copy-start.4
  5.3 0.0 copy-start.5
  5.3 0.0 collective-permute-done.1.near_mask_ref
  5.3 0.0 collective-permute-done.near_ref
  5.4 0.8 %copy-done.3 = f32[2,8,768]{2,1,0:T(8,128)S(1)} copy-done((f32[2,8,768]{2,1,0:T(8,128)S(1)}, f32[2,8,768]{2,1,0:T(8,128)}, u32[]{:S(2)}) %copy-start.3) | copy-done | bytes 49176
  6.1 0.0 copy-done.4
  6.1 0.0 copy-done.5
  6.1 1.4 %whiten.1 = (bf16[16,2048]{1,0:T(8,128)(2,1)S(1)}, bf16[8,2048]{1,0:T(8,128)(2,1)S(1)}) custom-call(s32[4]{0:T(128)S(1)} %copy-done.4, s32[8]{0:T(128)S(1)} %copy-done.5, s32[8]{0:T(128)S(1)} %collective-permute-done.1.near_mask_ref, f32[2,8,768]{2,1,0:T(8,128)S(1)} %copy-done.3, f32[2,8,768]{2,1,0:T(8,128)S(1)} %collective-permute-done.near_ref, ...), custom_call_target="tpu_custom_call" | custom-call | tf_op jit(solution)/shard_map/whiten/pallas_call | solution.py:128
  7.5 0.0 copy-start.2
  7.5 5.9 %collective-permute-start.4 = (bf16[16,2048]{1,0:T(8,128)(2,1)S(1)}, bf16[16,2048]{1,0:T(8,128)(2,1)S(1)}, u32[]{:S(2)}, u32[]{:S(2)}) collective-permute-start(bf16[16,2048]{1,0:T(8,128)(2,1)S(1)} %get-tuple-element.26), channel_id=1, source_target_pairs={{0,48},{2,50},{4,52},{6,54},{1,49},{3,51},{5,53},{7,55},{8,56},{10... | collective-permute-start | bytes 196616 | tf_op jit(solution)/shard_map/ppermute | solution.py:51
  13.4 1.0 %collective-permute-start.3 = (bf16[16,2048]{1,0:T(8,128)(2,1)S(1)}, bf16[16,2048]{1,0:T(8,128)(2,1)S(1)}, u32[]{:S(2)}, u32[]{:S(2)}) collective-permute-start(bf16[16,2048]{1,0:T(8,128)(2,1)S(1)} %get-tuple-element.26), channel_id=1, source_target_pairs={{0,32},{2,34},{4,36},{6,38},{1,33},{3,35},{5,37},{7,39},{8,40},{10... | collective-permute-start | bytes 196616 | tf_op jit(solution)/shard_map/ppermute | solution.py:51
  14.4 1.2 %collective-permute-start.2 = (bf16[16,2048]{1,0:T(8,128)(2,1)S(1)}, bf16[16,2048]{1,0:T(8,128)(2,1)S(1)}, u32[]{:S(2)}, u32[]{:S(2)}) collective-permute-start(bf16[16,2048]{1,0:T(8,128)(2,1)S(1)} %get-tuple-element.26), channel_id=1, source_target_pairs={{0,16},{2,18},{4,20},{6,22},{1,17},{3,19},{5,21},{7,23},{8,24},{10... | collective-permute-start | bytes 196616 | tf_op jit(solution)/shard_map/ppermute | solution.py:51
  15.6 0.0 collective-permute-done.4
  15.6 5.4 %collective-permute-done.3 = bf16[16,2048]{1,0:T(8,128)(2,1)S(1)} collective-permute-done((bf16[16,2048]{1,0:T(8,128)(2,1)S(1)}, bf16[16,2048]{1,0:T(8,128)(2,1)S(1)}, u32[]{:S(2)}, u32[]{:S(2)}) %collective-permute-start.3) | collective-permute-done | bytes 65568 | tf_op jit(solution)/shard_map/ppermute | solution.py:51
  21.0 1.3 %collective-permute-done.2 = bf16[16,2048]{1,0:T(8,128)(2,1)S(1)} collective-permute-done((bf16[16,2048]{1,0:T(8,128)(2,1)S(1)}, bf16[16,2048]{1,0:T(8,128)(2,1)S(1)}, u32[]{:S(2)}, u32[]{:S(2)}) %collective-permute-start.2) | collective-permute-done | bytes 65568 | tf_op jit(solution)/shard_map/ppermute | solution.py:51
  22.4 2.6 %collective-permute-start.7 = (bf16[64,2048]{1,0:T(8,128)(2,1)S(1)}, bf16[64,2048]{1,0:T(8,128)(2,1)S(1)}, u32[]{:S(2)}, u32[]{:S(2)}) collective-permute-start(bf16[64,2048]{1,0:T(8,128)(2,1)S(1)} %pad_maximum_fusion.1), channel_id=1, source_target_pairs={{0,192},{2,7},{4,196},{6,3},{1,193},{3,6},{5,197},{7,2},{8,200},{1... | collective-permute-start | bytes 786440 | tf_op jit(solution)/shard_map/ppermute | solution.py:51
  24.9 0.5 collective-permute-start.6
  25.4 0.3 collective-permute-start.5
  25.7 2.7 %collective-permute-start.8 = (bf16[8,2048]{1,0:T(8,128)(2,1)S(1)}, bf16[8,2048]{1,0:T(8,128)(2,1)S(1)}, u32[]{:S(2)}, u32[]{:S(2)}) collective-permute-start(bf16[8,2048]{1,0:T(8,128)(2,1)S(1)} %get-tuple-element.31.own_ref), channel_id=1, source_target_pairs={{0,1},{2,3},{4,5},{6,7},{1,0},{3,2},{5,4},{7,6},{8,9},{10,11},{12,... | collective-permute-start | bytes 98312 | tf_op jit(solution)/shard_map/ppermute | solution.py:51
  28.4 2.6 %collective-permute-done.7 = bf16[64,2048]{1,0:T(8,128)(2,1)S(1)} collective-permute-done((bf16[64,2048]{1,0:T(8,128)(2,1)S(1)}, bf16[64,2048]{1,0:T(8,128)(2,1)S(1)}, u32[]{:S(2)}, u32[]{:S(2)}) %collective-permute-start.7) | collective-permute-done | bytes 262176 | tf_op jit(solution)/shard_map/ppermute | solution.py:51
  31.1 0.9 %collective-permute-done.6 = bf16[64,2048]{1,0:T(8,128)(2,1)S(1)} collective-permute-done((bf16[64,2048]{1,0:T(8,128)(2,1)S(1)}, bf16[64,2048]{1,0:T(8,128)(2,1)S(1)}, u32[]{:S(2)}, u32[]{:S(2)}) %collective-permute-start.6) | collective-permute-done | bytes 262176 | tf_op jit(solution)/shard_map/ppermute | solution.py:51
  32.0 0.7 collective-permute-done.5
  32.6 0.1 pad_maximum_fusion.refs_0_
  32.7 2.5 %collective-permute-done.8.other_ref = bf16[8,2048]{1,0:T(8,128)(2,1)S(1)} collective-permute-done((bf16[8,2048]{1,0:T(8,128)(2,1)S(1)}, bf16[8,2048]{1,0:T(8,128)(2,1)S(1)}, u32[]{:S(2)}, u32[]{:S(2)}) %collective-permute-start.8) | collective-permute-done | bytes 32800 | tf_op jit(solution)/shard_map/ppermute | solution.py:51
  35.2 2.7 %collective-permute-start.10 = (bf16[256,2048]{1,0:T(8,128)(2,1)S(1)}, bf16[256,2048]{1,0:T(8,128)(2,1)S(1)}, u32[]{:S(2)}, u32[]{:S(2)}) collective-permute-start(bf16[256,2048]{1,0:T(8,128)(2,1)S(1)} %pad_maximum_fusion.refs_0_), channel_id=1, source_target_pairs={{0,5},{2,194},{4,1},{6,198},{1,4},{3,195},{5,0},{7,199},{8,13},{10... | collective-permute-start | bytes 3145736 | tf_op jit(solution)/shard_map/ppermute | solution.py:51
  37.9 0.0 collective-permute-start.9
  37.9 0.0 copy-done.2
  37.9 2.3 %fold.1.refs_2_.refs_3_ = bf16[1024,4096]{1,0:T(8,128)(2,1)S(1)} custom-call(bf16[8,2048]{1,0:T(8,128)(2,1)S(1)} %get-tuple-element.31.own_ref, bf16[8,2048]{1,0:T(8,128)(2,1)S(1)} %collective-permute-done.8.other_ref, bf16[256,1024]{1,0:T(8,128)(2,1)S(1)} %copy-done.2), custom_call_target="tpu_custom_call" | custom-call | flops 1048576 | bytes 1024 | tf_op jit(solution)/shard_map/fold/pallas_call | solution.py:161
  40.2 10.2 %collective-permute-done.10.refs_1_ = bf16[256,2048]{1,0:T(8,128)(2,1)S(1)} collective-permute-done((bf16[256,2048]{1,0:T(8,128)(2,1)S(1)}, bf16[256,2048]{1,0:T(8,128)(2,1)S(1)}, u32[]{:S(2)}, u32[]{:S(2)}) %collective-permute-start.10) | collective-permute-done | bytes 1048608 | tf_op jit(solution)/shard_map/ppermute | solution.py:51
  50.4 1.5 %collective-permute-done.9.refs_0_ = bf16[256,2048]{1,0:T(8,128)(2,1)S(1)} collective-permute-done((bf16[256,2048]{1,0:T(8,128)(2,1)S(1)}, bf16[256,2048]{1,0:T(8,128)(2,1)S(1)}, u32[]{:S(2)}, u32[]{:S(2)}) %collective-permute-start.9) | collective-permute-done | bytes 1048608 | tf_op jit(solution)/shard_map/ppermute | solution.py:51
  51.8 1.0 %collective-permute-start.15 = (bf16[256,2048]{1,0:T(8,128)(2,1)S(1)}, bf16[256,2048]{1,0:T(8,128)(2,1)S(1)}, u32[]{:S(2)}, u32[]{:S(2)}) collective-permute-start(bf16[256,2048]{1,0:T(8,128)(2,1)S(1)} %collective-permute-done.10.refs_1_), channel_id=1, source_target_pairs={{0,2},{2,0},{4,6},{6,4},{1,3},{3,1},{5,7},{7,5},{8,10},{10,8},{12,... | collective-permute-start | bytes 3145736 | tf_op jit(solution)/shard_map/ppermute | solution.py:51
  52.9 0.0 collective-permute-start.14
  52.9 0.5 collective-permute-start.13
  53.5 2.8 %collective-permute-start.12 = (bf16[128,2048]{1,0:T(8,128)(2,1)S(1)}, bf16[128,2048]{1,0:T(8,128)(2,1)S(1)}, u32[]{:S(2)}, u32[]{:S(2)}) collective-permute-start(bf16[128,2048]{1,0:T(8,128)(2,1)S(1)} %slice.7), channel_id=1, source_target_pairs={{0,5},{2,194},{4,1},{6,198},{1,4},{3,195},{5,0},{7,199},{8,13},{10... | collective-permute-start | bytes 1572872 | tf_op jit(solution)/shard_map/ppermute | solution.py:51
  56.3 0.0 collective-permute-start.11
  56.3 3.2 %correlate.4.refs_3_ = f32[4,4,8,2,2,8,256]{6,5,4,3,2,1,0:T(8,128)} custom-call(bf16[256,2048]{1,0:T(8,128)(2,1)S(1)} %collective-permute-done.9.refs_0_, bf16[256,2048]{1,0:T(8,128)(2,1)S(1)} %collective-permute-done.10.refs_1_, bf16[1024,4096]{1,0:T(8,128)(2,1)S(1)} %fold.1.refs_2_.refs_3_), custom_call_target="tpu_custom_call" | custom-call | flops 1048576 | bytes 1024 | tf_op jit(solution)/shard_map/correlate/pallas_call | solution.py:226
  59.5 0.0 collective-permute-done.15.refs_1_
  59.5 0.0 collective-permute-done.14.refs_0_
  59.5 3.2 %correlate.5.refs_4_ = f32[4,4,8,2,2,8,256]{6,5,4,3,2,1,0:T(8,128)} custom-call(bf16[256,2048]{1,0:T(8,128)(2,1)S(1)} %collective-permute-done.14.refs_0_, bf16[256,2048]{1,0:T(8,128)(2,1)S(1)} %collective-permute-done.15.refs_1_, bf16[1024,4096]{1,0:T(8,128)(2,1)S(1)} %fold.1.refs_2_.refs_3_, ...), custom_call_target="tpu_custom_call", output_to_operand_aliasing={{}: (3, {})} | custom-call | flops 1048576 | bytes 1024 | tf_op jit(solution)/shard_map/correlate/pallas_call | solution.py:226
  62.8 0.4 collective-permute-done.12.refs_2_
  63.1 1.2 %collective-permute-done.11.refs_1_ = bf16[128,2048]{1,0:T(8,128)(2,1)S(1)} collective-permute-done((bf16[128,2048]{1,0:T(8,128)(2,1)S(1)}, bf16[128,2048]{1,0:T(8,128)(2,1)S(1)}, u32[]{:S(2)}, u32[]{:S(2)}) %collective-permute-start.11) | collective-permute-done | bytes 524320 | tf_op jit(solution)/shard_map/ppermute | solution.py:51
  64.3 0.0 collective-permute-done.13.refs_0_
  64.3 0.0 collective-permute-start.16
  64.3 0.5 collective-permute-start.17
  64.8 3.2 %correlate.6.refs_4_ = f32[4,4,8,2,2,8,256]{6,5,4,3,2,1,0:T(8,128)} custom-call(bf16[256,2048]{1,0:T(8,128)(2,1)S(1)} %pad_maximum_fusion.refs_0_, bf16[128,2048]{1,0:T(8,128)(2,1)S(1)} %collective-permute-done.11.refs_1_, bf16[128,2048]{1,0:T(8,128)(2,1)S(1)} %collective-permute-done.12.refs_2_, ...), custom_call_target="tpu_custom_call", output_to_operand_aliasing={{}: (4, {})} | custom-call | flops 1048576 | bytes 1024 | tf_op jit(solution)/shard_map/correlate/pallas_call | solution.py:226
  68.0 0.0 collective-permute-done.16.refs_1_
  68.0 0.0 collective-permute-done.17.refs_2_
  68.1 3.5 %correlate.7 = f32[4,4,8,2,2,8,256]{6,5,4,3,2,1,0:T(8,128)} custom-call(bf16[256,2048]{1,0:T(8,128)(2,1)S(1)} %collective-permute-done.13.refs_0_, bf16[128,2048]{1,0:T(8,128)(2,1)S(1)} %collective-permute-done.16.refs_1_, bf16[128,2048]{1,0:T(8,128)(2,1)S(1)} %collective-permute-done.17.refs_2_, ...), custom_call_target="tpu_custom_call", output_to_operand_aliasing={{}: (4, {})} | custom-call | flops 1048576 | bytes 1024 | tf_op jit(solution)/shard_map/correlate/pallas_call | solution.py:226
  (4 shorter events, 0.1 us)
Async XLA Ops:
  0.0 5.3 %collective-permute-start = (f32[2,8,768]{2,1,0:T(8,128)}, f32[2,8,768]{2,1,0:T(8,128)S(1)}, u32[]{:S(2)}, u32[]{:S(2)}) collective-permute-start(f32[2,8,768]{2,1,0:T(8,128)} %own_ref.1), channel_id=1, source_target_pairs={{0,8},{2,10},{4,12},{6,14},{1,9},{3,11},{5,13},{7,15},{8,0},{10,2}... | collective-permute-start | bytes 147464 | tf_op jit(solution)/shard_map/ppermute | solution.py:51
  2.5 2.9 %collective-permute-start.1 = (s32[8]{0:T(128)}, s32[8]{0:T(128)S(1)}, u32[]{:S(2)}, u32[]{:S(2)}) collective-permute-start(s32[8]{0:T(128)} %own_mask_ref.1), channel_id=1, source_target_pairs={{0,8},{2,10},{4,12},{6,14},{1,9},{3,11},{5,13},{7,15},{8,0},{10,2}... | collective-permute-start | bytes 104 | tf_op jit(solution)/shard_map/ppermute | solution.py:51
  2.5 1.4 %copy-start = (bf16[768,1024]{1,0:T(8,128)(2,1)S(1)}, bf16[768,1024]{1,0:T(8,128)(2,1)}, u32[]{:S(2)}) copy-start(bf16[768,1024]{1,0:T(8,128)(2,1)} %constant.7.clone.low_ref) | copy-start | bytes 4718596
  3.9 1.4 %copy-start.1 = (bf16[768,1024]{1,0:T(8,128)(2,1)S(1)}, bf16[768,1024]{1,0:T(8,128)(2,1)}, u32[]{:S(2)}) copy-start(bf16[768,1024]{1,0:T(8,128)(2,1)} %constant.6.clone.high_ref) | copy-start | bytes 4718596
  5.3 0.8 %copy-start.3 = (f32[2,8,768]{2,1,0:T(8,128)S(1)}, f32[2,8,768]{2,1,0:T(8,128)}, u32[]{:S(2)}) copy-start(f32[2,8,768]{2,1,0:T(8,128)} %own_ref.1) | copy-start | bytes 147460
  5.3 0.8 %copy-start.4 = (s32[4]{0:T(128)S(1)}, s32[4]{0:T(128)}, u32[]{:S(2)}) copy-start(s32[4]{0:T(128)} %lengths_ref.1) | copy-start | bytes 52
  5.3 0.8 %copy-start.5 = (s32[8]{0:T(128)S(1)}, s32[8]{0:T(128)}, u32[]{:S(2)}) copy-start(s32[8]{0:T(128)} %own_mask_ref.1) | copy-start | bytes 100
  7.5 30.4 %copy-start.2 = (bf16[256,1024]{1,0:T(8,128)(2,1)S(1)}, bf16[256,1024]{1,0:T(8,128)(2,1)}, u32[]{:S(2)}) copy-start(bf16[256,1024]{1,0:T(8,128)(2,1)} %constant.8.clone.lag_ref) | copy-start | bytes 1572868
  7.5 8.1 %collective-permute-start.4 = (bf16[16,2048]{1,0:T(8,128)(2,1)S(1)}, bf16[16,2048]{1,0:T(8,128)(2,1)S(1)}, u32[]{:S(2)}, u32[]{:S(2)}) collective-permute-start(bf16[16,2048]{1,0:T(8,128)(2,1)S(1)} %get-tuple-element.26), channel_id=1, source_target_pairs={{0,48},{2,50},{4,52},{6,54},{1,49},{3,51},{5,53},{7,55},{8,56},{10... | collective-permute-start | bytes 196616 | tf_op jit(solution)/shard_map/ppermute | solution.py:51
  13.4 7.6 %collective-permute-start.3 = (bf16[16,2048]{1,0:T(8,128)(2,1)S(1)}, bf16[16,2048]{1,0:T(8,128)(2,1)S(1)}, u32[]{:S(2)}, u32[]{:S(2)}) collective-permute-start(bf16[16,2048]{1,0:T(8,128)(2,1)S(1)} %get-tuple-element.26), channel_id=1, source_target_pairs={{0,32},{2,34},{4,36},{6,38},{1,33},{3,35},{5,37},{7,39},{8,40},{10... | collective-permute-start | bytes 196616 | tf_op jit(solution)/shard_map/ppermute | solution.py:51
  14.4 7.9 %collective-permute-start.2 = (bf16[16,2048]{1,0:T(8,128)(2,1)S(1)}, bf16[16,2048]{1,0:T(8,128)(2,1)S(1)}, u32[]{:S(2)}, u32[]{:S(2)}) collective-permute-start(bf16[16,2048]{1,0:T(8,128)(2,1)S(1)} %get-tuple-element.26), channel_id=1, source_target_pairs={{0,16},{2,18},{4,20},{6,22},{1,17},{3,19},{5,21},{7,23},{8,24},{10... | collective-permute-start | bytes 196616 | tf_op jit(solution)/shard_map/ppermute | solution.py:51
  22.4 8.7 %collective-permute-start.7 = (bf16[64,2048]{1,0:T(8,128)(2,1)S(1)}, bf16[64,2048]{1,0:T(8,128)(2,1)S(1)}, u32[]{:S(2)}, u32[]{:S(2)}) collective-permute-start(bf16[64,2048]{1,0:T(8,128)(2,1)S(1)} %pad_maximum_fusion.1), channel_id=1, source_target_pairs={{0,192},{2,7},{4,196},{6,3},{1,193},{3,6},{5,197},{7,2},{8,200},{1... | collective-permute-start | bytes 786440 | tf_op jit(solution)/shard_map/ppermute | solution.py:51
  24.9 7.0 %collective-permute-start.6 = (bf16[64,2048]{1,0:T(8,128)(2,1)S(1)}, bf16[64,2048]{1,0:T(8,128)(2,1)S(1)}, u32[]{:S(2)}, u32[]{:S(2)}) collective-permute-start(bf16[64,2048]{1,0:T(8,128)(2,1)S(1)} %pad_maximum_fusion.1), channel_id=1, source_target_pairs={{0,128},{2,3},{4,132},{6,7},{1,129},{3,2},{5,133},{7,6},{8,136},{1... | collective-permute-start | bytes 786440 | tf_op jit(solution)/shard_map/ppermute | solution.py:51
  25.4 7.2 %collective-permute-start.5 = (bf16[64,2048]{1,0:T(8,128)(2,1)S(1)}, bf16[64,2048]{1,0:T(8,128)(2,1)S(1)}, u32[]{:S(2)}, u32[]{:S(2)}) collective-permute-start(bf16[64,2048]{1,0:T(8,128)(2,1)S(1)} %pad_maximum_fusion.1), channel_id=1, source_target_pairs={{0,64},{2,6},{4,68},{6,2},{1,65},{3,7},{5,69},{7,3},{8,72},{10,14}... | collective-permute-start | bytes 786440 | tf_op jit(solution)/shard_map/ppermute | solution.py:51
  25.7 9.5 %collective-permute-start.8 = (bf16[8,2048]{1,0:T(8,128)(2,1)S(1)}, bf16[8,2048]{1,0:T(8,128)(2,1)S(1)}, u32[]{:S(2)}, u32[]{:S(2)}) collective-permute-start(bf16[8,2048]{1,0:T(8,128)(2,1)S(1)} %get-tuple-element.31.own_ref), channel_id=1, source_target_pairs={{0,1},{2,3},{4,5},{6,7},{1,0},{3,2},{5,4},{7,6},{8,9},{10,11},{12,... | collective-permute-start | bytes 98312 | tf_op jit(solution)/shard_map/ppermute | solution.py:51
  35.2 15.2 %collective-permute-start.10 = (bf16[256,2048]{1,0:T(8,128)(2,1)S(1)}, bf16[256,2048]{1,0:T(8,128)(2,1)S(1)}, u32[]{:S(2)}, u32[]{:S(2)}) collective-permute-start(bf16[256,2048]{1,0:T(8,128)(2,1)S(1)} %pad_maximum_fusion.refs_0_), channel_id=1, source_target_pairs={{0,5},{2,194},{4,1},{6,198},{1,4},{3,195},{5,0},{7,199},{8,13},{10... | collective-permute-start | bytes 3145736 | tf_op jit(solution)/shard_map/ppermute | solution.py:51
  37.9 13.9 %collective-permute-start.9 = (bf16[256,2048]{1,0:T(8,128)(2,1)S(1)}, bf16[256,2048]{1,0:T(8,128)(2,1)S(1)}, u32[]{:S(2)}, u32[]{:S(2)}) collective-permute-start(bf16[256,2048]{1,0:T(8,128)(2,1)S(1)} %pad_maximum_fusion.refs_0_), channel_id=1, source_target_pairs={{0,4},{2,66},{4,0},{6,70},{1,5},{3,67},{5,1},{7,71},{8,12},{10,74}... | collective-permute-start | bytes 3145736 | tf_op jit(solution)/shard_map/ppermute | solution.py:51
  51.8 7.7 %collective-permute-start.15 = (bf16[256,2048]{1,0:T(8,128)(2,1)S(1)}, bf16[256,2048]{1,0:T(8,128)(2,1)S(1)}, u32[]{:S(2)}, u32[]{:S(2)}) collective-permute-start(bf16[256,2048]{1,0:T(8,128)(2,1)S(1)} %collective-permute-done.10.refs_1_), channel_id=1, source_target_pairs={{0,2},{2,0},{4,6},{6,4},{1,3},{3,1},{5,7},{7,5},{8,10},{10,8},{12,... | collective-permute-start | bytes 3145736 | tf_op jit(solution)/shard_map/ppermute | solution.py:51
  52.9 6.6 %collective-permute-start.14 = (bf16[256,2048]{1,0:T(8,128)(2,1)S(1)}, bf16[256,2048]{1,0:T(8,128)(2,1)S(1)}, u32[]{:S(2)}, u32[]{:S(2)}) collective-permute-start(bf16[256,2048]{1,0:T(8,128)(2,1)S(1)} %collective-permute-done.9.refs_0_), channel_id=1, source_target_pairs={{0,2},{2,0},{4,6},{6,4},{1,3},{3,1},{5,7},{7,5},{8,10},{10,8},{12,... | collective-permute-start | bytes 3145736 | tf_op jit(solution)/shard_map/ppermute | solution.py:51
  52.9 11.4 %collective-permute-start.13 = (bf16[256,2048]{1,0:T(8,128)(2,1)S(1)}, bf16[256,2048]{1,0:T(8,128)(2,1)S(1)}, u32[]{:S(2)}, u32[]{:S(2)}) collective-permute-start(bf16[256,2048]{1,0:T(8,128)(2,1)S(1)} %pad_maximum_fusion.refs_0_), channel_id=1, source_target_pairs={{0,2},{2,0},{4,6},{6,4},{1,3},{3,1},{5,7},{7,5},{8,10},{10,8},{12,... | collective-permute-start | bytes 3145736 | tf_op jit(solution)/shard_map/ppermute | solution.py:51
  53.5 9.6 %collective-permute-start.12 = (bf16[128,2048]{1,0:T(8,128)(2,1)S(1)}, bf16[128,2048]{1,0:T(8,128)(2,1)S(1)}, u32[]{:S(2)}, u32[]{:S(2)}) collective-permute-start(bf16[128,2048]{1,0:T(8,128)(2,1)S(1)} %slice.7), channel_id=1, source_target_pairs={{0,5},{2,194},{4,1},{6,198},{1,4},{3,195},{5,0},{7,199},{8,13},{10... | collective-permute-start | bytes 1572872 | tf_op jit(solution)/shard_map/ppermute | solution.py:51
  56.3 8.0 %collective-permute-start.11 = (bf16[128,2048]{1,0:T(8,128)(2,1)S(1)}, bf16[128,2048]{1,0:T(8,128)(2,1)S(1)}, u32[]{:S(2)}, u32[]{:S(2)}) collective-permute-start(bf16[128,2048]{1,0:T(8,128)(2,1)S(1)} %slice.6), channel_id=1, source_target_pairs={{0,4},{2,66},{4,0},{6,70},{1,5},{3,67},{5,1},{7,71},{8,12},{10,74}... | collective-permute-start | bytes 1572872 | tf_op jit(solution)/shard_map/ppermute | solution.py:51
  64.3 3.7 %collective-permute-start.16 = (bf16[128,2048]{1,0:T(8,128)(2,1)S(1)}, bf16[128,2048]{1,0:T(8,128)(2,1)S(1)}, u32[]{:S(2)}, u32[]{:S(2)}) collective-permute-start(bf16[128,2048]{1,0:T(8,128)(2,1)S(1)} %collective-permute-done.11.refs_1_), channel_id=1, source_target_pairs={{0,2},{2,0},{4,6},{6,4},{1,3},{3,1},{5,7},{7,5},{8,10},{10,8},{12,... | collective-permute-start | bytes 1572872 | tf_op jit(solution)/shard_map/ppermute | solution.py:51
  64.3 3.8 %collective-permute-start.17 = (bf16[128,2048]{1,0:T(8,128)(2,1)S(1)}, bf16[128,2048]{1,0:T(8,128)(2,1)S(1)}, u32[]{:S(2)}, u32[]{:S(2)}) collective-permute-start(bf16[128,2048]{1,0:T(8,128)(2,1)S(1)} %collective-permute-done.12.refs_2_), channel_id=1, source_target_pairs={{0,2},{2,0},{4,6},{6,4},{1,3},{3,1},{5,7},{7,5},{8,10},{10,8},{12,... | collective-permute-start | bytes 1572872 | tf_op jit(solution)/shard_map/ppermute | solution.py:51

commit v4 on v3

--- a/solution.py
+++ b/solution.py
@@ -17,6 +17,7 @@
 SEG = 768
 SUBWIN = 4
 NY, NZ, NX = 4, 8, 4
+Z_ORDER = (0, 2, 1, 3, 6, 4, 7, 5)
 AXES = ("y", "z", "xl", "core", "tm")
 
 
@@ -177,82 +178,146 @@
     1: ([(0, TOP), (1, TOP)], [(0, BOTTOM), (1, BOTTOM)], [(1, 0), (1, 1), (3, 0), (3, 1)]),
 }
 FAR = {
-    0: ([(0, ALL)], [(1, TOP), (2, TOP)], [(b, 0) for b in range(4)]),
+    0: (None, [(1, TOP), (2, TOP)], [(b, 0) for b in range(4)]),
     1: ([(0, TOP), (1, TOP)], [(0, BOTTOM), (2, TOP)], [(0, 0), (0, 1), (2, 0), (2, 1)]),
 }
 
 
-def part_kernel(work, count, *refs):
-    chunks, folded, out_ref, blocks, stored = refs[:count], refs[count], *refs[-3:]
+def part_kernel(work, earlier, has_early, last, count, *refs):
+    refs = list(refs)
+    chunks, folded = [refs.pop(0) for _ in range(count)], refs.pop(0)
+    early = refs.pop(0) if has_early else None
+    before = refs.pop(0) if earlier else None
+    out_ref = refs.pop(0) if earlier else None
+    result, sent = refs
     y, z, xl, core = (lax.axis_index(name) for name in ("y", "z", "xl", "core"))
     half = 4 * F
 
-    def rows_of(mine, pieces):
+    def product(mine, pieces, columns):
         rows = [mine[p][at, :] for p, at in pieces]
-        return rows[0] if len(rows) == 1 else jnp.concatenate(rows, axis=0)
-
-    def product(rows, columns):
+        rows = rows[0] if len(rows) == 1 else jnp.concatenate(rows, axis=0)
         return lax.dot_general(rows, columns, (((1,), (1,)), ((), ())), preferred_element_type=jnp.float32)
 
-    def run(kind, operands, job):
-        first, second, offsets = job
-        mine = [chunks[p] for p in operands]
+    def copies_of(source, kind, offsets, i, slot):
+        return [
+            pltpu.make_async_copy(source.at[i, n], out_ref.at[i, y ^ dy, :, xl ^ dxl, kind], sent.at[slot, i, n])
+            for n, (dy, dxl) in enumerate(offsets)
+        ]
+
+    def run(c):
         copies = []
+        if earlier:
+            for i in range(4):
+                copies += copies_of(before, earlier[c][0], earlier[c][1][2], i, 0)
+        for copy in copies:
+            copy.start()
+        kind, (first, second, offsets) = work[c]
         for i in range(4):
             at = slice(2 * LAG * i, 2 * LAG * (i + 1))
-            values = product(rows_of(mine, first), folded[at, :half]) + product(rows_of(mine, second), folded[at, half:])
-            for n, (dy, dxl) in enumerate(offsets):
+            values = early[:, at] if first is None else product(chunks, first, folded[at, :half])
+            values += product(chunks, second, folded[at, half:])
+            for n in range(len(offsets)):
                 for g in range(NZ):
-                    blocks[i, n, z ^ g] = values[64 * n + 8 * g : 64 * n + 8 * g + 8]
-                copy = pltpu.make_async_copy(blocks.at[i, n], out_ref.at[i, y ^ dy, :, xl ^ dxl, kind], stored.at[i, n])
-                copy.start()
-                copies.append(copy)
+                    result[i, n, z ^ Z_ORDER[g]] = values[64 * n + 8 * g : 64 * n + 8 * g + 8]
+            if last:
+                own = copies_of(result, kind, offsets, i, 1)
+                for copy in own:
+                    copy.start()
+                copies += own
         for copy in copies:
             copy.wait()
 
-    for to_core in range(2):
-
-        @pl.when(core == to_core)
+    for c in range(2):
+
+        @pl.when(core == c)
         def _():
-            run(*work[to_core])
-
-
-def correlate_part(work, chunks, folded, out):
-    count = len(chunks)
-    blocks = max(len(job[2]) for _, _, job in work)
-    vmem = pl.BlockSpec(memory_space=pltpu.VMEM)
-    hbm = pl.BlockSpec(memory_space=pltpu.HBM)
-    operands = [*chunks, folded] + ([] if out is None else [out])
-    return pl.pallas_call(
-        functools.partial(part_kernel, work, count),
-        in_specs=[vmem] * (count + 1) + ([] if out is None else [hbm]),
-        out_specs=hbm,
-        out_shape=jax.ShapeDtypeStruct((4, NY, NZ, 2, 2, 8, 2 * LAG), jnp.float32),
-        scratch_shapes=[
-            pltpu.VMEM((4, blocks, NZ, 8, 2 * LAG), jnp.float32),
-            pltpu.SemaphoreType.DMA((4, blocks)),
-        ],
-        input_output_aliases={} if out is None else {count + 1: 0},
-        cost_estimate=pl.CostEstimate(flops=2**20, bytes_accessed=2**10, transcendentals=0),
+            run(c)
+
+
+RESULT = (4, 4, NZ, 8, 2 * LAG)
+VMEM_SPEC = pl.BlockSpec(memory_space=pltpu.VMEM)
+HBM_SPEC = pl.BlockSpec(memory_space=pltpu.HBM)
+OUT = jax.ShapeDtypeStruct((4, NY, NZ, 2, 2, 8, 2 * LAG), jnp.float32)
+SMALL = pl.CostEstimate(flops=2**20, bytes_accessed=2**10, transcendentals=0)
+
+
+def correlate_part(work, chunks, folded, early=None, before=None, earlier=None, out=None, last=False):
+    operands = [*chunks, folded] + [array for array in (early, before) if array is not None]
+    in_specs = [VMEM_SPEC] * len(operands)
+    aliases = {}
+    if out is not None:
+        aliases = {len(operands): 0}
+        operands, in_specs = [*operands, out], [*in_specs, HBM_SPEC]
+    results = ([(HBM_SPEC, OUT)] if earlier else []) + (
+        [] if last else [(VMEM_SPEC, jax.ShapeDtypeStruct(RESULT, jnp.float32))]
+    )
+    kernel = functools.partial(part_kernel, work, earlier, early is not None, last, len(chunks))
+    return pl.pallas_call(
+        kernel if out is None else lambda *refs: kernel(*refs[: len(operands) - 1], *refs[len(operands) :]),
+        in_specs=in_specs,
+        out_specs=[spec for spec, _ in results],
+        out_shape=[shape for _, shape in results],
+        scratch_shapes=([pltpu.VMEM(RESULT, jnp.float32)] if last else []) + [pltpu.SemaphoreType.DMA((2, 4, 4))],
+        input_output_aliases=aliases,
+        cost_estimate=SMALL,
         compiler_params=pltpu.CompilerParams(vmem_limit_bytes=24 * 2**20),
         name="correlate",
     )(*operands)
 
 
-def of_own_class(part, chunks, folded, out):
-    return correlate_part([(k, range(len(chunks)), part[k]) for k in (0, 1)], chunks, folded, out)
-
-
-def of_other_class(part, chunks, folded, out):
-    return correlate_part([(k, range(len(chunks)), part[k]) for k in (1, 0)], chunks, folded, out)
+def plane_kernel(earlier, mine_ref, theirs_ref, folded, before, _, out_ref, early, sent):
+    y, xl, core = (lax.axis_index(name) for name in ("y", "xl", "core"))
+
+    def run(c, rows):
+        kind, (_, _, offsets) = earlier[c]
+        copies = [
+            pltpu.make_async_copy(before.at[i, n], out_ref.at[i, y ^ dy, :, xl ^ dxl, kind], sent.at[i, n])
+            for i in range(4)
+            for n, (dy, dxl) in enumerate(offsets)
+        ]
+        for copy in copies:
+            copy.start()
+        early[...] = lax.dot_general(
+            rows[...], folded[:, : 4 * F], (((1,), (1,)), ((), ())), preferred_element_type=jnp.float32
+        )
+        for copy in copies:
+            copy.wait()
+
+    for c in range(2):
+
+        @pl.when(core == c)
+        def _():
+            run(c, (mine_ref, theirs_ref)[c])
+
+
+def correlate_plane(mine, theirs, folded, before, earlier, out):
+    return pl.pallas_call(
+        functools.partial(plane_kernel, earlier),
+        in_specs=[VMEM_SPEC] * 4 + [HBM_SPEC],
+        out_specs=[HBM_SPEC, VMEM_SPEC],
+        out_shape=[OUT, jax.ShapeDtypeStruct((256, 8 * LAG), jnp.float32)],
+        scratch_shapes=[pltpu.SemaphoreType.DMA((4, 4))],
+        input_output_aliases={4: 0},
+        cost_estimate=SMALL,
+        compiler_params=pltpu.CompilerParams(vmem_limit_bytes=24 * 2**20),
+        name="plane",
+    )(mine, theirs, folded, before, out)
+
+
+def of_own_class(part):
+    return [(kind, part[kind]) for kind in (0, 1)]
+
+
+def of_other_class(part):
+    return [(kind, part[kind]) for kind in (1, 0)]
 
 
 def local(traces, lengths, mask):
-    near_traces, near_mask = permute(traces, along_z(1)), permute(mask, along_z(1))
+    near_traces, near_mask = permute(traces, along_z(2)), permute(mask, along_z(2))
     tables = [jnp.asarray(table) for table in dft_tables()]
     near_traces, near_mask, touched = lax.optimization_barrier((near_traces, near_mask, touch(tables)))
     pair, own = whiten(lengths, mask, near_mask, traces, near_traces, tables, touched)
-    ring = jnp.concatenate([pair] + [permute(pair, along_z(d)) for d in (2, 4, 6)], axis=0)
+    ring = jnp.concatenate([pair] + [permute(pair, along_z(d)) for d in (1, 6, 7)], axis=0)
     ring, own = lax.optimization_barrier((ring, own))
     other = permute(own, other_group)
     plane = jnp.concatenate([ring] + [permute(ring, along_first(d)) for d in range(1, 4)], axis=0)
@@ -263,12 +328,23 @@
     top, bottom = permute(near[1][:128], along_second(1)), permute(near[0][128:], along_second(3))
     near_too = [permute(chunk, other_core) for chunk in near]
     plane_too = permute(plane, other_core)
-    out = of_own_class(NEAR, near, folded, None)
-    out = of_other_class(NEAR, near_too, folded, out)
-    top, bottom, plane_too, out = lax.optimization_barrier((top, bottom, plane_too, out))
+    (before,) = correlate_part(of_own_class(NEAR), near, folded)
+    out, before = correlate_part(of_other_class(NEAR), near_too, folded, before=before, earlier=of_own_class(NEAR))
+    plane, plane_too, before, out = lax.optimization_barrier((plane, plane_too, before, out))
+    out, early = correlate_plane(plane, plane_too, folded, before, of_other_class(NEAR), out)
+    top, bottom, out, early = lax.optimization_barrier((top, bottom, out, early))
     top_too, bottom_too = permute(top, other_core), permute(bottom, other_core)
-    out = of_own_class(FAR, [plane, top, bottom], folded, out)
-    out = of_other_class(FAR, [plane_too, top_too, bottom_too], folded, out)
+    (before,) = correlate_part(of_own_class(FAR), [plane, top, bottom], folded, early)
+    (out,) = correlate_part(
+        of_other_class(FAR),
+        [plane_too, top_too, bottom_too],
+        folded,
+        early,
+        before=before,
+        earlier=of_own_class(FAR),
+        out=out,
+        last=True,
+    )
     return out.reshape(4, NY * NZ * 4 * 8, 2 * LAG)
 
 

time: 71.9 us -> 70.2 us (0.976)
  waiting for transfers between devices: 26.6 us -> 23.2 us
  starting transfers between devices: 24.2 us -> 26.3 us
  local copies, waits for them, and re-layouts: 3.68 us -> 2.91 us
    ppermute x18, waiting for transfers between devices: 26.6 us -> 23.2 us  [permute(): return lax.ppermute(value, AXES, pairs)]
    ppermute x18, starting transfers between devices: 24.2 us -> 26.3 us  [permute(): return lax.ppermute(value, AXES, pairs)]
    unnamed x12, local copies, waits for them, and re-layouts: 3.59 us -> 2.83 us
    pallas_call x4 -> x5, Pallas kernels: 13.2 us -> 13.6 us  [the longest x4 11.4 us: correlate_part(): pl.pallas_call(kernel if out is None else lambda *refs: kernel(*refs[:len...]
  transfers between devices with their start and end apart: 18 -> 18, of which waited for: 10 -> 9; matrix products, arithmetic and copies ran while one was open for 0% -> 0% of each run, Pallas kernels for 17% -> 19%
where the time goes in v4:
time: 70.2 us; the launch traced here: 70 us
  starting transfers between devices  26.3 us (37%)
  waiting for transfers between devices  23.2 us (33%)
  Pallas kernels  17.2 us (25%)
  local copies, waits for them, and re-layouts  2.91 us (4%)
    ppermute x18, starting transfers between devices, permute(): return lax.ppermute(value, AXES, pairs)  26.3 us
    ppermute x18, waiting for transfers between devices, permute(): return lax.ppermute(value, AXES, pairs)  23.2 us
    pallas_call x4, Pallas kernels, correlate_part(): pl.pallas_call(kernel if out is None else lambda *refs: kernel(*refs[:len...  11.4 us
    unnamed x12, local copies, waits for them, and re-layouts  2.83 us
    pallas_call x1, Pallas kernels, fold(): pl.pallas_call(fold_kernel, grid=(4,), in_specs=[whole, whole, pl.BlockSp...  2.28 us
    pallas_call x1, Pallas kernels, correlate_plane(): pl.pallas_call(functools.partial(plane_kernel, earlier), in_specs=[VMEM_S...  2.19 us
  transfers between devices with their start and end apart: 18, of which 9 were waited for; matrix products, arithmetic and copies ran while one was open for 0% of the time, Pallas kernels for 19%

profile of v4, /device:TPU:1, one launch (start us, length us, event | category | flops | bytes accessed | tf_op | source)
XLA Modules:
  0.0 70.0 jit_solution(3812739291401495000)
XLA Ops:
  0.0 3.8 %collective-permute-start = (f32[2,8,768]{2,1,0:T(8,128)}, f32[2,8,768]{2,1,0:T(8,128)S(1)}, u32[]{:S(2)}, u32[]{:S(2)}) collective-permute-start(f32[2,8,768]{2,1,0:T(8,128)} %own_ref.1), channel_id=1, source_target_pairs={{0,16},{2,18},{4,20},{6,22},{1,17},{3,19},{5,21},{7,23},{8,24},{10... | collective-permute-start | bytes 147464 | tf_op jit(solution)/shard_map/ppermute | solution.py:52
  3.8 0.0 collective-permute-start.1
  3.9 0.0 copy-start
  3.9 1.4 %copy-done = bf16[768,1024]{1,0:T(8,128)(2,1)S(1)} copy-done((bf16[768,1024]{1,0:T(8,128)(2,1)S(1)}, bf16[768,1024]{1,0:T(8,128)(2,1)}, u32[]{:S(2)}) %copy-start) | copy-done | bytes 1572888
  5.3 0.0 copy-start.1
  5.3 1.4 %copy-done.1 = bf16[768,1024]{1,0:T(8,128)(2,1)S(1)} copy-done((bf16[768,1024]{1,0:T(8,128)(2,1)S(1)}, bf16[768,1024]{1,0:T(8,128)(2,1)}, u32[]{:S(2)}) %copy-start.1) | copy-done | bytes 1572888
  6.7 0.0 copy-start.3
  6.7 0.0 copy-start.4
  6.7 0.0 copy-start.5
  6.7 0.9 %collective-permute-done.1.near_mask_ref = s32[8]{0:T(128)S(1)} collective-permute-done((s32[8]{0:T(128)}, s32[8]{0:T(128)S(1)}, u32[]{:S(2)}, u32[]{:S(2)}) %collective-permute-start.1) | collective-permute-done | bytes 64 | tf_op jit(solution)/shard_map/ppermute | solution.py:52
  7.6 0.0 collective-permute-done.near_ref
  7.6 0.0 copy-done.3
  7.6 0.0 copy-done.4
  7.6 0.0 copy-done.5
  7.6 1.4 %whiten.1 = (bf16[16,2048]{1,0:T(8,128)(2,1)S(1)}, bf16[8,2048]{1,0:T(8,128)(2,1)S(1)}) custom-call(s32[4]{0:T(128)S(1)} %copy-done.4, s32[8]{0:T(128)S(1)} %copy-done.5, s32[8]{0:T(128)S(1)} %collective-permute-done.1.near_mask_ref, f32[2,8,768]{2,1,0:T(8,128)S(1)} %copy-done.3, f32[2,8,768]{2,1,0:T(8,128)S(1)} %collective-permute-done.near_ref, ...), custom_call_target="tpu_custom_call" | custom-call | tf_op jit(solution)/shard_map/whiten/pallas_call | solution.py:129
  9.0 0.0 copy-start.2
  9.0 4.8 %collective-permute-start.4 = (bf16[16,2048]{1,0:T(8,128)(2,1)S(1)}, bf16[16,2048]{1,0:T(8,128)(2,1)S(1)}, u32[]{:S(2)}, u32[]{:S(2)}) collective-permute-start(bf16[16,2048]{1,0:T(8,128)(2,1)S(1)} %get-tuple-element.34), channel_id=1, source_target_pairs={{0,56},{2,58},{4,60},{6,62},{1,57},{3,59},{5,61},{7,63},{8,48},{10... | collective-permute-start | bytes 196616 | tf_op jit(solution)/shard_map/ppermute | solution.py:52
  13.9 0.5 collective-permute-start.3
  14.4 1.1 %collective-permute-start.2 = (bf16[16,2048]{1,0:T(8,128)(2,1)S(1)}, bf16[16,2048]{1,0:T(8,128)(2,1)S(1)}, u32[]{:S(2)}, u32[]{:S(2)}) collective-permute-start(bf16[16,2048]{1,0:T(8,128)(2,1)S(1)} %get-tuple-element.34), channel_id=1, source_target_pairs={{0,8},{2,10},{4,12},{6,14},{1,9},{3,11},{5,13},{7,15},{8,0},{10,2}... | collective-permute-start | bytes 196616 | tf_op jit(solution)/shard_map/ppermute | solution.py:52
  15.5 0.7 %collective-permute-done.4 = bf16[16,2048]{1,0:T(8,128)(2,1)S(1)} collective-permute-done((bf16[16,2048]{1,0:T(8,128)(2,1)S(1)}, bf16[16,2048]{1,0:T(8,128)(2,1)S(1)}, u32[]{:S(2)}, u32[]{:S(2)}) %collective-permute-start.4) | collective-permute-done | bytes 65568 | tf_op jit(solution)/shard_map/ppermute | solution.py:52
  16.2 2.9 %collective-permute-done.3 = bf16[16,2048]{1,0:T(8,128)(2,1)S(1)} collective-permute-done((bf16[16,2048]{1,0:T(8,128)(2,1)S(1)}, bf16[16,2048]{1,0:T(8,128)(2,1)S(1)}, u32[]{:S(2)}, u32[]{:S(2)}) %collective-permute-start.3) | collective-permute-done | bytes 65568 | tf_op jit(solution)/shard_map/ppermute | solution.py:52
  19.1 0.0 collective-permute-done.2
  19.2 2.6 %collective-permute-start.7 = (bf16[64,2048]{1,0:T(8,128)(2,1)S(1)}, bf16[64,2048]{1,0:T(8,128)(2,1)S(1)}, u32[]{:S(2)}, u32[]{:S(2)}) collective-permute-start(bf16[64,2048]{1,0:T(8,128)(2,1)S(1)} %pad_maximum_fusion.1), channel_id=1, source_target_pairs={{0,192},{2,7},{4,196},{6,3},{1,193},{3,6},{5,197},{7,2},{8,200},{1... | collective-permute-start | bytes 786440 | tf_op jit(solution)/shard_map/ppermute | solution.py:52
  21.7 0.5 collective-permute-start.6
  22.2 0.3 collective-permute-start.5
  22.5 2.7 %collective-permute-start.8 = (bf16[8,2048]{1,0:T(8,128)(2,1)S(1)}, bf16[8,2048]{1,0:T(8,128)(2,1)S(1)}, u32[]{:S(2)}, u32[]{:S(2)}) collective-permute-start(bf16[8,2048]{1,0:T(8,128)(2,1)S(1)} %get-tuple-element.39.own_ref), channel_id=1, source_target_pairs={{0,1},{2,3},{4,5},{6,7},{1,0},{3,2},{5,4},{7,6},{8,9},{10,11},{12,... | collective-permute-start | bytes 98312 | tf_op jit(solution)/shard_map/ppermute | solution.py:52
  25.2 2.6 %collective-permute-done.7 = bf16[64,2048]{1,0:T(8,128)(2,1)S(1)} collective-permute-done((bf16[64,2048]{1,0:T(8,128)(2,1)S(1)}, bf16[64,2048]{1,0:T(8,128)(2,1)S(1)}, u32[]{:S(2)}, u32[]{:S(2)}) %collective-permute-start.7) | collective-permute-done | bytes 262176 | tf_op jit(solution)/shard_map/ppermute | solution.py:52
  27.9 0.6 collective-permute-done.6
  28.5 0.9 %collective-permute-done.5 = bf16[64,2048]{1,0:T(8,128)(2,1)S(1)} collective-permute-done((bf16[64,2048]{1,0:T(8,128)(2,1)S(1)}, bf16[64,2048]{1,0:T(8,128)(2,1)S(1)}, u32[]{:S(2)}, u32[]{:S(2)}) %collective-permute-start.5) | collective-permute-done | bytes 262176 | tf_op jit(solution)/shard_map/ppermute | solution.py:52
  29.4 0.1 pad_maximum_fusion.mine_ref.refs_0_
  29.5 2.8 %collective-permute-done.8.other_ref = bf16[8,2048]{1,0:T(8,128)(2,1)S(1)} collective-permute-done((bf16[8,2048]{1,0:T(8,128)(2,1)S(1)}, bf16[8,2048]{1,0:T(8,128)(2,1)S(1)}, u32[]{:S(2)}, u32[]{:S(2)}) %collective-permute-start.8) | collective-permute-done | bytes 32800 | tf_op jit(solution)/shard_map/ppermute | solution.py:52
  32.3 2.4 %collective-permute-start.10 = (bf16[256,2048]{1,0:T(8,128)(2,1)S(1)}, bf16[256,2048]{1,0:T(8,128)(2,1)S(1)}, u32[]{:S(2)}, u32[]{:S(2)}) collective-permute-start(bf16[256,2048]{1,0:T(8,128)(2,1)S(1)} %pad_maximum_fusion.mine_ref.refs_0_), channel_id=1, source_target_pairs={{0,5},{2,194},{4,1},{6,198},{1,4},{3,195},{5,0},{7,199},{8,13},{10... | collective-permute-start | bytes 3145736 | tf_op jit(solution)/shard_map/ppermute | solution.py:52
  34.7 0.0 collective-permute-start.9
  34.7 0.0 copy-done.2
  34.7 2.3 %fold.1.refs_2_.folded.refs_3_ = bf16[1024,4096]{1,0:T(8,128)(2,1)S(1)} custom-call(bf16[8,2048]{1,0:T(8,128)(2,1)S(1)} %get-tuple-element.39.own_ref, bf16[8,2048]{1,0:T(8,128)(2,1)S(1)} %collective-permute-done.8.other_ref, bf16[256,1024]{1,0:T(8,128)(2,1)S(1)} %copy-done.2), custom_call_target="tpu_custom_call" | custom-call | flops 1048576 | bytes 1024 | tf_op jit(solution)/shard_map/fold/pallas_call | solution.py:162
  37.0 10.4 %collective-permute-done.10.refs_1_ = bf16[256,2048]{1,0:T(8,128)(2,1)S(1)} collective-permute-done((bf16[256,2048]{1,0:T(8,128)(2,1)S(1)}, bf16[256,2048]{1,0:T(8,128)(2,1)S(1)}, u32[]{:S(2)}, u32[]{:S(2)}) %collective-permute-start.10) | collective-permute-done | bytes 1048608 | tf_op jit(solution)/shard_map/ppermute | solution.py:52
  47.4 1.2 %collective-permute-done.9.refs_0_ = bf16[256,2048]{1,0:T(8,128)(2,1)S(1)} collective-permute-done((bf16[256,2048]{1,0:T(8,128)(2,1)S(1)}, bf16[256,2048]{1,0:T(8,128)(2,1)S(1)}, u32[]{:S(2)}, u32[]{:S(2)}) %collective-permute-start.9) | collective-permute-done | bytes 1048608 | tf_op jit(solution)/shard_map/ppermute | solution.py:52
  48.6 2.7 %collective-permute-start.12 = (bf16[256,2048]{1,0:T(8,128)(2,1)S(1)}, bf16[256,2048]{1,0:T(8,128)(2,1)S(1)}, u32[]{:S(2)}, u32[]{:S(2)}) collective-permute-start(bf16[256,2048]{1,0:T(8,128)(2,1)S(1)} %collective-permute-done.9.refs_0_), channel_id=1, source_target_pairs={{0,2},{2,0},{4,6},{6,4},{1,3},{3,1},{5,7},{7,5},{8,10},{10,8},{12,... | collective-permute-start | bytes 3145736 | tf_op jit(solution)/shard_map/ppermute | solution.py:52
  51.4 0.0 collective-permute-start.13
  51.4 0.5 collective-permute-start.11
  52.0 1.4 %collective-permute-start.14 = (bf16[128,2048]{1,0:T(8,128)(2,1)S(1)}, bf16[128,2048]{1,0:T(8,128)(2,1)S(1)}, u32[]{:S(2)}, u32[]{:S(2)}) collective-permute-start(bf16[128,2048]{1,0:T(8,128)(2,1)S(1)} %slice.6), channel_id=1, source_target_pairs={{0,4},{2,66},{4,0},{6,70},{1,5},{3,67},{5,1},{7,71},{8,12},{10,74}... | collective-permute-start | bytes 1572872 | tf_op jit(solution)/shard_map/ppermute | solution.py:52
  53.4 2.2 %collective-permute-start.15 = (bf16[128,2048]{1,0:T(8,128)(2,1)S(1)}, bf16[128,2048]{1,0:T(8,128)(2,1)S(1)}, u32[]{:S(2)}, u32[]{:S(2)}) collective-permute-start(bf16[128,2048]{1,0:T(8,128)(2,1)S(1)} %slice.7), channel_id=1, source_target_pairs={{0,5},{2,194},{4,1},{6,198},{1,4},{3,195},{5,0},{7,199},{8,13},{10... | collective-permute-start | bytes 1572872 | tf_op jit(solution)/shard_map/ppermute | solution.py:52
  55.6 2.7 %correlate.4.refs_3_ = f32[4,4,8,8,256]{4,3,2,1,0:T(8,128)S(1)} custom-call(bf16[256,2048]{1,0:T(8,128)(2,1)S(1)} %collective-permute-done.9.refs_0_, bf16[256,2048]{1,0:T(8,128)(2,1)S(1)} %collective-permute-done.10.refs_1_, bf16[1024,4096]{1,0:T(8,128)(2,1)S(1)} %fold.1.refs_2_.folded.refs_3_), custom_call_target="tpu_custom_call" | custom-call | flops 1048576 | bytes 1024 | tf_op jit(solution)/shard_map/correlate/pallas_call | solution.py:255
  58.3 0.0 collective-permute-done.12.refs_0_
  58.3 0.0 collective-permute-done.13.refs_1_
  58.3 3.4 %correlate.5 = (f32[4,4,8,2,2,8,256]{6,5,4,3,2,1,0:T(8,128)}, f32[4,4,8,8,256]{4,3,2,1,0:T(8,128)S(1)}) custom-call(bf16[256,2048]{1,0:T(8,128)(2,1)S(1)} %collective-permute-done.12.refs_0_, bf16[256,2048]{1,0:T(8,128)(2,1)S(1)} %collective-permute-done.13.refs_1_, bf16[1024,4096]{1,0:T(8,128)(2,1)S(1)} %fold.1.refs_2_.folded.refs_3_, ...), custom_call_target="tpu_custom_call" | custom-call | flops 1048576 | bytes 1024 | tf_op jit(solution)/shard_map/correlate/pallas_call | solution.py:255
  61.7 0.0 collective-permute-done.11.theirs_ref.refs_0_
  61.7 2.2 %plane.1 = (f32[4,4,8,2,2,8,256]{6,5,4,3,2,1,0:T(8,128)}, f32[256,1024]{1,0:T(8,128)S(1)}) custom-call(bf16[256,2048]{1,0:T(8,128)(2,1)S(1)} %pad_maximum_fusion.mine_ref.refs_0_, bf16[256,2048]{1,0:T(8,128)(2,1)S(1)} %collective-permute-done.11.theirs_ref.refs_0_, ...), custom_call_target="tpu_custom_call", output_to_operand_aliasing={{0}: (4, {})} | custom-call | flops 1048576 | bytes 1024 | tf_op jit(solution)/shard_map/plane/pallas_call | solution.py:294
  63.9 0.0 collective-permute-done.14.refs_1_
  63.9 0.0 collective-permute-done.15.refs_2_
  63.9 0.1 collective-permute-start.16
  64.0 0.5 collective-permute-start.17
  64.5 2.7 %correlate.6.refs_5_ = f32[4,4,8,8,256]{4,3,2,1,0:T(8,128)S(1)} custom-call(bf16[256,2048]{1,0:T(8,128)(2,1)S(1)} %pad_maximum_fusion.mine_ref.refs_0_, bf16[128,2048]{1,0:T(8,128)(2,1)S(1)} %collective-permute-done.14.refs_1_, bf16[128,2048]{1,0:T(8,128)(2,1)S(1)} %collective-permute-done.15.refs_2_, bf16[1024,4096]{1,0:T(8,128)(2,1)S(1)} %fold.1.refs_2_.folded.refs_3_, ...), custom_call_target="tpu_custom_call" | custom-call | flops 1048576 | bytes 1024 | tf_op jit(solution)/shard_map/correlate/pallas_call | solution.py:255
  67.2 0.0 collective-permute-done.16.refs_1_
  67.2 0.0 collective-permute-done.17.refs_2_
  67.2 2.6 %correlate.7 = f32[4,4,8,2,2,8,256]{6,5,4,3,2,1,0:T(8,128)} custom-call(bf16[256,2048]{1,0:T(8,128)(2,1)S(1)} %collective-permute-done.11.theirs_ref.refs_0_, bf16[128,2048]{1,0:T(8,128)(2,1)S(1)} %collective-permute-done.16.refs_1_, bf16[128,2048]{1,0:T(8,128)(2,1)S(1)} %collective-permute-done.17.refs_2_, ...), custom_call_target="tpu_custom_call", output_to_operand_aliasing={{}: (6, {})} | custom-call | flops 1048576 | bytes 1024 | tf_op jit(solution)/shard_map/correlate/pallas_call | solution.py:255
  (4 shorter events, 0.1 us)
Async XLA Ops:
  0.0 7.6 %collective-permute-start = (f32[2,8,768]{2,1,0:T(8,128)}, f32[2,8,768]{2,1,0:T(8,128)S(1)}, u32[]{:S(2)}, u32[]{:S(2)}) collective-permute-start(f32[2,8,768]{2,1,0:T(8,128)} %own_ref.1), channel_id=1, source_target_pairs={{0,16},{2,18},{4,20},{6,22},{1,17},{3,19},{5,21},{7,23},{8,24},{10... | collective-permute-start | bytes 147464 | tf_op jit(solution)/shard_map/ppermute | solution.py:52
  3.8 3.8 %collective-permute-start.1 = (s32[8]{0:T(128)}, s32[8]{0:T(128)S(1)}, u32[]{:S(2)}, u32[]{:S(2)}) collective-permute-start(s32[8]{0:T(128)} %own_mask_ref.1), channel_id=1, source_target_pairs={{0,16},{2,18},{4,20},{6,22},{1,17},{3,19},{5,21},{7,23},{8,24},{10... | collective-permute-start | bytes 104 | tf_op jit(solution)/shard_map/ppermute | solution.py:52
  3.9 1.4 %copy-start = (bf16[768,1024]{1,0:T(8,128)(2,1)S(1)}, bf16[768,1024]{1,0:T(8,128)(2,1)}, u32[]{:S(2)}) copy-start(bf16[768,1024]{1,0:T(8,128)(2,1)} %constant.7.clone.low_ref) | copy-start | bytes 4718596
  5.3 1.4 %copy-start.1 = (bf16[768,1024]{1,0:T(8,128)(2,1)S(1)}, bf16[768,1024]{1,0:T(8,128)(2,1)}, u32[]{:S(2)}) copy-start(bf16[768,1024]{1,0:T(8,128)(2,1)} %constant.6.clone.high_ref) | copy-start | bytes 4718596
  6.7 0.9 %copy-start.3 = (f32[2,8,768]{2,1,0:T(8,128)S(1)}, f32[2,8,768]{2,1,0:T(8,128)}, u32[]{:S(2)}) copy-start(f32[2,8,768]{2,1,0:T(8,128)} %own_ref.1) | copy-start | bytes 147460
  6.7 0.9 %copy-start.4 = (s32[4]{0:T(128)S(1)}, s32[4]{0:T(128)}, u32[]{:S(2)}) copy-start(s32[4]{0:T(128)} %lengths_ref.1) | copy-start | bytes 52
  6.7 0.9 %copy-start.5 = (s32[8]{0:T(128)S(1)}, s32[8]{0:T(128)}, u32[]{:S(2)}) copy-start(s32[8]{0:T(128)} %own_mask_ref.1) | copy-start | bytes 100
  9.0 25.7 %copy-start.2 = (bf16[256,1024]{1,0:T(8,128)(2,1)S(1)}, bf16[256,1024]{1,0:T(8,128)(2,1)}, u32[]{:S(2)}) copy-start(bf16[256,1024]{1,0:T(8,128)(2,1)} %constant.8.clone.lag_ref) | copy-start | bytes 1572868
  9.0 7.2 %collective-permute-start.4 = (bf16[16,2048]{1,0:T(8,128)(2,1)S(1)}, bf16[16,2048]{1,0:T(8,128)(2,1)S(1)}, u32[]{:S(2)}, u32[]{:S(2)}) collective-permute-start(bf16[16,2048]{1,0:T(8,128)(2,1)S(1)} %get-tuple-element.34), channel_id=1, source_target_pairs={{0,56},{2,58},{4,60},{6,62},{1,57},{3,59},{5,61},{7,63},{8,48},{10... | collective-permute-start | bytes 196616 | tf_op jit(solution)/shard_map/ppermute | solution.py:52
  13.9 5.3 %collective-permute-start.3 = (bf16[16,2048]{1,0:T(8,128)(2,1)S(1)}, bf16[16,2048]{1,0:T(8,128)(2,1)S(1)}, u32[]{:S(2)}, u32[]{:S(2)}) collective-permute-start(bf16[16,2048]{1,0:T(8,128)(2,1)S(1)} %get-tuple-element.34), channel_id=1, source_target_pairs={{0,48},{2,50},{4,52},{6,54},{1,49},{3,51},{5,53},{7,55},{8,56},{10... | collective-permute-start | bytes 196616 | tf_op jit(solution)/shard_map/ppermute | solution.py:52
  14.4 4.7 %collective-permute-start.2 = (bf16[16,2048]{1,0:T(8,128)(2,1)S(1)}, bf16[16,2048]{1,0:T(8,128)(2,1)S(1)}, u32[]{:S(2)}, u32[]{:S(2)}) collective-permute-start(bf16[16,2048]{1,0:T(8,128)(2,1)S(1)} %get-tuple-element.34), channel_id=1, source_target_pairs={{0,8},{2,10},{4,12},{6,14},{1,9},{3,11},{5,13},{7,15},{8,0},{10,2}... | collective-permute-start | bytes 196616 | tf_op jit(solution)/shard_map/ppermute | solution.py:52
  19.2 8.7 %collective-permute-start.7 = (bf16[64,2048]{1,0:T(8,128)(2,1)S(1)}, bf16[64,2048]{1,0:T(8,128)(2,1)S(1)}, u32[]{:S(2)}, u32[]{:S(2)}) collective-permute-start(bf16[64,2048]{1,0:T(8,128)(2,1)S(1)} %pad_maximum_fusion.1), channel_id=1, source_target_pairs={{0,192},{2,7},{4,196},{6,3},{1,193},{3,6},{5,197},{7,2},{8,200},{1... | collective-permute-start | bytes 786440 | tf_op jit(solution)/shard_map/ppermute | solution.py:52
  21.7 6.8 %collective-permute-start.6 = (bf16[64,2048]{1,0:T(8,128)(2,1)S(1)}, bf16[64,2048]{1,0:T(8,128)(2,1)S(1)}, u32[]{:S(2)}, u32[]{:S(2)}) collective-permute-start(bf16[64,2048]{1,0:T(8,128)(2,1)S(1)} %pad_maximum_fusion.1), channel_id=1, source_target_pairs={{0,128},{2,3},{4,132},{6,7},{1,129},{3,2},{5,133},{7,6},{8,136},{1... | collective-permute-start | bytes 786440 | tf_op jit(solution)/shard_map/ppermute | solution.py:52
  22.2 7.2 %collective-permute-start.5 = (bf16[64,2048]{1,0:T(8,128)(2,1)S(1)}, bf16[64,2048]{1,0:T(8,128)(2,1)S(1)}, u32[]{:S(2)}, u32[]{:S(2)}) collective-permute-start(bf16[64,2048]{1,0:T(8,128)(2,1)S(1)} %pad_maximum_fusion.1), channel_id=1, source_target_pairs={{0,64},{2,6},{4,68},{6,2},{1,65},{3,7},{5,69},{7,3},{8,72},{10,14}... | collective-permute-start | bytes 786440 | tf_op jit(solution)/shard_map/ppermute | solution.py:52
  22.5 9.8 %collective-permute-start.8 = (bf16[8,2048]{1,0:T(8,128)(2,1)S(1)}, bf16[8,2048]{1,0:T(8,128)(2,1)S(1)}, u32[]{:S(2)}, u32[]{:S(2)}) collective-permute-start(bf16[8,2048]{1,0:T(8,128)(2,1)S(1)} %get-tuple-element.39.own_ref), channel_id=1, source_target_pairs={{0,1},{2,3},{4,5},{6,7},{1,0},{3,2},{5,4},{7,6},{8,9},{10,11},{12,... | collective-permute-start | bytes 98312 | tf_op jit(solution)/shard_map/ppermute | solution.py:52
  32.3 15.2 %collective-permute-start.10 = (bf16[256,2048]{1,0:T(8,128)(2,1)S(1)}, bf16[256,2048]{1,0:T(8,128)(2,1)S(1)}, u32[]{:S(2)}, u32[]{:S(2)}) collective-permute-start(bf16[256,2048]{1,0:T(8,128)(2,1)S(1)} %pad_maximum_fusion.mine_ref.refs_0_), channel_id=1, source_target_pairs={{0,5},{2,194},{4,1},{6,198},{1,4},{3,195},{5,0},{7,199},{8,13},{10... | collective-permute-start | bytes 3145736 | tf_op jit(solution)/shard_map/ppermute | solution.py:52
  34.7 13.9 %collective-permute-start.9 = (bf16[256,2048]{1,0:T(8,128)(2,1)S(1)}, bf16[256,2048]{1,0:T(8,128)(2,1)S(1)}, u32[]{:S(2)}, u32[]{:S(2)}) collective-permute-start(bf16[256,2048]{1,0:T(8,128)(2,1)S(1)} %pad_maximum_fusion.mine_ref.refs_0_), channel_id=1, source_target_pairs={{0,4},{2,66},{4,0},{6,70},{1,5},{3,67},{5,1},{7,71},{8,12},{10,74}... | collective-permute-start | bytes 3145736 | tf_op jit(solution)/shard_map/ppermute | solution.py:52
  48.6 9.6 %collective-permute-start.12 = (bf16[256,2048]{1,0:T(8,128)(2,1)S(1)}, bf16[256,2048]{1,0:T(8,128)(2,1)S(1)}, u32[]{:S(2)}, u32[]{:S(2)}) collective-permute-start(bf16[256,2048]{1,0:T(8,128)(2,1)S(1)} %collective-permute-done.9.refs_0_), channel_id=1, source_target_pairs={{0,2},{2,0},{4,6},{6,4},{1,3},{3,1},{5,7},{7,5},{8,10},{10,8},{12,... | collective-permute-start | bytes 3145736 | tf_op jit(solution)/shard_map/ppermute | solution.py:52
  51.4 6.9 %collective-permute-start.13 = (bf16[256,2048]{1,0:T(8,128)(2,1)S(1)}, bf16[256,2048]{1,0:T(8,128)(2,1)S(1)}, u32[]{:S(2)}, u32[]{:S(2)}) collective-permute-start(bf16[256,2048]{1,0:T(8,128)(2,1)S(1)} %collective-permute-done.10.refs_1_), channel_id=1, source_target_pairs={{0,2},{2,0},{4,6},{6,4},{1,3},{3,1},{5,7},{7,5},{8,10},{10,8},{12,... | collective-permute-start | bytes 3145736 | tf_op jit(solution)/shard_map/ppermute | solution.py:52
  51.4 10.4 %collective-permute-start.11 = (bf16[256,2048]{1,0:T(8,128)(2,1)S(1)}, bf16[256,2048]{1,0:T(8,128)(2,1)S(1)}, u32[]{:S(2)}, u32[]{:S(2)}) collective-permute-start(bf16[256,2048]{1,0:T(8,128)(2,1)S(1)} %pad_maximum_fusion.mine_ref.refs_0_), channel_id=1, source_target_pairs={{0,2},{2,0},{4,6},{6,4},{1,3},{3,1},{5,7},{7,5},{8,10},{10,8},{12,... | collective-permute-start | bytes 3145736 | tf_op jit(solution)/shard_map/ppermute | solution.py:52
  52.0 12.0 %collective-permute-start.14 = (bf16[128,2048]{1,0:T(8,128)(2,1)S(1)}, bf16[128,2048]{1,0:T(8,128)(2,1)S(1)}, u32[]{:S(2)}, u32[]{:S(2)}) collective-permute-start(bf16[128,2048]{1,0:T(8,128)(2,1)S(1)} %slice.6), channel_id=1, source_target_pairs={{0,4},{2,66},{4,0},{6,70},{1,5},{3,67},{5,1},{7,71},{8,12},{10,74}... | collective-permute-start | bytes 1572872 | tf_op jit(solution)/shard_map/ppermute | solution.py:52
  53.4 10.6 %collective-permute-start.15 = (bf16[128,2048]{1,0:T(8,128)(2,1)S(1)}, bf16[128,2048]{1,0:T(8,128)(2,1)S(1)}, u32[]{:S(2)}, u32[]{:S(2)}) collective-permute-start(bf16[128,2048]{1,0:T(8,128)(2,1)S(1)} %slice.7), channel_id=1, source_target_pairs={{0,5},{2,194},{4,1},{6,198},{1,4},{3,195},{5,0},{7,199},{8,13},{10... | collective-permute-start | bytes 1572872 | tf_op jit(solution)/shard_map/ppermute | solution.py:52
  63.9 3.3 %collective-permute-start.16 = (bf16[128,2048]{1,0:T(8,128)(2,1)S(1)}, bf16[128,2048]{1,0:T(8,128)(2,1)S(1)}, u32[]{:S(2)}, u32[]{:S(2)}) collective-permute-start(bf16[128,2048]{1,0:T(8,128)(2,1)S(1)} %collective-permute-done.14.refs_1_), channel_id=1, source_target_pairs={{0,2},{2,0},{4,6},{6,4},{1,3},{3,1},{5,7},{7,5},{8,10},{10,8},{12,... | collective-permute-start | bytes 1572872 | tf_op jit(solution)/shard_map/ppermute | solution.py:52
  64.0 3.2 %collective-permute-start.17 = (bf16[128,2048]{1,0:T(8,128)(2,1)S(1)}, bf16[128,2048]{1,0:T(8,128)(2,1)S(1)}, u32[]{:S(2)}, u32[]{:S(2)}) collective-permute-start(bf16[128,2048]{1,0:T(8,128)(2,1)S(1)} %collective-permute-done.15.refs_2_), channel_id=1, source_target_pairs={{0,2},{2,0},{4,6},{6,4},{1,3},{3,1},{5,7},{7,5},{8,10},{10,8},{12,... | collective-permute-start | bytes 1572872 | tf_op jit(solution)/shard_map/ppermute | solution.py:52

commit v5 on v4

--- a/solution.py
+++ b/solution.py
@@ -174,12 +174,12 @@
 
 ALL, TOP, BOTTOM = slice(0, 256), slice(0, 128), slice(128, 256)
 NEAR = {
-    0: ([(0, ALL)], [(1, ALL)], [(b, 1) for b in range(4)]),
-    1: ([(0, TOP), (1, TOP)], [(0, BOTTOM), (1, BOTTOM)], [(1, 0), (1, 1), (3, 0), (3, 1)]),
+    0: ([(0, TOP), (1, TOP)], [(2, TOP), (3, TOP)], [(b, 1) for b in range(4)]),
+    1: ([(0, TOP), (2, TOP)], [(1, TOP), (3, TOP)], [(1, 0), (1, 1), (3, 0), (3, 1)]),
 }
 FAR = {
-    0: (None, [(1, TOP), (2, TOP)], [(b, 0) for b in range(4)]),
-    1: ([(0, TOP), (1, TOP)], [(0, BOTTOM), (2, TOP)], [(0, 0), (0, 1), (2, 0), (2, 1)]),
+    0: (None, [(2, TOP), (3, TOP)], [(b, 0) for b in range(4)]),
+    1: ([(0, TOP), (2, TOP)], [(1, TOP), (3, TOP)], [(0, 0), (0, 1), (2, 0), (2, 1)]),
 }
 
 
@@ -265,7 +265,7 @@
     )(*operands)
 
 
-def plane_kernel(earlier, mine_ref, theirs_ref, folded, before, _, out_ref, early, sent):
+def plane_kernel(earlier, top, bottom, top_too, bottom_too, folded, before, _, out_ref, early, sent):
     y, xl, core = (lax.axis_index(name) for name in ("y", "xl", "core"))
 
     def run(c, rows):
@@ -278,7 +278,10 @@
         for copy in copies:
             copy.start()
         early[...] = lax.dot_general(
-            rows[...], folded[:, : 4 * F], (((1,), (1,)), ((), ())), preferred_element_type=jnp.float32
+            jnp.concatenate([half[...] for half in rows], axis=0),
+            folded[:, : 4 * F],
+            (((1,), (1,)), ((), ())),
+            preferred_element_type=jnp.float32,
         )
         for copy in copies:
             copy.wait()
@@ -287,21 +290,21 @@
 
         @pl.when(core == c)
         def _():
-            run(c, (mine_ref, theirs_ref)[c])
+            run(c, ((top, bottom), (top_too, bottom_too))[c])
 
 
 def correlate_plane(mine, theirs, folded, before, earlier, out):
     return pl.pallas_call(
         functools.partial(plane_kernel, earlier),
-        in_specs=[VMEM_SPEC] * 4 + [HBM_SPEC],
+        in_specs=[VMEM_SPEC] * 6 + [HBM_SPEC],
         out_specs=[HBM_SPEC, VMEM_SPEC],
         out_shape=[OUT, jax.ShapeDtypeStruct((256, 8 * LAG), jnp.float32)],
         scratch_shapes=[pltpu.SemaphoreType.DMA((4, 4))],
-        input_output_aliases={4: 0},
+        input_output_aliases={6: 0},
         cost_estimate=SMALL,
         compiler_params=pltpu.CompilerParams(vmem_limit_bytes=24 * 2**20),
         name="plane",
-    )(mine, theirs, folded, before, out)
+    )(*mine, *theirs, folded, before, out)
 
 
 def of_own_class(part):
@@ -320,24 +323,28 @@
     ring = jnp.concatenate([pair] + [permute(pair, along_z(d)) for d in (1, 6, 7)], axis=0)
     ring, own = lax.optimization_barrier((ring, own))
     other = permute(own, other_group)
-    plane = jnp.concatenate([ring] + [permute(ring, along_first(d)) for d in range(1, 4)], axis=0)
-    plane, own, other = lax.optimization_barrier((plane, own, other))
-    near = [permute(plane, along_second(1)), permute(plane, along_second(3))]
+    first = [permute(ring, along_first(d)) for d in range(1, 4)]
+    top = jnp.concatenate([ring, first[0]], axis=0)
+    bottom, own, other = lax.optimization_barrier((jnp.concatenate(first[1:], axis=0), own, other))
+    near_bottom = [permute(bottom, along_second(d)) for d in (1, 3)]
+    near_top = [permute(top, along_second(d)) for d in (1, 3)]
     folded = fold(own, other)
-    near[0], near[1], plane, folded = lax.optimization_barrier((near[0], near[1], plane, folded))
-    top, bottom = permute(near[1][:128], along_second(1)), permute(near[0][128:], along_second(3))
-    near_too = [permute(chunk, other_core) for chunk in near]
-    plane_too = permute(plane, other_core)
+    near = [near_top[0], near_bottom[0], near_top[1], near_bottom[1]]
+    *near, top, bottom, folded = lax.optimization_barrier((*near, top, bottom, folded))
+    near_too = [permute(half, other_core) for half in near]
+    plane = [top, bottom]
+    plane_too = [permute(half, other_core) for half in plane]
+    far = [permute(near[2], along_second(1)), permute(near[1], along_second(3))]
     (before,) = correlate_part(of_own_class(NEAR), near, folded)
     out, before = correlate_part(of_other_class(NEAR), near_too, folded, before=before, earlier=of_own_class(NEAR))
-    plane, plane_too, before, out = lax.optimization_barrier((plane, plane_too, before, out))
+    plane_too[0], plane_too[1], before, out = lax.optimization_barrier((*plane_too, before, out))
     out, early = correlate_plane(plane, plane_too, folded, before, of_other_class(NEAR), out)
-    top, bottom, out, early = lax.optimization_barrier((top, bottom, out, early))
-    top_too, bottom_too = permute(top, other_core), permute(bottom, other_core)
-    (before,) = correlate_part(of_own_class(FAR), [plane, top, bottom], folded, early)
+    far[0], far[1], out, early = lax.optimization_barrier((*far, out, early))
+    far_too = [permute(half, other_core) for half in far]
+    (before,) = correlate_part(of_own_class(FAR), [*plane, *far], folded, early)
     (out,) = correlate_part(
         of_other_class(FAR),
-        [plane_too, top_too, bottom_too],
+        [*plane_too, *far_too],
         folded,
         early,
         before=before,

time: 70.2 us -> 69.3 us (0.987)
  waiting for transfers between devices: 23.2 us -> 18.1 us
  starting transfers between devices: 26.3 us -> 28.7 us
  local copies, waits for them, and re-layouts: 2.91 us -> 4.96 us
    ppermute x18 -> x23, waiting for transfers between devices: 23.2 us -> 18.1 us  [permute(): return lax.ppermute(value, AXES, pairs)]
    ppermute x18 -> x23, starting transfers between devices: 26.3 us -> 28.7 us  [permute(): return lax.ppermute(value, AXES, pairs)]
    unnamed x12 -> x13, local copies, waits for them, and re-layouts: 2.83 us -> 4.95 us
  transfers between devices with their start and end apart: 18 -> 23, of which waited for: 9 -> 10; matrix products, arithmetic and copies ran while one was open for 0% -> 0% of each run, Pallas kernels for 19% -> 19%
where the time goes in v5:
time: 69.3 us; the launch traced here: 69.1 us
  starting transfers between devices  28.7 us (41%)
  waiting for transfers between devices  18.1 us (26%)
  Pallas kernels  17 us (25%)
  local copies, waits for them, and re-layouts  4.96 us (7%)
    ppermute x23, starting transfers between devices, permute(): return lax.ppermute(value, AXES, pairs)  28.7 us
    ppermute x23, waiting for transfers between devices, permute(): return lax.ppermute(value, AXES, pairs)  18.1 us
    pallas_call x4, Pallas kernels, correlate_part(): pl.pallas_call(kernel if out is None else lambda *refs: kernel(*refs[:len...  11.1 us
    unnamed x13, local copies, waits for them, and re-layouts  4.95 us
    pallas_call x1, Pallas kernels, fold(): pl.pallas_call(fold_kernel, grid=(4,), in_specs=[whole, whole, pl.BlockSp...  2.28 us
    pallas_call x1, Pallas kernels, correlate_plane(): pl.pallas_call(functools.partial(plane_kernel, earlier), in_specs=[VMEM_S...  2.19 us
  transfers between devices with their start and end apart: 23, of which 10 were waited for; matrix products, arithmetic and copies ran while one was open for 0% of the time, Pallas kernels for 19%

profile of v5, /device:TPU:1, one launch (start us, length us, event | category | flops | bytes accessed | tf_op | source)
XLA Modules:
  0.0 69.1 jit_solution(1092007545683336728)
XLA Ops:
  0.0 3.8 %collective-permute-start = (f32[2,8,768]{2,1,0:T(8,128)}, f32[2,8,768]{2,1,0:T(8,128)S(1)}, u32[]{:S(2)}, u32[]{:S(2)}) collective-permute-start(f32[2,8,768]{2,1,0:T(8,128)} %own_ref.1), channel_id=1, source_target_pairs={{0,16},{2,18},{4,20},{6,22},{1,17},{3,19},{5,21},{7,23},{8,24},{10... | collective-permute-start | bytes 147464 | tf_op jit(solution)/shard_map/ppermute | solution.py:52
  3.8 0.0 collective-permute-start.1
  3.9 0.0 copy-start
  3.9 1.4 %copy-done = bf16[768,1024]{1,0:T(8,128)(2,1)S(1)} copy-done((bf16[768,1024]{1,0:T(8,128)(2,1)S(1)}, bf16[768,1024]{1,0:T(8,128)(2,1)}, u32[]{:S(2)}) %copy-start) | copy-done | bytes 1572888
  5.3 0.0 copy-start.1
  5.3 1.4 %copy-done.1 = bf16[768,1024]{1,0:T(8,128)(2,1)S(1)} copy-done((bf16[768,1024]{1,0:T(8,128)(2,1)S(1)}, bf16[768,1024]{1,0:T(8,128)(2,1)}, u32[]{:S(2)}) %copy-start.1) | copy-done | bytes 1572888
  6.7 0.0 copy-start.2
  6.7 0.9 %collective-permute-done.1.near_mask_ref = s32[8]{0:T(128)S(1)} collective-permute-done((s32[8]{0:T(128)}, s32[8]{0:T(128)S(1)}, u32[]{:S(2)}, u32[]{:S(2)}) %collective-permute-start.1) | collective-permute-done | bytes 64 | tf_op jit(solution)/shard_map/ppermute | solution.py:52
  7.6 0.0 collective-permute-done.near_ref
  7.6 0.0 copy-start.3
  7.6 0.8 %copy-done.3 = f32[2,8,768]{2,1,0:T(8,128)S(1)} copy-done((f32[2,8,768]{2,1,0:T(8,128)S(1)}, f32[2,8,768]{2,1,0:T(8,128)}, u32[]{:S(2)}) %copy-start.3) | copy-done | bytes 49176
  8.4 0.0 copy-start.4
  8.4 0.7 copy-done.4
  9.1 0.7 copy-done.5
  9.7 1.4 %whiten.1 = (bf16[16,2048]{1,0:T(8,128)(2,1)S(1)}, bf16[8,2048]{1,0:T(8,128)(2,1)S(1)}) custom-call(s32[4]{0:T(128)S(1)} %copy-done.4, s32[8]{0:T(128)S(1)} %copy-done.5, s32[8]{0:T(128)S(1)} %collective-permute-done.1.near_mask_ref, f32[2,8,768]{2,1,0:T(8,128)S(1)} %copy-done.3, f32[2,8,768]{2,1,0:T(8,128)S(1)} %collective-permute-done.near_ref, ...), custom_call_target="tpu_custom_call" | custom-call | tf_op jit(solution)/shard_map/whiten/pallas_call | solution.py:129
  11.1 4.1 %collective-permute-start.4 = (bf16[16,2048]{1,0:T(8,128)(2,1)S(1)}, bf16[16,2048]{1,0:T(8,128)(2,1)S(1)}, u32[]{:S(2)}, u32[]{:S(2)}) collective-permute-start(bf16[16,2048]{1,0:T(8,128)(2,1)S(1)} %get-tuple-element.37), channel_id=1, source_target_pairs={{0,56},{2,58},{4,60},{6,62},{1,57},{3,59},{5,61},{7,63},{8,48},{10... | collective-permute-start | bytes 196616 | tf_op jit(solution)/shard_map/ppermute | solution.py:52
  15.2 0.6 collective-permute-start.3
  15.8 1.1 %collective-permute-start.2 = (bf16[16,2048]{1,0:T(8,128)(2,1)S(1)}, bf16[16,2048]{1,0:T(8,128)(2,1)S(1)}, u32[]{:S(2)}, u32[]{:S(2)}) collective-permute-start(bf16[16,2048]{1,0:T(8,128)(2,1)S(1)} %get-tuple-element.37), channel_id=1, source_target_pairs={{0,8},{2,10},{4,12},{6,14},{1,9},{3,11},{5,13},{7,15},{8,0},{10,2}... | collective-permute-start | bytes 196616 | tf_op jit(solution)/shard_map/ppermute | solution.py:52
  16.9 0.7 %collective-permute-done.4 = bf16[16,2048]{1,0:T(8,128)(2,1)S(1)} collective-permute-done((bf16[16,2048]{1,0:T(8,128)(2,1)S(1)}, bf16[16,2048]{1,0:T(8,128)(2,1)S(1)}, u32[]{:S(2)}, u32[]{:S(2)}) %collective-permute-start.4) | collective-permute-done | bytes 65568 | tf_op jit(solution)/shard_map/ppermute | solution.py:52
  17.6 3.1 %collective-permute-done.3 = bf16[16,2048]{1,0:T(8,128)(2,1)S(1)} collective-permute-done((bf16[16,2048]{1,0:T(8,128)(2,1)S(1)}, bf16[16,2048]{1,0:T(8,128)(2,1)S(1)}, u32[]{:S(2)}, u32[]{:S(2)}) %collective-permute-start.3) | collective-permute-done | bytes 65568 | tf_op jit(solution)/shard_map/ppermute | solution.py:52
  20.7 0.0 collective-permute-done.2
  20.8 1.3 %collective-permute-start.5 = (bf16[64,2048]{1,0:T(8,128)(2,1)S(1)}, bf16[64,2048]{1,0:T(8,128)(2,1)S(1)}, u32[]{:S(2)}, u32[]{:S(2)}) collective-permute-start(bf16[64,2048]{1,0:T(8,128)(2,1)S(1)} %pad_maximum_fusion.1), channel_id=1, source_target_pairs={{0,64},{2,6},{4,68},{6,2},{1,65},{3,7},{5,69},{7,3},{8,72},{10,14}... | collective-permute-start | bytes 786440 | tf_op jit(solution)/shard_map/ppermute | solution.py:52
  22.0 1.8 %collective-permute-start.8 = (bf16[64,2048]{1,0:T(8,128)(2,1)S(1)}, bf16[64,2048]{1,0:T(8,128)(2,1)S(1)}, u32[]{:S(2)}, u32[]{:S(2)}) collective-permute-start(bf16[64,2048]{1,0:T(8,128)(2,1)S(1)} %pad_maximum_fusion.1), channel_id=1, source_target_pairs={{0,192},{2,7},{4,196},{6,3},{1,193},{3,6},{5,197},{7,2},{8,200},{1... | collective-permute-start | bytes 786440 | tf_op jit(solution)/shard_map/ppermute | solution.py:52
  23.9 0.6 collective-permute-start.7
  24.5 2.4 %collective-permute-start.9 = (bf16[8,2048]{1,0:T(8,128)(2,1)S(1)}, bf16[8,2048]{1,0:T(8,128)(2,1)S(1)}, u32[]{:S(2)}, u32[]{:S(2)}) collective-permute-start(bf16[8,2048]{1,0:T(8,128)(2,1)S(1)} %get-tuple-element.42.own_ref), channel_id=1, source_target_pairs={{0,1},{2,3},{4,5},{6,7},{1,0},{3,2},{5,4},{7,6},{8,9},{10,11},{12,... | collective-permute-start | bytes 98312 | tf_op jit(solution)/shard_map/ppermute | solution.py:52
  26.9 0.0 collective-permute-done.5
  27.0 2.8 %collective-permute-start.11 = (bf16[128,2048]{1,0:T(8,128)(2,1)S(1)}, bf16[128,2048]{1,0:T(8,128)(2,1)S(1)}, u32[]{:S(2)}, u32[]{:S(2)}) collective-permute-start(bf16[128,2048]{1,0:T(8,128)(2,1)S(1)} %constant_dynamic-update-slice_fusion.top.refs_0_), channel_id=1, source_target_pairs={{0,5},{2,194},{4,1},{6,198},{1,4},{3,195},{5,0},{7,199},{8,13},{10... | collective-permute-start | bytes 1572872 | tf_op jit(solution)/shard_map/ppermute | solution.py:52
  29.8 0.0 collective-permute-start.6
  29.8 2.1 %collective-permute-done.8 = bf16[64,2048]{1,0:T(8,128)(2,1)S(1)} collective-permute-done((bf16[64,2048]{1,0:T(8,128)(2,1)S(1)}, bf16[64,2048]{1,0:T(8,128)(2,1)S(1)}, u32[]{:S(2)}, u32[]{:S(2)}) %collective-permute-start.8) | collective-permute-done | bytes 262176 | tf_op jit(solution)/shard_map/ppermute | solution.py:52
  31.9 0.0 collective-permute-done.7
  32.0 0.0 collective-permute-done.9.other_ref
  32.0 2.8 %collective-permute-start.12 = (bf16[128,2048]{1,0:T(8,128)(2,1)S(1)}, bf16[128,2048]{1,0:T(8,128)(2,1)S(1)}, u32[]{:S(2)}, u32[]{:S(2)}) collective-permute-start(bf16[128,2048]{1,0:T(8,128)(2,1)S(1)} %pad_maximum_fusion.bottom.refs_1_), channel_id=1, source_target_pairs={{0,5},{2,194},{4,1},{6,198},{1,4},{3,195},{5,0},{7,199},{8,13},{10... | collective-permute-start | bytes 1572872 | tf_op jit(solution)/shard_map/ppermute | solution.py:52
  34.8 0.0 collective-permute-start.10
  34.8 0.0 copy-done.2
  34.8 2.3 %fold.1.refs_4_.folded = bf16[1024,4096]{1,0:T(8,128)(2,1)S(1)} custom-call(bf16[8,2048]{1,0:T(8,128)(2,1)S(1)} %get-tuple-element.42.own_ref, bf16[8,2048]{1,0:T(8,128)(2,1)S(1)} %collective-permute-done.9.other_ref, bf16[256,1024]{1,0:T(8,128)(2,1)S(1)} %copy-done.2), custom_call_target="tpu_custom_call" | custom-call | flops 1048576 | bytes 1024 | tf_op jit(solution)/shard_map/fold/pallas_call | solution.py:162
  37.1 3.7 %collective-permute-done.11.refs_2_ = bf16[128,2048]{1,0:T(8,128)(2,1)S(1)} collective-permute-done((bf16[128,2048]{1,0:T(8,128)(2,1)S(1)}, bf16[128,2048]{1,0:T(8,128)(2,1)S(1)}, u32[]{:S(2)}, u32[]{:S(2)}) %collective-permute-start.11) | collective-permute-done | bytes 524320 | tf_op jit(solution)/shard_map/ppermute | solution.py:52
  40.8 0.0 collective-permute-done.6.refs_0_
  40.8 5.6 %collective-permute-done.12.refs_3_ = bf16[128,2048]{1,0:T(8,128)(2,1)S(1)} collective-permute-done((bf16[128,2048]{1,0:T(8,128)(2,1)S(1)}, bf16[128,2048]{1,0:T(8,128)(2,1)S(1)}, u32[]{:S(2)}, u32[]{:S(2)}) %collective-permute-start.12) | collective-permute-done | bytes 524320 | tf_op jit(solution)/shard_map/ppermute | solution.py:52
  46.5 0.0 collective-permute-done.10.refs_1_
  46.5 4.3 %collective-permute-start.15 = (bf16[128,2048]{1,0:T(8,128)(2,1)S(1)}, bf16[128,2048]{1,0:T(8,128)(2,1)S(1)}, u32[]{:S(2)}, u32[]{:S(2)}) collective-permute-start(bf16[128,2048]{1,0:T(8,128)(2,1)S(1)} %collective-permute-done.6.refs_0_), channel_id=1, source_target_pairs={{0,2},{2,0},{4,6},{6,4},{1,3},{3,1},{5,7},{7,5},{8,10},{10,8},{12,... | collective-permute-start | bytes 1572872 | tf_op jit(solution)/shard_map/ppermute | solution.py:52
  50.8 0.0 collective-permute-start.18
  50.8 0.5 collective-permute-start.16
  51.3 0.0 collective-permute-start.17
  51.3 0.5 collective-permute-start.13
  51.8 0.5 collective-permute-done.15.refs_0_
  52.3 0.4 collective-permute-start.14
  52.7 0.4 collective-permute-done.18.refs_3_
  53.0 0.3 collective-permute-start.20
  53.3 0.5 collective-permute-done.16.refs_1_
  53.8 0.0 collective-permute-start.19
  53.8 2.7 %correlate.4.refs_5_ = f32[4,4,8,8,256]{4,3,2,1,0:T(8,128)S(1)} custom-call(bf16[128,2048]{1,0:T(8,128)(2,1)S(1)} %collective-permute-done.6.refs_0_, bf16[128,2048]{1,0:T(8,128)(2,1)S(1)} %collective-permute-done.10.refs_1_, bf16[128,2048]{1,0:T(8,128)(2,1)S(1)} %collective-permute-done.11.refs_2_, bf16[128,2048]{1,0:T(8,128)(2,1)S(1)} %collective-permute-done.12.refs_3_, ...), custom_call_target="tpu_custom_call" | custom-call | flops 1048576 | bytes 1024 | tf_op jit(solution)/shard_map/correlate/pallas_call | solution.py:255
  56.5 0.0 collective-permute-done.17.refs_2_
  56.5 3.4 %correlate.5 = (f32[4,4,8,2,2,8,256]{6,5,4,3,2,1,0:T(8,128)}, f32[4,4,8,8,256]{4,3,2,1,0:T(8,128)S(1)}) custom-call(bf16[128,2048]{1,0:T(8,128)(2,1)S(1)} %collective-permute-done.15.refs_0_, bf16[128,2048]{1,0:T(8,128)(2,1)S(1)} %collective-permute-done.16.refs_1_, bf16[128,2048]{1,0:T(8,128)(2,1)S(1)} %collective-permute-done.17.refs_2_, ...), custom_call_target="tpu_custom_call" | custom-call | flops 1048576 | bytes 1024 | tf_op jit(solution)/shard_map/correlate/pallas_call | solution.py:255
  59.9 0.0 collective-permute-done.13.top_too.refs_0_
  59.9 0.0 collective-permute-done.14.bottom_too.refs_1_
  59.9 2.2 %plane.1 = (f32[4,4,8,2,2,8,256]{6,5,4,3,2,1,0:T(8,128)}, f32[256,1024]{1,0:T(8,128)S(1)}) custom-call(bf16[128,2048]{1,0:T(8,128)(2,1)S(1)} %constant_dynamic-update-slice_fusion.top.refs_0_, bf16[128,2048]{1,0:T(8,128)(2,1)S(1)} %pad_maximum_fusion.bottom.refs_1_, ...), custom_call_target="tpu_custom_call", output_to_operand_aliasing={{0}: (6, {})} | custom-call | flops 1048576 | bytes 1024 | tf_op jit(solution)/shard_map/plane/pallas_call | solution.py:297
  62.1 0.4 collective-permute-done.20.refs_3_
  62.6 0.0 collective-permute-done.19.refs_2_
  62.6 1.2 %collective-permute-start.21 = (bf16[128,2048]{1,0:T(8,128)(2,1)S(1)}, bf16[128,2048]{1,0:T(8,128)(2,1)S(1)}, u32[]{:S(2)}, u32[]{:S(2)}) collective-permute-start(bf16[128,2048]{1,0:T(8,128)(2,1)S(1)} %collective-permute-done.19.refs_2_), channel_id=1, source_target_pairs={{0,2},{2,0},{4,6},{6,4},{1,3},{3,1},{5,7},{7,5},{8,10},{10,8},{12,... | collective-permute-start | bytes 1572872 | tf_op jit(solution)/shard_map/ppermute | solution.py:52
  63.8 0.0 collective-permute-start.22
  63.8 2.7 %correlate.6.refs_6_ = f32[4,4,8,8,256]{4,3,2,1,0:T(8,128)S(1)} custom-call(bf16[128,2048]{1,0:T(8,128)(2,1)S(1)} %constant_dynamic-update-slice_fusion.top.refs_0_, bf16[128,2048]{1,0:T(8,128)(2,1)S(1)} %pad_maximum_fusion.bottom.refs_1_, bf16[128,2048]{1,0:T(8,128)(2,1)S(1)} %collective-permute-done.19.refs_2_, ...), custom_call_target="tpu_custom_call" | custom-call | flops 1048576 | bytes 1024 | tf_op jit(solution)/shard_map/correlate/pallas_call | solution.py:255
  66.5 0.0 collective-permute-done.21.refs_2_
  66.5 0.0 collective-permute-done.22.refs_3_
  66.5 2.4 %correlate.7 = f32[4,4,8,2,2,8,256]{6,5,4,3,2,1,0:T(8,128)} custom-call(bf16[128,2048]{1,0:T(8,128)(2,1)S(1)} %collective-permute-done.13.top_too.refs_0_, bf16[128,2048]{1,0:T(8,128)(2,1)S(1)} %collective-permute-done.14.bottom_too.refs_1_, bf16[128,2048]{1,0:T(8,128)(2,1)S(1)} %collective-permute-done.21.refs_2_, ...), custom_call_target="tpu_custom_call", output_to_operand_aliasing={{}: (7, {})} | custom-call | flops 1048576 | bytes 1024 | tf_op jit(solution)/shard_map/correlate/pallas_call | solution.py:255
  (6 shorter events, 0.1 us)
Async XLA Ops:
  0.0 7.6 %collective-permute-start = (f32[2,8,768]{2,1,0:T(8,128)}, f32[2,8,768]{2,1,0:T(8,128)S(1)}, u32[]{:S(2)}, u32[]{:S(2)}) collective-permute-start(f32[2,8,768]{2,1,0:T(8,128)} %own_ref.1), channel_id=1, source_target_pairs={{0,16},{2,18},{4,20},{6,22},{1,17},{3,19},{5,21},{7,23},{8,24},{10... | collective-permute-start | bytes 147464 | tf_op jit(solution)/shard_map/ppermute | solution.py:52
  3.8 3.8 %collective-permute-start.1 = (s32[8]{0:T(128)}, s32[8]{0:T(128)S(1)}, u32[]{:S(2)}, u32[]{:S(2)}) collective-permute-start(s32[8]{0:T(128)} %own_mask_ref.1), channel_id=1, source_target_pairs={{0,16},{2,18},{4,20},{6,22},{1,17},{3,19},{5,21},{7,23},{8,24},{10... | collective-permute-start | bytes 104 | tf_op jit(solution)/shard_map/ppermute | solution.py:52
  3.9 1.4 %copy-start = (bf16[768,1024]{1,0:T(8,128)(2,1)S(1)}, bf16[768,1024]{1,0:T(8,128)(2,1)}, u32[]{:S(2)}) copy-start(bf16[768,1024]{1,0:T(8,128)(2,1)} %constant.7.clone.low_ref) | copy-start | bytes 4718596
  5.3 1.4 %copy-start.1 = (bf16[768,1024]{1,0:T(8,128)(2,1)S(1)}, bf16[768,1024]{1,0:T(8,128)(2,1)}, u32[]{:S(2)}) copy-start(bf16[768,1024]{1,0:T(8,128)(2,1)} %constant.6.clone.high_ref) | copy-start | bytes 4718596
  6.7 28.2 %copy-start.2 = (bf16[256,1024]{1,0:T(8,128)(2,1)S(1)}, bf16[256,1024]{1,0:T(8,128)(2,1)}, u32[]{:S(2)}) copy-start(bf16[256,1024]{1,0:T(8,128)(2,1)} %constant.8.clone.lag_ref) | copy-start | bytes 1572868
  7.6 0.8 %copy-start.3 = (f32[2,8,768]{2,1,0:T(8,128)S(1)}, f32[2,8,768]{2,1,0:T(8,128)}, u32[]{:S(2)}) copy-start(f32[2,8,768]{2,1,0:T(8,128)} %own_ref.1) | copy-start | bytes 147460
  8.4 0.7 copy-start.4
  9.1 0.7 copy-start.5
  11.1 6.5 %collective-permute-start.4 = (bf16[16,2048]{1,0:T(8,128)(2,1)S(1)}, bf16[16,2048]{1,0:T(8,128)(2,1)S(1)}, u32[]{:S(2)}, u32[]{:S(2)}) collective-permute-start(bf16[16,2048]{1,0:T(8,128)(2,1)S(1)} %get-tuple-element.37), channel_id=1, source_target_pairs={{0,56},{2,58},{4,60},{6,62},{1,57},{3,59},{5,61},{7,63},{8,48},{10... | collective-permute-start | bytes 196616 | tf_op jit(solution)/shard_map/ppermute | solution.py:52
  15.2 5.5 %collective-permute-start.3 = (bf16[16,2048]{1,0:T(8,128)(2,1)S(1)}, bf16[16,2048]{1,0:T(8,128)(2,1)S(1)}, u32[]{:S(2)}, u32[]{:S(2)}) collective-permute-start(bf16[16,2048]{1,0:T(8,128)(2,1)S(1)} %get-tuple-element.37), channel_id=1, source_target_pairs={{0,48},{2,50},{4,52},{6,54},{1,49},{3,51},{5,53},{7,55},{8,56},{10... | collective-permute-start | bytes 196616 | tf_op jit(solution)/shard_map/ppermute | solution.py:52
  15.8 4.9 %collective-permute-start.2 = (bf16[16,2048]{1,0:T(8,128)(2,1)S(1)}, bf16[16,2048]{1,0:T(8,128)(2,1)S(1)}, u32[]{:S(2)}, u32[]{:S(2)}) collective-permute-start(bf16[16,2048]{1,0:T(8,128)(2,1)S(1)} %get-tuple-element.37), channel_id=1, source_target_pairs={{0,8},{2,10},{4,12},{6,14},{1,9},{3,11},{5,13},{7,15},{8,0},{10,2}... | collective-permute-start | bytes 196616 | tf_op jit(solution)/shard_map/ppermute | solution.py:52
  20.8 6.2 %collective-permute-start.5 = (bf16[64,2048]{1,0:T(8,128)(2,1)S(1)}, bf16[64,2048]{1,0:T(8,128)(2,1)S(1)}, u32[]{:S(2)}, u32[]{:S(2)}) collective-permute-start(bf16[64,2048]{1,0:T(8,128)(2,1)S(1)} %pad_maximum_fusion.1), channel_id=1, source_target_pairs={{0,64},{2,6},{4,68},{6,2},{1,65},{3,7},{5,69},{7,3},{8,72},{10,14}... | collective-permute-start | bytes 786440 | tf_op jit(solution)/shard_map/ppermute | solution.py:52
  22.0 9.9 %collective-permute-start.8 = (bf16[64,2048]{1,0:T(8,128)(2,1)S(1)}, bf16[64,2048]{1,0:T(8,128)(2,1)S(1)}, u32[]{:S(2)}, u32[]{:S(2)}) collective-permute-start(bf16[64,2048]{1,0:T(8,128)(2,1)S(1)} %pad_maximum_fusion.1), channel_id=1, source_target_pairs={{0,192},{2,7},{4,196},{6,3},{1,193},{3,6},{5,197},{7,2},{8,200},{1... | collective-permute-start | bytes 786440 | tf_op jit(solution)/shard_map/ppermute | solution.py:52
  23.9 8.1 %collective-permute-start.7 = (bf16[64,2048]{1,0:T(8,128)(2,1)S(1)}, bf16[64,2048]{1,0:T(8,128)(2,1)S(1)}, u32[]{:S(2)}, u32[]{:S(2)}) collective-permute-start(bf16[64,2048]{1,0:T(8,128)(2,1)S(1)} %pad_maximum_fusion.1), channel_id=1, source_target_pairs={{0,128},{2,3},{4,132},{6,7},{1,129},{3,2},{5,133},{7,6},{8,136},{1... | collective-permute-start | bytes 786440 | tf_op jit(solution)/shard_map/ppermute | solution.py:52
  24.5 7.5 %collective-permute-start.9 = (bf16[8,2048]{1,0:T(8,128)(2,1)S(1)}, bf16[8,2048]{1,0:T(8,128)(2,1)S(1)}, u32[]{:S(2)}, u32[]{:S(2)}) collective-permute-start(bf16[8,2048]{1,0:T(8,128)(2,1)S(1)} %get-tuple-element.42.own_ref), channel_id=1, source_target_pairs={{0,1},{2,3},{4,5},{6,7},{1,0},{3,2},{5,4},{7,6},{8,9},{10,11},{12,... | collective-permute-start | bytes 98312 | tf_op jit(solution)/shard_map/ppermute | solution.py:52
  27.0 13.9 %collective-permute-start.11 = (bf16[128,2048]{1,0:T(8,128)(2,1)S(1)}, bf16[128,2048]{1,0:T(8,128)(2,1)S(1)}, u32[]{:S(2)}, u32[]{:S(2)}) collective-permute-start(bf16[128,2048]{1,0:T(8,128)(2,1)S(1)} %constant_dynamic-update-slice_fusion.top.refs_0_), channel_id=1, source_target_pairs={{0,5},{2,194},{4,1},{6,198},{1,4},{3,195},{5,0},{7,199},{8,13},{10... | collective-permute-start | bytes 1572872 | tf_op jit(solution)/shard_map/ppermute | solution.py:52
  29.8 11.1 %collective-permute-start.6 = (bf16[128,2048]{1,0:T(8,128)(2,1)S(1)}, bf16[128,2048]{1,0:T(8,128)(2,1)S(1)}, u32[]{:S(2)}, u32[]{:S(2)}) collective-permute-start(bf16[128,2048]{1,0:T(8,128)(2,1)S(1)} %constant_dynamic-update-slice_fusion.top.refs_0_), channel_id=1, source_target_pairs={{0,4},{2,66},{4,0},{6,70},{1,5},{3,67},{5,1},{7,71},{8,12},{10,74}... | collective-permute-start | bytes 1572872 | tf_op jit(solution)/shard_map/ppermute | solution.py:52
  32.0 14.5 %collective-permute-start.12 = (bf16[128,2048]{1,0:T(8,128)(2,1)S(1)}, bf16[128,2048]{1,0:T(8,128)(2,1)S(1)}, u32[]{:S(2)}, u32[]{:S(2)}) collective-permute-start(bf16[128,2048]{1,0:T(8,128)(2,1)S(1)} %pad_maximum_fusion.bottom.refs_1_), channel_id=1, source_target_pairs={{0,5},{2,194},{4,1},{6,198},{1,4},{3,195},{5,0},{7,199},{8,13},{10... | collective-permute-start | bytes 1572872 | tf_op jit(solution)/shard_map/ppermute | solution.py:52
  34.8 11.6 %collective-permute-start.10 = (bf16[128,2048]{1,0:T(8,128)(2,1)S(1)}, bf16[128,2048]{1,0:T(8,128)(2,1)S(1)}, u32[]{:S(2)}, u32[]{:S(2)}) collective-permute-start(bf16[128,2048]{1,0:T(8,128)(2,1)S(1)} %pad_maximum_fusion.bottom.refs_1_), channel_id=1, source_target_pairs={{0,4},{2,66},{4,0},{6,70},{1,5},{3,67},{5,1},{7,71},{8,12},{10,74}... | collective-permute-start | bytes 1572872 | tf_op jit(solution)/shard_map/ppermute | solution.py:52
  46.5 5.8 %collective-permute-start.15 = (bf16[128,2048]{1,0:T(8,128)(2,1)S(1)}, bf16[128,2048]{1,0:T(8,128)(2,1)S(1)}, u32[]{:S(2)}, u32[]{:S(2)}) collective-permute-start(bf16[128,2048]{1,0:T(8,128)(2,1)S(1)} %collective-permute-done.6.refs_0_), channel_id=1, source_target_pairs={{0,2},{2,0},{4,6},{6,4},{1,3},{3,1},{5,7},{7,5},{8,10},{10,8},{12,... | collective-permute-start | bytes 1572872 | tf_op jit(solution)/shard_map/ppermute | solution.py:52
  50.8 2.3 %collective-permute-start.18 = (bf16[128,2048]{1,0:T(8,128)(2,1)S(1)}, bf16[128,2048]{1,0:T(8,128)(2,1)S(1)}, u32[]{:S(2)}, u32[]{:S(2)}) collective-permute-start(bf16[128,2048]{1,0:T(8,128)(2,1)S(1)} %collective-permute-done.12.refs_3_), channel_id=1, source_target_pairs={{0,2},{2,0},{4,6},{6,4},{1,3},{3,1},{5,7},{7,5},{8,10},{10,8},{12,... | collective-permute-start | bytes 1572872 | tf_op jit(solution)/shard_map/ppermute | solution.py:52
  50.8 3.0 %collective-permute-start.16 = (bf16[128,2048]{1,0:T(8,128)(2,1)S(1)}, bf16[128,2048]{1,0:T(8,128)(2,1)S(1)}, u32[]{:S(2)}, u32[]{:S(2)}) collective-permute-start(bf16[128,2048]{1,0:T(8,128)(2,1)S(1)} %collective-permute-done.10.refs_1_), channel_id=1, source_target_pairs={{0,2},{2,0},{4,6},{6,4},{1,3},{3,1},{5,7},{7,5},{8,10},{10,8},{12,... | collective-permute-start | bytes 1572872 | tf_op jit(solution)/shard_map/ppermute | solution.py:52
  51.3 5.2 %collective-permute-start.17 = (bf16[128,2048]{1,0:T(8,128)(2,1)S(1)}, bf16[128,2048]{1,0:T(8,128)(2,1)S(1)}, u32[]{:S(2)}, u32[]{:S(2)}) collective-permute-start(bf16[128,2048]{1,0:T(8,128)(2,1)S(1)} %collective-permute-done.11.refs_2_), channel_id=1, source_target_pairs={{0,2},{2,0},{4,6},{6,4},{1,3},{3,1},{5,7},{7,5},{8,10},{10,8},{12,... | collective-permute-start | bytes 1572872 | tf_op jit(solution)/shard_map/ppermute | solution.py:52
  51.3 8.7 %collective-permute-start.13 = (bf16[128,2048]{1,0:T(8,128)(2,1)S(1)}, bf16[128,2048]{1,0:T(8,128)(2,1)S(1)}, u32[]{:S(2)}, u32[]{:S(2)}) collective-permute-start(bf16[128,2048]{1,0:T(8,128)(2,1)S(1)} %constant_dynamic-update-slice_fusion.top.refs_0_), channel_id=1, source_target_pairs={{0,2},{2,0},{4,6},{6,4},{1,3},{3,1},{5,7},{7,5},{8,10},{10,8},{12,... | collective-permute-start | bytes 1572872 | tf_op jit(solution)/shard_map/ppermute | solution.py:52
  52.3 7.6 %collective-permute-start.14 = (bf16[128,2048]{1,0:T(8,128)(2,1)S(1)}, bf16[128,2048]{1,0:T(8,128)(2,1)S(1)}, u32[]{:S(2)}, u32[]{:S(2)}) collective-permute-start(bf16[128,2048]{1,0:T(8,128)(2,1)S(1)} %pad_maximum_fusion.bottom.refs_1_), channel_id=1, source_target_pairs={{0,2},{2,0},{4,6},{6,4},{1,3},{3,1},{5,7},{7,5},{8,10},{10,8},{12,... | collective-permute-start | bytes 1572872 | tf_op jit(solution)/shard_map/ppermute | solution.py:52
  53.0 9.5 %collective-permute-start.20 = (bf16[128,2048]{1,0:T(8,128)(2,1)S(1)}, bf16[128,2048]{1,0:T(8,128)(2,1)S(1)}, u32[]{:S(2)}, u32[]{:S(2)}) collective-permute-start(bf16[128,2048]{1,0:T(8,128)(2,1)S(1)} %collective-permute-done.10.refs_1_), channel_id=1, source_target_pairs={{0,5},{2,194},{4,1},{6,198},{1,4},{3,195},{5,0},{7,199},{8,13},{10... | collective-permute-start | bytes 1572872 | tf_op jit(solution)/shard_map/ppermute | solution.py:52
  53.8 8.8 %collective-permute-start.19 = (bf16[128,2048]{1,0:T(8,128)(2,1)S(1)}, bf16[128,2048]{1,0:T(8,128)(2,1)S(1)}, u32[]{:S(2)}, u32[]{:S(2)}) collective-permute-start(bf16[128,2048]{1,0:T(8,128)(2,1)S(1)} %collective-permute-done.11.refs_2_), channel_id=1, source_target_pairs={{0,4},{2,66},{4,0},{6,70},{1,5},{3,67},{5,1},{7,71},{8,12},{10,74}... | collective-permute-start | bytes 1572872 | tf_op jit(solution)/shard_map/ppermute | solution.py:52
  62.6 3.9 %collective-permute-start.21 = (bf16[128,2048]{1,0:T(8,128)(2,1)S(1)}, bf16[128,2048]{1,0:T(8,128)(2,1)S(1)}, u32[]{:S(2)}, u32[]{:S(2)}) collective-permute-start(bf16[128,2048]{1,0:T(8,128)(2,1)S(1)} %collective-permute-done.19.refs_2_), channel_id=1, source_target_pairs={{0,2},{2,0},{4,6},{6,4},{1,3},{3,1},{5,7},{7,5},{8,10},{10,8},{12,... | collective-permute-start | bytes 1572872 | tf_op jit(solution)/shard_map/ppermute | solution.py:52
  63.8 2.7 %collective-permute-start.22 = (bf16[128,2048]{1,0:T(8,128)(2,1)S(1)}, bf16[128,2048]{1,0:T(8,128)(2,1)S(1)}, u32[]{:S(2)}, u32[]{:S(2)}) collective-permute-start(bf16[128,2048]{1,0:T(8,128)(2,1)S(1)} %collective-permute-done.20.refs_3_), channel_id=1, source_target_pairs={{0,2},{2,0},{4,6},{6,4},{1,3},{3,1},{5,7},{7,5},{8,10},{10,8},{12,... | collective-permute-start | bytes 1572872 | tf_op jit(solution)/shard_map/ppermute | solution.py:52

commit v6 on v5

--- a/solution.py
+++ b/solution.py
@@ -183,6 +183,16 @@
 }
 
 
+NEAR_TOO = {
+    0: ([(0, TOP), (1, TOP)], [(0, BOTTOM), (1, BOTTOM)], NEAR[0][2]),
+    1: ([(0, ALL)], [(1, ALL)], NEAR[1][2]),
+}
+FAR_TOO = {
+    0: (None, [(1, TOP), (2, TOP)], FAR[0][2]),
+    1: ([(0, TOP), (1, TOP)], [(0, BOTTOM), (2, TOP)], FAR[1][2]),
+}
+
+
 def part_kernel(work, earlier, has_early, last, count, *refs):
     refs = list(refs)
     chunks, folded = [refs.pop(0) for _ in range(count)], refs.pop(0)
@@ -265,7 +275,7 @@
     )(*operands)
 
 
-def plane_kernel(earlier, top, bottom, top_too, bottom_too, folded, before, _, out_ref, early, sent):
+def plane_kernel(earlier, top, bottom, plane_too, folded, before, _, out_ref, early, sent):
     y, xl, core = (lax.axis_index(name) for name in ("y", "xl", "core"))
 
     def run(c, rows):
@@ -290,21 +300,21 @@
 
         @pl.when(core == c)
         def _():
-            run(c, ((top, bottom), (top_too, bottom_too))[c])
+            run(c, ((top, bottom), (plane_too,))[c])
 
 
 def correlate_plane(mine, theirs, folded, before, earlier, out):
     return pl.pallas_call(
         functools.partial(plane_kernel, earlier),
-        in_specs=[VMEM_SPEC] * 6 + [HBM_SPEC],
+        in_specs=[VMEM_SPEC] * 5 + [HBM_SPEC],
         out_specs=[HBM_SPEC, VMEM_SPEC],
         out_shape=[OUT, jax.ShapeDtypeStruct((256, 8 * LAG), jnp.float32)],
         scratch_shapes=[pltpu.SemaphoreType.DMA((4, 4))],
-        input_output_aliases={6: 0},
+        input_output_aliases={5: 0},
         cost_estimate=SMALL,
         compiler_params=pltpu.CompilerParams(vmem_limit_bytes=24 * 2**20),
         name="plane",
-    )(*mine, *theirs, folded, before, out)
+    )(*mine, theirs, folded, before, out)
 
 
 def of_own_class(part):
@@ -321,30 +331,32 @@
     near_traces, near_mask, touched = lax.optimization_barrier((near_traces, near_mask, touch(tables)))
     pair, own = whiten(lengths, mask, near_mask, traces, near_traces, tables, touched)
     ring = jnp.concatenate([pair] + [permute(pair, along_z(d)) for d in (1, 6, 7)], axis=0)
-    ring, own = lax.optimization_barrier((ring, own))
     other = permute(own, other_group)
+    ring, own, other = lax.optimization_barrier((ring, own, other))
     first = [permute(ring, along_first(d)) for d in range(1, 4)]
     top = jnp.concatenate([ring, first[0]], axis=0)
-    bottom, own, other = lax.optimization_barrier((jnp.concatenate(first[1:], axis=0), own, other))
+    bottom = jnp.concatenate(first[1:], axis=0)
     near_bottom = [permute(bottom, along_second(d)) for d in (1, 3)]
     near_top = [permute(top, along_second(d)) for d in (1, 3)]
     folded = fold(own, other)
     near = [near_top[0], near_bottom[0], near_top[1], near_bottom[1]]
-    *near, top, bottom, folded = lax.optimization_barrier((*near, top, bottom, folded))
-    near_too = [permute(half, other_core) for half in near]
-    plane = [top, bottom]
-    plane_too = [permute(half, other_core) for half in plane]
+    tops = jnp.concatenate([near_top[0], near_top[1]], axis=0)
+    plane = jnp.concatenate([top, bottom], axis=0)
+    *near, top, bottom, folded, tops, plane = lax.optimization_barrier((*near, top, bottom, folded, tops, plane))
     far = [permute(near[2], along_second(1)), permute(near[1], along_second(3))]
+    bottoms = jnp.concatenate([near[1], near[3]], axis=0)
+    near_too = [permute(chunk, other_core) for chunk in (tops, bottoms)]
+    plane_too = permute(plane, other_core)
     (before,) = correlate_part(of_own_class(NEAR), near, folded)
-    out, before = correlate_part(of_other_class(NEAR), near_too, folded, before=before, earlier=of_own_class(NEAR))
-    plane_too[0], plane_too[1], before, out = lax.optimization_barrier((*plane_too, before, out))
-    out, early = correlate_plane(plane, plane_too, folded, before, of_other_class(NEAR), out)
+    out, before = correlate_part(of_other_class(NEAR_TOO), near_too, folded, before=before, earlier=of_own_class(NEAR))
+    plane_too, before, out = lax.optimization_barrier((plane_too, before, out))
+    out, early = correlate_plane([top, bottom], plane_too, folded, before, of_other_class(NEAR), out)
     far[0], far[1], out, early = lax.optimization_barrier((*far, out, early))
     far_too = [permute(half, other_core) for half in far]
-    (before,) = correlate_part(of_own_class(FAR), [*plane, *far], folded, early)
+    (before,) = correlate_part(of_own_class(FAR), [top, bottom, *far], folded, early)
     (out,) = correlate_part(
-        of_other_class(FAR),
-        [*plane_too, *far_too],
+        of_other_class(FAR_TOO),
+        [plane_too, *far_too],
         folded,
         early,
         before=before,

time: 69.3 us -> 66.8 us (0.964)
  local copies, waits for them, and re-layouts: 4.96 us -> 2.9 us
  waiting for transfers between devices: 18.1 us -> 16.8 us
    unnamed x13 -> x14, local copies, waits for them, and re-layouts: 4.95 us -> 2.87 us
    ppermute x23 -> x20, waiting for transfers between devices: 18.1 us -> 16.8 us  [permute(): return lax.ppermute(value, AXES, pairs)]
    ppermute x23 -> x20, starting transfers between devices: 28.7 us -> 29.3 us  [permute(): return lax.ppermute(value, AXES, pairs)]
  transfers between devices with their start and end apart: 23 -> 20, of which waited for: 10 -> 9; matrix products, arithmetic and copies ran while one was open for 0% -> 0% of each run, Pallas kernels for 19% -> 20%
where the time goes in v6:
time: 66.8 us; the launch traced here: 66.6 us
  starting transfers between devices  29.3 us (44%)
  Pallas kernels  17 us (25%)
  waiting for transfers between devices  16.8 us (25%)
  local copies, waits for them, and re-layouts  2.9 us (4%)
    ppermute x20, starting transfers between devices, permute(): return lax.ppermute(value, AXES, pairs)  29.3 us
    ppermute x20, waiting for transfers between devices, permute(): return lax.ppermute(value, AXES, pairs)  16.8 us
    pallas_call x4, Pallas kernels, correlate_part(): pl.pallas_call(kernel if out is None else lambda *refs: kernel(*refs[:len...  11.1 us
    unnamed x14, local copies, waits for them, and re-layouts  2.87 us
    pallas_call x1, Pallas kernels, fold(): pl.pallas_call(fold_kernel, grid=(4,), in_specs=[whole, whole, pl.BlockSp...  2.28 us
    pallas_call x1, Pallas kernels, correlate_plane(): pl.pallas_call(functools.partial(plane_kernel, earlier), in_specs=[VMEM_S...  2.19 us
    pallas_call x1, Pallas kernels, whiten(): pl.pallas_call(whiten_kernel, in_specs=[smem, smem, smem, vmem, vmem, vme...  1.39 us
  transfers between devices with their start and end apart: 20, of which 9 were waited for; matrix products, arithmetic and copies ran while one was open for 0% of the time, Pallas kernels for 20%

profile of v6, /device:TPU:1, one launch (start us, length us, event | category | flops | bytes accessed | tf_op | source)
XLA Modules:
  0.0 66.6 jit_solution(6222413092516397451)
XLA Ops:
  0.0 3.8 %collective-permute-start = (f32[2,8,768]{2,1,0:T(8,128)}, f32[2,8,768]{2,1,0:T(8,128)S(1)}, u32[]{:S(2)}, u32[]{:S(2)}) collective-permute-start(f32[2,8,768]{2,1,0:T(8,128)} %own_ref.1), channel_id=1, source_target_pairs={{0,16},{2,18},{4,20},{6,22},{1,17},{3,19},{5,21},{7,23},{8,24},{10... | collective-permute-start | bytes 147464 | tf_op jit(solution)/shard_map/ppermute | solution.py:52
  3.8 0.0 collective-permute-start.1
  3.9 0.0 copy-start
  3.9 1.4 %copy-done = bf16[768,1024]{1,0:T(8,128)(2,1)S(1)} copy-done((bf16[768,1024]{1,0:T(8,128)(2,1)S(1)}, bf16[768,1024]{1,0:T(8,128)(2,1)}, u32[]{:S(2)}) %copy-start) | copy-done | bytes 1572888
  5.3 0.0 copy-start.1
  5.3 1.4 %copy-done.1 = bf16[768,1024]{1,0:T(8,128)(2,1)S(1)} copy-done((bf16[768,1024]{1,0:T(8,128)(2,1)S(1)}, bf16[768,1024]{1,0:T(8,128)(2,1)}, u32[]{:S(2)}) %copy-start.1) | copy-done | bytes 1572888
  6.7 0.0 copy-start.3
  6.7 0.0 copy-start.4
  6.7 0.0 copy-start.5
  6.7 0.9 %collective-permute-done.1.near_mask_ref = s32[8]{0:T(128)S(1)} collective-permute-done((s32[8]{0:T(128)}, s32[8]{0:T(128)S(1)}, u32[]{:S(2)}, u32[]{:S(2)}) %collective-permute-start.1) | collective-permute-done | bytes 64 | tf_op jit(solution)/shard_map/ppermute | solution.py:52
  7.6 0.0 collective-permute-done.near_ref
  7.6 0.0 copy-done.3
  7.6 0.0 copy-done.4
  7.6 0.0 copy-done.5
  7.6 1.4 %whiten.1 = (bf16[16,2048]{1,0:T(8,128)(2,1)S(1)}, bf16[8,2048]{1,0:T(8,128)(2,1)S(1)}) custom-call(s32[4]{0:T(128)S(1)} %copy-done.4, s32[8]{0:T(128)S(1)} %copy-done.5, s32[8]{0:T(128)S(1)} %collective-permute-done.1.near_mask_ref, f32[2,8,768]{2,1,0:T(8,128)S(1)} %copy-done.3, f32[2,8,768]{2,1,0:T(8,128)S(1)} %collective-permute-done.near_ref, ...), custom_call_target="tpu_custom_call" | custom-call | tf_op jit(solution)/shard_map/whiten/pallas_call | solution.py:129
  9.0 0.0 copy-start.2
  9.0 4.8 %collective-permute-start.4 = (bf16[16,2048]{1,0:T(8,128)(2,1)S(1)}, bf16[16,2048]{1,0:T(8,128)(2,1)S(1)}, u32[]{:S(2)}, u32[]{:S(2)}) collective-permute-start(bf16[16,2048]{1,0:T(8,128)(2,1)S(1)} %get-tuple-element.36), channel_id=1, source_target_pairs={{0,56},{2,58},{4,60},{6,62},{1,57},{3,59},{5,61},{7,63},{8,48},{10... | collective-permute-start | bytes 196616 | tf_op jit(solution)/shard_map/ppermute | solution.py:52
  13.9 0.5 collective-permute-start.3
  14.4 1.1 %collective-permute-start.2 = (bf16[16,2048]{1,0:T(8,128)(2,1)S(1)}, bf16[16,2048]{1,0:T(8,128)(2,1)S(1)}, u32[]{:S(2)}, u32[]{:S(2)}) collective-permute-start(bf16[16,2048]{1,0:T(8,128)(2,1)S(1)} %get-tuple-element.36), channel_id=1, source_target_pairs={{0,8},{2,10},{4,12},{6,14},{1,9},{3,11},{5,13},{7,15},{8,0},{10,2}... | collective-permute-start | bytes 196616 | tf_op jit(solution)/shard_map/ppermute | solution.py:52
  15.5 2.8 %collective-permute-start.5 = (bf16[8,2048]{1,0:T(8,128)(2,1)S(1)}, bf16[8,2048]{1,0:T(8,128)(2,1)S(1)}, u32[]{:S(2)}, u32[]{:S(2)}) collective-permute-start(bf16[8,2048]{1,0:T(8,128)(2,1)S(1)} %get-tuple-element.39.own_ref), channel_id=1, source_target_pairs={{0,1},{2,3},{4,5},{6,7},{1,0},{3,2},{5,4},{7,6},{8,9},{10,11},{12,... | collective-permute-start | bytes 98312 | tf_op jit(solution)/shard_map/ppermute | solution.py:52
  18.3 0.0 collective-permute-done.4
  18.3 0.9 %collective-permute-done.3 = bf16[16,2048]{1,0:T(8,128)(2,1)S(1)} collective-permute-done((bf16[16,2048]{1,0:T(8,128)(2,1)S(1)}, bf16[16,2048]{1,0:T(8,128)(2,1)S(1)}, u32[]{:S(2)}, u32[]{:S(2)}) %collective-permute-start.3) | collective-permute-done | bytes 65568 | tf_op jit(solution)/shard_map/ppermute | solution.py:52
  19.1 0.0 collective-permute-done.2
  19.2 0.6 collective-permute-done.5.other_ref
  19.8 1.2 %collective-permute-start.6 = (bf16[64,2048]{1,0:T(8,128)(2,1)S(1)}, bf16[64,2048]{1,0:T(8,128)(2,1)S(1)}, u32[]{:S(2)}, u32[]{:S(2)}) collective-permute-start(bf16[64,2048]{1,0:T(8,128)(2,1)S(1)} %pad_maximum_fusion.3), channel_id=1, source_target_pairs={{0,64},{2,6},{4,68},{6,2},{1,65},{3,7},{5,69},{7,3},{8,72},{10,14}... | collective-permute-start | bytes 786440 | tf_op jit(solution)/shard_map/ppermute | solution.py:52
  21.0 1.8 %collective-permute-start.9 = (bf16[64,2048]{1,0:T(8,128)(2,1)S(1)}, bf16[64,2048]{1,0:T(8,128)(2,1)S(1)}, u32[]{:S(2)}, u32[]{:S(2)}) collective-permute-start(bf16[64,2048]{1,0:T(8,128)(2,1)S(1)} %pad_maximum_fusion.3), channel_id=1, source_target_pairs={{0,192},{2,7},{4,196},{6,3},{1,193},{3,6},{5,197},{7,2},{8,200},{1... | collective-permute-start | bytes 786440 | tf_op jit(solution)/shard_map/ppermute | solution.py:52
  22.8 0.6 collective-permute-start.8
  23.5 1.5 %collective-permute-done.6 = bf16[64,2048]{1,0:T(8,128)(2,1)S(1)} collective-permute-done((bf16[64,2048]{1,0:T(8,128)(2,1)S(1)}, bf16[64,2048]{1,0:T(8,128)(2,1)S(1)}, u32[]{:S(2)}, u32[]{:S(2)}) %collective-permute-start.6) | collective-permute-done | bytes 262176 | tf_op jit(solution)/shard_map/ppermute | solution.py:52
  25.0 2.8 %collective-permute-start.11 = (bf16[128,2048]{1,0:T(8,128)(2,1)S(1)}, bf16[128,2048]{1,0:T(8,128)(2,1)S(1)}, u32[]{:S(2)}, u32[]{:S(2)}) collective-permute-start(bf16[128,2048]{1,0:T(8,128)(2,1)S(1)} %constant_dynamic-update-slice_fusion.top.refs_0_), channel_id=1, source_target_pairs={{0,5},{2,194},{4,1},{6,198},{1,4},{3,195},{5,0},{7,199},{8,13},{10... | collective-permute-start | bytes 1572872 | tf_op jit(solution)/shard_map/ppermute | solution.py:52
  27.9 0.0 collective-permute-start.7
  27.9 2.3 %collective-permute-done.8 = bf16[64,2048]{1,0:T(8,128)(2,1)S(1)} collective-permute-done((bf16[64,2048]{1,0:T(8,128)(2,1)S(1)}, bf16[64,2048]{1,0:T(8,128)(2,1)S(1)}, u32[]{:S(2)}, u32[]{:S(2)}) %collective-permute-start.8) | collective-permute-done | bytes 262176 | tf_op jit(solution)/shard_map/ppermute | solution.py:52
  30.1 0.4 collective-permute-done.9
  30.6 2.8 %collective-permute-start.12 = (bf16[128,2048]{1,0:T(8,128)(2,1)S(1)}, bf16[128,2048]{1,0:T(8,128)(2,1)S(1)}, u32[]{:S(2)}, u32[]{:S(2)}) collective-permute-start(bf16[128,2048]{1,0:T(8,128)(2,1)S(1)} %constant_dynamic-update-slice_fusion.2.bottom.refs_1_), channel_id=1, source_target_pairs={{0,5},{2,194},{4,1},{6,198},{1,4},{3,195},{5,0},{7,199},{8,13},{10... | collective-permute-start | bytes 1572872 | tf_op jit(solution)/shard_map/ppermute | solution.py:52
  33.4 0.0 collective-permute-start.10
  33.4 0.0 copy-done.2
  33.4 2.3 %fold.1.refs_4_.refs_2_.folded.refs_3_ = bf16[1024,4096]{1,0:T(8,128)(2,1)S(1)} custom-call(bf16[8,2048]{1,0:T(8,128)(2,1)S(1)} %get-tuple-element.39.own_ref, bf16[8,2048]{1,0:T(8,128)(2,1)S(1)} %collective-permute-done.5.other_ref, bf16[256,1024]{1,0:T(8,128)(2,1)S(1)} %copy-done.2), custom_call_target="tpu_custom_call" | custom-call | flops 1048576 | bytes 1024 | tf_op jit(solution)/shard_map/fold/pallas_call | solution.py:162
  35.7 0.1 pad_maximum_fusion.1
  35.7 3.9 %collective-permute-done.11.refs_2_ = bf16[128,2048]{1,0:T(8,128)(2,1)S(1)} collective-permute-done((bf16[128,2048]{1,0:T(8,128)(2,1)S(1)}, bf16[128,2048]{1,0:T(8,128)(2,1)S(1)}, u32[]{:S(2)}, u32[]{:S(2)}) %collective-permute-start.11) | collective-permute-done | bytes 524320 | tf_op jit(solution)/shard_map/ppermute | solution.py:52
  39.6 0.0 collective-permute-done.7.refs_0_
  39.6 0.1 pad_maximum_fusion
  39.7 5.8 %collective-permute-done.12.refs_3_ = bf16[128,2048]{1,0:T(8,128)(2,1)S(1)} collective-permute-done((bf16[128,2048]{1,0:T(8,128)(2,1)S(1)}, bf16[128,2048]{1,0:T(8,128)(2,1)S(1)}, u32[]{:S(2)}, u32[]{:S(2)}) %collective-permute-start.12) | collective-permute-done | bytes 524320 | tf_op jit(solution)/shard_map/ppermute | solution.py:52
  45.5 0.0 collective-permute-done.10.refs_1_
  45.5 0.1 pad_maximum_fusion.2
  45.7 4.5 %collective-permute-start.15 = (bf16[256,2048]{1,0:T(8,128)(2,1)S(1)}, bf16[256,2048]{1,0:T(8,128)(2,1)S(1)}, u32[]{:S(2)}, u32[]{:S(2)}) collective-permute-start(bf16[256,2048]{1,0:T(8,128)(2,1)S(1)} %pad_maximum_fusion.2), channel_id=1, source_target_pairs={{0,2},{2,0},{4,6},{6,4},{1,3},{3,1},{5,7},{7,5},{8,10},{10,8},{12,... | collective-permute-start | bytes 3145736 | tf_op jit(solution)/shard_map/ppermute | solution.py:52
  50.1 0.1 collective-permute-start.14
  50.2 0.4 collective-permute-start.13
  50.7 0.0 collective-permute-start.16
  50.7 0.7 %collective-permute-start.17 = (bf16[128,2048]{1,0:T(8,128)(2,1)S(1)}, bf16[128,2048]{1,0:T(8,128)(2,1)S(1)}, u32[]{:S(2)}, u32[]{:S(2)}) collective-permute-start(bf16[128,2048]{1,0:T(8,128)(2,1)S(1)} %collective-permute-done.10.refs_1_), channel_id=1, source_target_pairs={{0,5},{2,194},{4,1},{6,198},{1,4},{3,195},{5,0},{7,199},{8,13},{10... | collective-permute-start | bytes 1572872 | tf_op jit(solution)/shard_map/ppermute | solution.py:52
  51.3 2.7 %correlate.4.refs_3_ = f32[4,4,8,8,256]{4,3,2,1,0:T(8,128)S(1)} custom-call(bf16[128,2048]{1,0:T(8,128)(2,1)S(1)} %collective-permute-done.7.refs_0_, bf16[128,2048]{1,0:T(8,128)(2,1)S(1)} %collective-permute-done.10.refs_1_, bf16[128,2048]{1,0:T(8,128)(2,1)S(1)} %collective-permute-done.11.refs_2_, bf16[128,2048]{1,0:T(8,128)(2,1)S(1)} %collective-permute-done.12.refs_3_, ...), custom_call_target="tpu_custom_call" | custom-call | flops 1048576 | bytes 1024 | tf_op jit(solution)/shard_map/correlate/pallas_call | solution.py:265
  54.0 0.0 collective-permute-done.15.refs_1_
  54.0 0.0 collective-permute-done.14.refs_0_
  54.0 3.4 %correlate.5 = (f32[4,4,8,2,2,8,256]{6,5,4,3,2,1,0:T(8,128)}, f32[4,4,8,8,256]{4,3,2,1,0:T(8,128)S(1)}) custom-call(bf16[256,2048]{1,0:T(8,128)(2,1)S(1)} %collective-permute-done.14.refs_0_, bf16[256,2048]{1,0:T(8,128)(2,1)S(1)} %collective-permute-done.15.refs_1_, bf16[1024,4096]{1,0:T(8,128)(2,1)S(1)} %fold.1.refs_4_.refs_2_.folded.refs_3_, ...), custom_call_target="tpu_custom_call" | custom-call | flops 1048576 | bytes 1024 | tf_op jit(solution)/shard_map/correlate/pallas_call | solution.py:265
  57.5 0.0 collective-permute-done.13.plane_too.refs_0_
  57.5 2.2 %plane.1 = (f32[4,4,8,2,2,8,256]{6,5,4,3,2,1,0:T(8,128)}, f32[256,1024]{1,0:T(8,128)S(1)}) custom-call(bf16[128,2048]{1,0:T(8,128)(2,1)S(1)} %constant_dynamic-update-slice_fusion.top.refs_0_, bf16[128,2048]{1,0:T(8,128)(2,1)S(1)} %constant_dynamic-update-slice_fusion.2.bottom.refs_1_, ...), custom_call_target="tpu_custom_call", output_to_operand_aliasing={{0}: (5, {})} | custom-call | flops 1048576 | bytes 1024 | tf_op jit(solution)/shard_map/plane/pallas_call | solution.py:307
  59.7 0.0 collective-permute-done.16.refs_2_
  59.7 0.5 collective-permute-done.17.refs_3_
  60.2 1.2 %collective-permute-start.18 = (bf16[128,2048]{1,0:T(8,128)(2,1)S(1)}, bf16[128,2048]{1,0:T(8,128)(2,1)S(1)}, u32[]{:S(2)}, u32[]{:S(2)}) collective-permute-start(bf16[128,2048]{1,0:T(8,128)(2,1)S(1)} %collective-permute-done.16.refs_2_), channel_id=1, source_target_pairs={{0,2},{2,0},{4,6},{6,4},{1,3},{3,1},{5,7},{7,5},{8,10},{10,8},{12,... | collective-permute-start | bytes 1572872 | tf_op jit(solution)/shard_map/ppermute | solution.py:52
  61.4 0.0 collective-permute-start.19
  61.4 2.7 %correlate.6.refs_5_ = f32[4,4,8,8,256]{4,3,2,1,0:T(8,128)S(1)} custom-call(bf16[128,2048]{1,0:T(8,128)(2,1)S(1)} %constant_dynamic-update-slice_fusion.top.refs_0_, bf16[128,2048]{1,0:T(8,128)(2,1)S(1)} %constant_dynamic-update-slice_fusion.2.bottom.refs_1_, bf16[128,2048]{1,0:T(8,128)(2,1)S(1)} %collective-permute-done.16.refs_2_, ...), custom_call_target="tpu_custom_call" | custom-call | flops 1048576 | bytes 1024 | tf_op jit(solution)/shard_map/correlate/pallas_call | solution.py:265
  64.1 0.0 collective-permute-done.18.refs_1_
  64.1 0.0 collective-permute-done.19.refs_2_
  64.1 2.4 %correlate.7 = f32[4,4,8,2,2,8,256]{6,5,4,3,2,1,0:T(8,128)} custom-call(bf16[256,2048]{1,0:T(8,128)(2,1)S(1)} %collective-permute-done.13.plane_too.refs_0_, bf16[128,2048]{1,0:T(8,128)(2,1)S(1)} %collective-permute-done.18.refs_1_, bf16[128,2048]{1,0:T(8,128)(2,1)S(1)} %collective-permute-done.19.refs_2_, ...), custom_call_target="tpu_custom_call", output_to_operand_aliasing={{}: (6, {})} | custom-call | flops 1048576 | bytes 1024 | tf_op jit(solution)/shard_map/correlate/pallas_call | solution.py:265
  (6 shorter events, 0.1 us)
Async XLA Ops:
  0.0 7.6 %collective-permute-start = (f32[2,8,768]{2,1,0:T(8,128)}, f32[2,8,768]{2,1,0:T(8,128)S(1)}, u32[]{:S(2)}, u32[]{:S(2)}) collective-permute-start(f32[2,8,768]{2,1,0:T(8,128)} %own_ref.1), channel_id=1, source_target_pairs={{0,16},{2,18},{4,20},{6,22},{1,17},{3,19},{5,21},{7,23},{8,24},{10... | collective-permute-start | bytes 147464 | tf_op jit(solution)/shard_map/ppermute | solution.py:52
  3.8 3.8 %collective-permute-start.1 = (s32[8]{0:T(128)}, s32[8]{0:T(128)S(1)}, u32[]{:S(2)}, u32[]{:S(2)}) collective-permute-start(s32[8]{0:T(128)} %own_mask_ref.1), channel_id=1, source_target_pairs={{0,16},{2,18},{4,20},{6,22},{1,17},{3,19},{5,21},{7,23},{8,24},{10... | collective-permute-start | bytes 104 | tf_op jit(solution)/shard_map/ppermute | solution.py:52
  3.9 1.4 %copy-start = (bf16[768,1024]{1,0:T(8,128)(2,1)S(1)}, bf16[768,1024]{1,0:T(8,128)(2,1)}, u32[]{:S(2)}) copy-start(bf16[768,1024]{1,0:T(8,128)(2,1)} %constant.7.clone.low_ref) | copy-start | bytes 4718596
  5.3 1.4 %copy-start.1 = (bf16[768,1024]{1,0:T(8,128)(2,1)S(1)}, bf16[768,1024]{1,0:T(8,128)(2,1)}, u32[]{:S(2)}) copy-start(bf16[768,1024]{1,0:T(8,128)(2,1)} %constant.6.clone.high_ref) | copy-start | bytes 4718596
  6.7 0.9 %copy-start.3 = (f32[2,8,768]{2,1,0:T(8,128)S(1)}, f32[2,8,768]{2,1,0:T(8,128)}, u32[]{:S(2)}) copy-start(f32[2,8,768]{2,1,0:T(8,128)} %own_ref.1) | copy-start | bytes 147460
  6.7 0.9 %copy-start.4 = (s32[4]{0:T(128)S(1)}, s32[4]{0:T(128)}, u32[]{:S(2)}) copy-start(s32[4]{0:T(128)} %lengths_ref.1) | copy-start | bytes 52
  6.7 0.9 %copy-start.5 = (s32[8]{0:T(128)S(1)}, s32[8]{0:T(128)}, u32[]{:S(2)}) copy-start(s32[8]{0:T(128)} %own_mask_ref.1) | copy-start | bytes 100
  9.0 24.3 %copy-start.2 = (bf16[256,1024]{1,0:T(8,128)(2,1)S(1)}, bf16[256,1024]{1,0:T(8,128)(2,1)}, u32[]{:S(2)}) copy-start(bf16[256,1024]{1,0:T(8,128)(2,1)} %constant.8.clone.lag_ref) | copy-start | bytes 1572868
  9.0 9.2 %collective-permute-start.4 = (bf16[16,2048]{1,0:T(8,128)(2,1)S(1)}, bf16[16,2048]{1,0:T(8,128)(2,1)S(1)}, u32[]{:S(2)}, u32[]{:S(2)}) collective-permute-start(bf16[16,2048]{1,0:T(8,128)(2,1)S(1)} %get-tuple-element.36), channel_id=1, source_target_pairs={{0,56},{2,58},{4,60},{6,62},{1,57},{3,59},{5,61},{7,63},{8,48},{10... | collective-permute-start | bytes 196616 | tf_op jit(solution)/shard_map/ppermute | solution.py:52
  13.9 5.3 %collective-permute-start.3 = (bf16[16,2048]{1,0:T(8,128)(2,1)S(1)}, bf16[16,2048]{1,0:T(8,128)(2,1)S(1)}, u32[]{:S(2)}, u32[]{:S(2)}) collective-permute-start(bf16[16,2048]{1,0:T(8,128)(2,1)S(1)} %get-tuple-element.36), channel_id=1, source_target_pairs={{0,48},{2,50},{4,52},{6,54},{1,49},{3,51},{5,53},{7,55},{8,56},{10... | collective-permute-start | bytes 196616 | tf_op jit(solution)/shard_map/ppermute | solution.py:52
  14.4 4.7 %collective-permute-start.2 = (bf16[16,2048]{1,0:T(8,128)(2,1)S(1)}, bf16[16,2048]{1,0:T(8,128)(2,1)S(1)}, u32[]{:S(2)}, u32[]{:S(2)}) collective-permute-start(bf16[16,2048]{1,0:T(8,128)(2,1)S(1)} %get-tuple-element.36), channel_id=1, source_target_pairs={{0,8},{2,10},{4,12},{6,14},{1,9},{3,11},{5,13},{7,15},{8,0},{10,2}... | collective-permute-start | bytes 196616 | tf_op jit(solution)/shard_map/ppermute | solution.py:52
  15.5 4.3 %collective-permute-start.5 = (bf16[8,2048]{1,0:T(8,128)(2,1)S(1)}, bf16[8,2048]{1,0:T(8,128)(2,1)S(1)}, u32[]{:S(2)}, u32[]{:S(2)}) collective-permute-start(bf16[8,2048]{1,0:T(8,128)(2,1)S(1)} %get-tuple-element.39.own_ref), channel_id=1, source_target_pairs={{0,1},{2,3},{4,5},{6,7},{1,0},{3,2},{5,4},{7,6},{8,9},{10,11},{12,... | collective-permute-start | bytes 98312 | tf_op jit(solution)/shard_map/ppermute | solution.py:52
  19.8 5.2 %collective-permute-start.6 = (bf16[64,2048]{1,0:T(8,128)(2,1)S(1)}, bf16[64,2048]{1,0:T(8,128)(2,1)S(1)}, u32[]{:S(2)}, u32[]{:S(2)}) collective-permute-start(bf16[64,2048]{1,0:T(8,128)(2,1)S(1)} %pad_maximum_fusion.3), channel_id=1, source_target_pairs={{0,64},{2,6},{4,68},{6,2},{1,65},{3,7},{5,69},{7,3},{8,72},{10,14}... | collective-permute-start | bytes 786440 | tf_op jit(solution)/shard_map/ppermute | solution.py:52
  21.0 9.5 %collective-permute-start.9 = (bf16[64,2048]{1,0:T(8,128)(2,1)S(1)}, bf16[64,2048]{1,0:T(8,128)(2,1)S(1)}, u32[]{:S(2)}, u32[]{:S(2)}) collective-permute-start(bf16[64,2048]{1,0:T(8,128)(2,1)S(1)} %pad_maximum_fusion.3), channel_id=1, source_target_pairs={{0,192},{2,7},{4,196},{6,3},{1,193},{3,6},{5,197},{7,2},{8,200},{1... | collective-permute-start | bytes 786440 | tf_op jit(solution)/shard_map/ppermute | solution.py:52
  22.8 7.3 %collective-permute-start.8 = (bf16[64,2048]{1,0:T(8,128)(2,1)S(1)}, bf16[64,2048]{1,0:T(8,128)(2,1)S(1)}, u32[]{:S(2)}, u32[]{:S(2)}) collective-permute-start(bf16[64,2048]{1,0:T(8,128)(2,1)S(1)} %pad_maximum_fusion.3), channel_id=1, source_target_pairs={{0,128},{2,3},{4,132},{6,7},{1,129},{3,2},{5,133},{7,6},{8,136},{1... | collective-permute-start | bytes 786440 | tf_op jit(solution)/shard_map/ppermute | solution.py:52
  25.0 14.6 %collective-permute-start.11 = (bf16[128,2048]{1,0:T(8,128)(2,1)S(1)}, bf16[128,2048]{1,0:T(8,128)(2,1)S(1)}, u32[]{:S(2)}, u32[]{:S(2)}) collective-permute-start(bf16[128,2048]{1,0:T(8,128)(2,1)S(1)} %constant_dynamic-update-slice_fusion.top.refs_0_), channel_id=1, source_target_pairs={{0,5},{2,194},{4,1},{6,198},{1,4},{3,195},{5,0},{7,199},{8,13},{10... | collective-permute-start | bytes 1572872 | tf_op jit(solution)/shard_map/ppermute | solution.py:52
  27.9 11.8 %collective-permute-start.7 = (bf16[128,2048]{1,0:T(8,128)(2,1)S(1)}, bf16[128,2048]{1,0:T(8,128)(2,1)S(1)}, u32[]{:S(2)}, u32[]{:S(2)}) collective-permute-start(bf16[128,2048]{1,0:T(8,128)(2,1)S(1)} %constant_dynamic-update-slice_fusion.top.refs_0_), channel_id=1, source_target_pairs={{0,4},{2,66},{4,0},{6,70},{1,5},{3,67},{5,1},{7,71},{8,12},{10,74}... | collective-permute-start | bytes 1572872 | tf_op jit(solution)/shard_map/ppermute | solution.py:52
  30.6 15.0 %collective-permute-start.12 = (bf16[128,2048]{1,0:T(8,128)(2,1)S(1)}, bf16[128,2048]{1,0:T(8,128)(2,1)S(1)}, u32[]{:S(2)}, u32[]{:S(2)}) collective-permute-start(bf16[128,2048]{1,0:T(8,128)(2,1)S(1)} %constant_dynamic-update-slice_fusion.2.bottom.refs_1_), channel_id=1, source_target_pairs={{0,5},{2,194},{4,1},{6,198},{1,4},{3,195},{5,0},{7,199},{8,13},{10... | collective-permute-start | bytes 1572872 | tf_op jit(solution)/shard_map/ppermute | solution.py:52
  33.4 12.2 %collective-permute-start.10 = (bf16[128,2048]{1,0:T(8,128)(2,1)S(1)}, bf16[128,2048]{1,0:T(8,128)(2,1)S(1)}, u32[]{:S(2)}, u32[]{:S(2)}) collective-permute-start(bf16[128,2048]{1,0:T(8,128)(2,1)S(1)} %constant_dynamic-update-slice_fusion.2.bottom.refs_1_), channel_id=1, source_target_pairs={{0,4},{2,66},{4,0},{6,70},{1,5},{3,67},{5,1},{7,71},{8,12},{10,74}... | collective-permute-start | bytes 1572872 | tf_op jit(solution)/shard_map/ppermute | solution.py:52
  45.7 8.4 %collective-permute-start.15 = (bf16[256,2048]{1,0:T(8,128)(2,1)S(1)}, bf16[256,2048]{1,0:T(8,128)(2,1)S(1)}, u32[]{:S(2)}, u32[]{:S(2)}) collective-permute-start(bf16[256,2048]{1,0:T(8,128)(2,1)S(1)} %pad_maximum_fusion.2), channel_id=1, source_target_pairs={{0,2},{2,0},{4,6},{6,4},{1,3},{3,1},{5,7},{7,5},{8,10},{10,8},{12,... | collective-permute-start | bytes 3145736 | tf_op jit(solution)/shard_map/ppermute | solution.py:52
  50.1 3.9 %collective-permute-start.14 = (bf16[256,2048]{1,0:T(8,128)(2,1)S(1)}, bf16[256,2048]{1,0:T(8,128)(2,1)S(1)}, u32[]{:S(2)}, u32[]{:S(2)}) collective-permute-start(bf16[256,2048]{1,0:T(8,128)(2,1)S(1)} %pad_maximum_fusion), channel_id=1, source_target_pairs={{0,2},{2,0},{4,6},{6,4},{1,3},{3,1},{5,7},{7,5},{8,10},{10,8},{12,... | collective-permute-start | bytes 3145736 | tf_op jit(solution)/shard_map/ppermute | solution.py:52
  50.2 7.2 %collective-permute-start.13 = (bf16[256,2048]{1,0:T(8,128)(2,1)S(1)}, bf16[256,2048]{1,0:T(8,128)(2,1)S(1)}, u32[]{:S(2)}, u32[]{:S(2)}) collective-permute-start(bf16[256,2048]{1,0:T(8,128)(2,1)S(1)} %pad_maximum_fusion.1), channel_id=1, source_target_pairs={{0,2},{2,0},{4,6},{6,4},{1,3},{3,1},{5,7},{7,5},{8,10},{10,8},{12,... | collective-permute-start | bytes 3145736 | tf_op jit(solution)/shard_map/ppermute | solution.py:52
  50.7 9.0 %collective-permute-start.16 = (bf16[128,2048]{1,0:T(8,128)(2,1)S(1)}, bf16[128,2048]{1,0:T(8,128)(2,1)S(1)}, u32[]{:S(2)}, u32[]{:S(2)}) collective-permute-start(bf16[128,2048]{1,0:T(8,128)(2,1)S(1)} %collective-permute-done.11.refs_2_), channel_id=1, source_target_pairs={{0,4},{2,66},{4,0},{6,70},{1,5},{3,67},{5,1},{7,71},{8,12},{10,74}... | collective-permute-start | bytes 1572872 | tf_op jit(solution)/shard_map/ppermute | solution.py:52
  50.7 9.5 %collective-permute-start.17 = (bf16[128,2048]{1,0:T(8,128)(2,1)S(1)}, bf16[128,2048]{1,0:T(8,128)(2,1)S(1)}, u32[]{:S(2)}, u32[]{:S(2)}) collective-permute-start(bf16[128,2048]{1,0:T(8,128)(2,1)S(1)} %collective-permute-done.10.refs_1_), channel_id=1, source_target_pairs={{0,5},{2,194},{4,1},{6,198},{1,4},{3,195},{5,0},{7,199},{8,13},{10... | collective-permute-start | bytes 1572872 | tf_op jit(solution)/shard_map/ppermute | solution.py:52
  60.2 3.9 %collective-permute-start.18 = (bf16[128,2048]{1,0:T(8,128)(2,1)S(1)}, bf16[128,2048]{1,0:T(8,128)(2,1)S(1)}, u32[]{:S(2)}, u32[]{:S(2)}) collective-permute-start(bf16[128,2048]{1,0:T(8,128)(2,1)S(1)} %collective-permute-done.16.refs_2_), channel_id=1, source_target_pairs={{0,2},{2,0},{4,6},{6,4},{1,3},{3,1},{5,7},{7,5},{8,10},{10,8},{12,... | collective-permute-start | bytes 1572872 | tf_op jit(solution)/shard_map/ppermute | solution.py:52
  61.4 2.7 %collective-permute-start.19 = (bf16[128,2048]{1,0:T(8,128)(2,1)S(1)}, bf16[128,2048]{1,0:T(8,128)(2,1)S(1)}, u32[]{:S(2)}, u32[]{:S(2)}) collective-permute-start(bf16[128,2048]{1,0:T(8,128)(2,1)S(1)} %collective-permute-done.17.refs_3_), channel_id=1, source_target_pairs={{0,2},{2,0},{4,6},{6,4},{1,3},{3,1},{5,7},{7,5},{8,10},{10,8},{12,... | collective-permute-start | bytes 1572872 | tf_op jit(solution)/shard_map/ppermute | solution.py:52

commit v7 on v6

--- a/solution.py
+++ b/solution.py
@@ -226,14 +226,13 @@
             at = slice(2 * LAG * i, 2 * LAG * (i + 1))
             values = early[:, at] if first is None else product(chunks, first, folded[at, :half])
             values += product(chunks, second, folded[at, half:])
+            own = copies_of(result, kind, offsets, i, 1) if last else []
             for n in range(len(offsets)):
                 for g in range(NZ):
                     result[i, n, z ^ Z_ORDER[g]] = values[64 * n + 8 * g : 64 * n + 8 * g + 8]
-            if last:
-                own = copies_of(result, kind, offsets, i, 1)
-                for copy in own:
-                    copy.start()
-                copies += own
+                if last:
+                    own[n].start()
+            copies += own
         for copy in copies:
             copy.wait()
 

time: 66.8 us -> 66.8 us (level)
  no operation moved by 1% of the time
where the time goes in v7:
time: 66.8 us; the launch traced here: 66.6 us
  starting transfers between devices  29.3 us (44%)
  Pallas kernels  17 us (25%)
  waiting for transfers between devices  16.8 us (25%)
  local copies, waits for them, and re-layouts  2.9 us (4%)
    ppermute x20, starting transfers between devices, permute(): return lax.ppermute(value, AXES, pairs)  29.3 us
    ppermute x20, waiting for transfers between devices, permute(): return lax.ppermute(value, AXES, pairs)  16.8 us
    pallas_call x4, Pallas kernels, correlate_part(): pl.pallas_call(kernel if out is None else lambda *refs: kernel(*refs[:len...  11.1 us
    unnamed x14, local copies, waits for them, and re-layouts  2.87 us
    pallas_call x1, Pallas kernels, fold(): pl.pallas_call(fold_kernel, grid=(4,), in_specs=[whole, whole, pl.BlockSp...  2.28 us
    pallas_call x1, Pallas kernels, correlate_plane(): pl.pallas_call(functools.partial(plane_kernel, earlier), in_specs=[VMEM_S...  2.19 us
    pallas_call x1, Pallas kernels, whiten(): pl.pallas_call(whiten_kernel, in_specs=[smem, smem, smem, vmem, vmem, vme...  1.39 us
  transfers between devices with their start and end apart: 20, of which 9 were waited for; matrix products, arithmetic and copies ran while one was open for 0% of the time, Pallas kernels for 20%

profile of v7, /device:TPU:1, one launch (start us, length us, event | category | flops | bytes accessed | tf_op | source)
XLA Modules:
  0.0 66.6 jit_solution(13474074985895911500)
XLA Ops:
  0.0 3.8 %collective-permute-start = (f32[2,8,768]{2,1,0:T(8,128)}, f32[2,8,768]{2,1,0:T(8,128)S(1)}, u32[]{:S(2)}, u32[]{:S(2)}) collective-permute-start(f32[2,8,768]{2,1,0:T(8,128)} %own_ref.1), channel_id=1, source_target_pairs={{0,16},{2,18},{4,20},{6,22},{1,17},{3,19},{5,21},{7,23},{8,24},{10... | collective-permute-start | bytes 147464 | tf_op jit(solution)/shard_map/ppermute | solution.py:52
  3.8 0.0 collective-permute-start.1
  3.9 0.0 copy-start
  3.9 1.4 %copy-done = bf16[768,1024]{1,0:T(8,128)(2,1)S(1)} copy-done((bf16[768,1024]{1,0:T(8,128)(2,1)S(1)}, bf16[768,1024]{1,0:T(8,128)(2,1)}, u32[]{:S(2)}) %copy-start) | copy-done | bytes 1572888
  5.3 0.0 copy-start.1
  5.3 1.4 %copy-done.1 = bf16[768,1024]{1,0:T(8,128)(2,1)S(1)} copy-done((bf16[768,1024]{1,0:T(8,128)(2,1)S(1)}, bf16[768,1024]{1,0:T(8,128)(2,1)}, u32[]{:S(2)}) %copy-start.1) | copy-done | bytes 1572888
  6.7 0.0 copy-start.3
  6.7 0.0 copy-start.4
  6.7 0.0 copy-start.5
  6.7 0.9 %collective-permute-done.1.near_mask_ref = s32[8]{0:T(128)S(1)} collective-permute-done((s32[8]{0:T(128)}, s32[8]{0:T(128)S(1)}, u32[]{:S(2)}, u32[]{:S(2)}) %collective-permute-start.1) | collective-permute-done | bytes 64 | tf_op jit(solution)/shard_map/ppermute | solution.py:52
  7.6 0.0 collective-permute-done.near_ref
  7.6 0.0 copy-done.3
  7.6 0.0 copy-done.4
  7.6 0.0 copy-done.5
  7.6 1.4 %whiten.1 = (bf16[16,2048]{1,0:T(8,128)(2,1)S(1)}, bf16[8,2048]{1,0:T(8,128)(2,1)S(1)}) custom-call(s32[4]{0:T(128)S(1)} %copy-done.4, s32[8]{0:T(128)S(1)} %copy-done.5, s32[8]{0:T(128)S(1)} %collective-permute-done.1.near_mask_ref, f32[2,8,768]{2,1,0:T(8,128)S(1)} %copy-done.3, f32[2,8,768]{2,1,0:T(8,128)S(1)} %collective-permute-done.near_ref, ...), custom_call_target="tpu_custom_call" | custom-call | tf_op jit(solution)/shard_map/whiten/pallas_call | solution.py:129
  9.0 0.0 copy-start.2
  9.0 4.8 %collective-permute-start.4 = (bf16[16,2048]{1,0:T(8,128)(2,1)S(1)}, bf16[16,2048]{1,0:T(8,128)(2,1)S(1)}, u32[]{:S(2)}, u32[]{:S(2)}) collective-permute-start(bf16[16,2048]{1,0:T(8,128)(2,1)S(1)} %get-tuple-element.36), channel_id=1, source_target_pairs={{0,56},{2,58},{4,60},{6,62},{1,57},{3,59},{5,61},{7,63},{8,48},{10... | collective-permute-start | bytes 196616 | tf_op jit(solution)/shard_map/ppermute | solution.py:52
  13.9 0.5 collective-permute-start.3
  14.4 1.1 %collective-permute-start.2 = (bf16[16,2048]{1,0:T(8,128)(2,1)S(1)}, bf16[16,2048]{1,0:T(8,128)(2,1)S(1)}, u32[]{:S(2)}, u32[]{:S(2)}) collective-permute-start(bf16[16,2048]{1,0:T(8,128)(2,1)S(1)} %get-tuple-element.36), channel_id=1, source_target_pairs={{0,8},{2,10},{4,12},{6,14},{1,9},{3,11},{5,13},{7,15},{8,0},{10,2}... | collective-permute-start | bytes 196616 | tf_op jit(solution)/shard_map/ppermute | solution.py:52
  15.5 2.8 %collective-permute-start.5 = (bf16[8,2048]{1,0:T(8,128)(2,1)S(1)}, bf16[8,2048]{1,0:T(8,128)(2,1)S(1)}, u32[]{:S(2)}, u32[]{:S(2)}) collective-permute-start(bf16[8,2048]{1,0:T(8,128)(2,1)S(1)} %get-tuple-element.39.own_ref), channel_id=1, source_target_pairs={{0,1},{2,3},{4,5},{6,7},{1,0},{3,2},{5,4},{7,6},{8,9},{10,11},{12,... | collective-permute-start | bytes 98312 | tf_op jit(solution)/shard_map/ppermute | solution.py:52
  18.3 0.0 collective-permute-done.4
  18.3 0.9 %collective-permute-done.3 = bf16[16,2048]{1,0:T(8,128)(2,1)S(1)} collective-permute-done((bf16[16,2048]{1,0:T(8,128)(2,1)S(1)}, bf16[16,2048]{1,0:T(8,128)(2,1)S(1)}, u32[]{:S(2)}, u32[]{:S(2)}) %collective-permute-start.3) | collective-permute-done | bytes 65568 | tf_op jit(solution)/shard_map/ppermute | solution.py:52
  19.1 0.0 collective-permute-done.2
  19.2 0.6 collective-permute-done.5.other_ref
  19.8 1.2 %collective-permute-start.6 = (bf16[64,2048]{1,0:T(8,128)(2,1)S(1)}, bf16[64,2048]{1,0:T(8,128)(2,1)S(1)}, u32[]{:S(2)}, u32[]{:S(2)}) collective-permute-start(bf16[64,2048]{1,0:T(8,128)(2,1)S(1)} %pad_maximum_fusion.3), channel_id=1, source_target_pairs={{0,64},{2,6},{4,68},{6,2},{1,65},{3,7},{5,69},{7,3},{8,72},{10,14}... | collective-permute-start | bytes 786440 | tf_op jit(solution)/shard_map/ppermute | solution.py:52
  21.0 1.8 %collective-permute-start.9 = (bf16[64,2048]{1,0:T(8,128)(2,1)S(1)}, bf16[64,2048]{1,0:T(8,128)(2,1)S(1)}, u32[]{:S(2)}, u32[]{:S(2)}) collective-permute-start(bf16[64,2048]{1,0:T(8,128)(2,1)S(1)} %pad_maximum_fusion.3), channel_id=1, source_target_pairs={{0,192},{2,7},{4,196},{6,3},{1,193},{3,6},{5,197},{7,2},{8,200},{1... | collective-permute-start | bytes 786440 | tf_op jit(solution)/shard_map/ppermute | solution.py:52
  22.8 0.6 collective-permute-start.8
  23.5 1.5 %collective-permute-done.6 = bf16[64,2048]{1,0:T(8,128)(2,1)S(1)} collective-permute-done((bf16[64,2048]{1,0:T(8,128)(2,1)S(1)}, bf16[64,2048]{1,0:T(8,128)(2,1)S(1)}, u32[]{:S(2)}, u32[]{:S(2)}) %collective-permute-start.6) | collective-permute-done | bytes 262176 | tf_op jit(solution)/shard_map/ppermute | solution.py:52
  25.0 2.8 %collective-permute-start.11 = (bf16[128,2048]{1,0:T(8,128)(2,1)S(1)}, bf16[128,2048]{1,0:T(8,128)(2,1)S(1)}, u32[]{:S(2)}, u32[]{:S(2)}) collective-permute-start(bf16[128,2048]{1,0:T(8,128)(2,1)S(1)} %constant_dynamic-update-slice_fusion.top.refs_0_), channel_id=1, source_target_pairs={{0,5},{2,194},{4,1},{6,198},{1,4},{3,195},{5,0},{7,199},{8,13},{10... | collective-permute-start | bytes 1572872 | tf_op jit(solution)/shard_map/ppermute | solution.py:52
  27.9 0.0 collective-permute-start.7
  27.9 2.3 %collective-permute-done.8 = bf16[64,2048]{1,0:T(8,128)(2,1)S(1)} collective-permute-done((bf16[64,2048]{1,0:T(8,128)(2,1)S(1)}, bf16[64,2048]{1,0:T(8,128)(2,1)S(1)}, u32[]{:S(2)}, u32[]{:S(2)}) %collective-permute-start.8) | collective-permute-done | bytes 262176 | tf_op jit(solution)/shard_map/ppermute | solution.py:52
  30.1 0.4 collective-permute-done.9
  30.6 2.8 %collective-permute-start.12 = (bf16[128,2048]{1,0:T(8,128)(2,1)S(1)}, bf16[128,2048]{1,0:T(8,128)(2,1)S(1)}, u32[]{:S(2)}, u32[]{:S(2)}) collective-permute-start(bf16[128,2048]{1,0:T(8,128)(2,1)S(1)} %constant_dynamic-update-slice_fusion.2.bottom.refs_1_), channel_id=1, source_target_pairs={{0,5},{2,194},{4,1},{6,198},{1,4},{3,195},{5,0},{7,199},{8,13},{10... | collective-permute-start | bytes 1572872 | tf_op jit(solution)/shard_map/ppermute | solution.py:52
  33.4 0.0 collective-permute-start.10
  33.4 0.0 copy-done.2
  33.4 2.3 %fold.1.refs_4_.refs_2_.folded.refs_3_ = bf16[1024,4096]{1,0:T(8,128)(2,1)S(1)} custom-call(bf16[8,2048]{1,0:T(8,128)(2,1)S(1)} %get-tuple-element.39.own_ref, bf16[8,2048]{1,0:T(8,128)(2,1)S(1)} %collective-permute-done.5.other_ref, bf16[256,1024]{1,0:T(8,128)(2,1)S(1)} %copy-done.2), custom_call_target="tpu_custom_call" | custom-call | flops 1048576 | bytes 1024 | tf_op jit(solution)/shard_map/fold/pallas_call | solution.py:162
  35.7 0.1 pad_maximum_fusion.1
  35.7 3.9 %collective-permute-done.11.refs_2_ = bf16[128,2048]{1,0:T(8,128)(2,1)S(1)} collective-permute-done((bf16[128,2048]{1,0:T(8,128)(2,1)S(1)}, bf16[128,2048]{1,0:T(8,128)(2,1)S(1)}, u32[]{:S(2)}, u32[]{:S(2)}) %collective-permute-start.11) | collective-permute-done | bytes 524320 | tf_op jit(solution)/shard_map/ppermute | solution.py:52
  39.6 0.0 collective-permute-done.7.refs_0_
  39.6 0.1 pad_maximum_fusion
  39.7 5.8 %collective-permute-done.12.refs_3_ = bf16[128,2048]{1,0:T(8,128)(2,1)S(1)} collective-permute-done((bf16[128,2048]{1,0:T(8,128)(2,1)S(1)}, bf16[128,2048]{1,0:T(8,128)(2,1)S(1)}, u32[]{:S(2)}, u32[]{:S(2)}) %collective-permute-start.12) | collective-permute-done | bytes 524320 | tf_op jit(solution)/shard_map/ppermute | solution.py:52
  45.5 0.0 collective-permute-done.10.refs_1_
  45.5 0.1 pad_maximum_fusion.2
  45.7 4.5 %collective-permute-start.15 = (bf16[256,2048]{1,0:T(8,128)(2,1)S(1)}, bf16[256,2048]{1,0:T(8,128)(2,1)S(1)}, u32[]{:S(2)}, u32[]{:S(2)}) collective-permute-start(bf16[256,2048]{1,0:T(8,128)(2,1)S(1)} %pad_maximum_fusion.2), channel_id=1, source_target_pairs={{0,2},{2,0},{4,6},{6,4},{1,3},{3,1},{5,7},{7,5},{8,10},{10,8},{12,... | collective-permute-start | bytes 3145736 | tf_op jit(solution)/shard_map/ppermute | solution.py:52
  50.1 0.1 collective-permute-start.14
  50.2 0.4 collective-permute-start.13
  50.7 0.0 collective-permute-start.16
  50.7 0.7 %collective-permute-start.17 = (bf16[128,2048]{1,0:T(8,128)(2,1)S(1)}, bf16[128,2048]{1,0:T(8,128)(2,1)S(1)}, u32[]{:S(2)}, u32[]{:S(2)}) collective-permute-start(bf16[128,2048]{1,0:T(8,128)(2,1)S(1)} %collective-permute-done.10.refs_1_), channel_id=1, source_target_pairs={{0,5},{2,194},{4,1},{6,198},{1,4},{3,195},{5,0},{7,199},{8,13},{10... | collective-permute-start | bytes 1572872 | tf_op jit(solution)/shard_map/ppermute | solution.py:52
  51.3 2.7 %correlate.4.refs_3_ = f32[4,4,8,8,256]{4,3,2,1,0:T(8,128)S(1)} custom-call(bf16[128,2048]{1,0:T(8,128)(2,1)S(1)} %collective-permute-done.7.refs_0_, bf16[128,2048]{1,0:T(8,128)(2,1)S(1)} %collective-permute-done.10.refs_1_, bf16[128,2048]{1,0:T(8,128)(2,1)S(1)} %collective-permute-done.11.refs_2_, bf16[128,2048]{1,0:T(8,128)(2,1)S(1)} %collective-permute-done.12.refs_3_, ...), custom_call_target="tpu_custom_call" | custom-call | flops 1048576 | bytes 1024 | tf_op jit(solution)/shard_map/correlate/pallas_call | solution.py:264
  54.0 0.0 collective-permute-done.15.refs_1_
  54.0 0.0 collective-permute-done.14.refs_0_
  54.0 3.4 %correlate.5 = (f32[4,4,8,2,2,8,256]{6,5,4,3,2,1,0:T(8,128)}, f32[4,4,8,8,256]{4,3,2,1,0:T(8,128)S(1)}) custom-call(bf16[256,2048]{1,0:T(8,128)(2,1)S(1)} %collective-permute-done.14.refs_0_, bf16[256,2048]{1,0:T(8,128)(2,1)S(1)} %collective-permute-done.15.refs_1_, bf16[1024,4096]{1,0:T(8,128)(2,1)S(1)} %fold.1.refs_4_.refs_2_.folded.refs_3_, ...), custom_call_target="tpu_custom_call" | custom-call | flops 1048576 | bytes 1024 | tf_op jit(solution)/shard_map/correlate/pallas_call | solution.py:264
  57.5 0.0 collective-permute-done.13.plane_too.refs_0_
  57.5 2.2 %plane.1 = (f32[4,4,8,2,2,8,256]{6,5,4,3,2,1,0:T(8,128)}, f32[256,1024]{1,0:T(8,128)S(1)}) custom-call(bf16[128,2048]{1,0:T(8,128)(2,1)S(1)} %constant_dynamic-update-slice_fusion.top.refs_0_, bf16[128,2048]{1,0:T(8,128)(2,1)S(1)} %constant_dynamic-update-slice_fusion.2.bottom.refs_1_, ...), custom_call_target="tpu_custom_call", output_to_operand_aliasing={{0}: (5, {})} | custom-call | flops 1048576 | bytes 1024 | tf_op jit(solution)/shard_map/plane/pallas_call | solution.py:306
  59.7 0.0 collective-permute-done.16.refs_2_
  59.7 0.5 collective-permute-done.17.refs_3_
  60.2 1.2 %collective-permute-start.18 = (bf16[128,2048]{1,0:T(8,128)(2,1)S(1)}, bf16[128,2048]{1,0:T(8,128)(2,1)S(1)}, u32[]{:S(2)}, u32[]{:S(2)}) collective-permute-start(bf16[128,2048]{1,0:T(8,128)(2,1)S(1)} %collective-permute-done.16.refs_2_), channel_id=1, source_target_pairs={{0,2},{2,0},{4,6},{6,4},{1,3},{3,1},{5,7},{7,5},{8,10},{10,8},{12,... | collective-permute-start | bytes 1572872 | tf_op jit(solution)/shard_map/ppermute | solution.py:52
  61.4 0.0 collective-permute-start.19
  61.4 2.7 %correlate.6.refs_5_ = f32[4,4,8,8,256]{4,3,2,1,0:T(8,128)S(1)} custom-call(bf16[128,2048]{1,0:T(8,128)(2,1)S(1)} %constant_dynamic-update-slice_fusion.top.refs_0_, bf16[128,2048]{1,0:T(8,128)(2,1)S(1)} %constant_dynamic-update-slice_fusion.2.bottom.refs_1_, bf16[128,2048]{1,0:T(8,128)(2,1)S(1)} %collective-permute-done.16.refs_2_, ...), custom_call_target="tpu_custom_call" | custom-call | flops 1048576 | bytes 1024 | tf_op jit(solution)/shard_map/correlate/pallas_call | solution.py:264
  64.1 0.0 collective-permute-done.18.refs_1_
  64.1 0.0 collective-permute-done.19.refs_2_
  64.1 2.3 %correlate.7 = f32[4,4,8,2,2,8,256]{6,5,4,3,2,1,0:T(8,128)} custom-call(bf16[256,2048]{1,0:T(8,128)(2,1)S(1)} %collective-permute-done.13.plane_too.refs_0_, bf16[128,2048]{1,0:T(8,128)(2,1)S(1)} %collective-permute-done.18.refs_1_, bf16[128,2048]{1,0:T(8,128)(2,1)S(1)} %collective-permute-done.19.refs_2_, ...), custom_call_target="tpu_custom_call", output_to_operand_aliasing={{}: (6, {})} | custom-call | flops 1048576 | bytes 1024 | tf_op jit(solution)/shard_map/correlate/pallas_call | solution.py:264
  (6 shorter events, 0.1 us)
Async XLA Ops:
  0.0 7.6 %collective-permute-start = (f32[2,8,768]{2,1,0:T(8,128)}, f32[2,8,768]{2,1,0:T(8,128)S(1)}, u32[]{:S(2)}, u32[]{:S(2)}) collective-permute-start(f32[2,8,768]{2,1,0:T(8,128)} %own_ref.1), channel_id=1, source_target_pairs={{0,16},{2,18},{4,20},{6,22},{1,17},{3,19},{5,21},{7,23},{8,24},{10... | collective-permute-start | bytes 147464 | tf_op jit(solution)/shard_map/ppermute | solution.py:52
  3.8 3.8 %collective-permute-start.1 = (s32[8]{0:T(128)}, s32[8]{0:T(128)S(1)}, u32[]{:S(2)}, u32[]{:S(2)}) collective-permute-start(s32[8]{0:T(128)} %own_mask_ref.1), channel_id=1, source_target_pairs={{0,16},{2,18},{4,20},{6,22},{1,17},{3,19},{5,21},{7,23},{8,24},{10... | collective-permute-start | bytes 104 | tf_op jit(solution)/shard_map/ppermute | solution.py:52
  3.9 1.4 %copy-start = (bf16[768,1024]{1,0:T(8,128)(2,1)S(1)}, bf16[768,1024]{1,0:T(8,128)(2,1)}, u32[]{:S(2)}) copy-start(bf16[768,1024]{1,0:T(8,128)(2,1)} %constant.7.clone.low_ref) | copy-start | bytes 4718596
  5.3 1.4 %copy-start.1 = (bf16[768,1024]{1,0:T(8,128)(2,1)S(1)}, bf16[768,1024]{1,0:T(8,128)(2,1)}, u32[]{:S(2)}) copy-start(bf16[768,1024]{1,0:T(8,128)(2,1)} %constant.6.clone.high_ref) | copy-start | bytes 4718596
  6.7 0.9 %copy-start.3 = (f32[2,8,768]{2,1,0:T(8,128)S(1)}, f32[2,8,768]{2,1,0:T(8,128)}, u32[]{:S(2)}) copy-start(f32[2,8,768]{2,1,0:T(8,128)} %own_ref.1) | copy-start | bytes 147460
  6.7 0.9 %copy-start.4 = (s32[4]{0:T(128)S(1)}, s32[4]{0:T(128)}, u32[]{:S(2)}) copy-start(s32[4]{0:T(128)} %lengths_ref.1) | copy-start | bytes 52
  6.7 0.9 %copy-start.5 = (s32[8]{0:T(128)S(1)}, s32[8]{0:T(128)}, u32[]{:S(2)}) copy-start(s32[8]{0:T(128)} %own_mask_ref.1) | copy-start | bytes 100
  9.0 24.3 %copy-start.2 = (bf16[256,1024]{1,0:T(8,128)(2,1)S(1)}, bf16[256,1024]{1,0:T(8,128)(2,1)}, u32[]{:S(2)}) copy-start(bf16[256,1024]{1,0:T(8,128)(2,1)} %constant.8.clone.lag_ref) | copy-start | bytes 1572868
  9.0 9.2 %collective-permute-start.4 = (bf16[16,2048]{1,0:T(8,128)(2,1)S(1)}, bf16[16,2048]{1,0:T(8,128)(2,1)S(1)}, u32[]{:S(2)}, u32[]{:S(2)}) collective-permute-start(bf16[16,2048]{1,0:T(8,128)(2,1)S(1)} %get-tuple-element.36), channel_id=1, source_target_pairs={{0,56},{2,58},{4,60},{6,62},{1,57},{3,59},{5,61},{7,63},{8,48},{10... | collective-permute-start | bytes 196616 | tf_op jit(solution)/shard_map/ppermute | solution.py:52
  13.9 5.3 %collective-permute-start.3 = (bf16[16,2048]{1,0:T(8,128)(2,1)S(1)}, bf16[16,2048]{1,0:T(8,128)(2,1)S(1)}, u32[]{:S(2)}, u32[]{:S(2)}) collective-permute-start(bf16[16,2048]{1,0:T(8,128)(2,1)S(1)} %get-tuple-element.36), channel_id=1, source_target_pairs={{0,48},{2,50},{4,52},{6,54},{1,49},{3,51},{5,53},{7,55},{8,56},{10... | collective-permute-start | bytes 196616 | tf_op jit(solution)/shard_map/ppermute | solution.py:52
  14.4 4.7 %collective-permute-start.2 = (bf16[16,2048]{1,0:T(8,128)(2,1)S(1)}, bf16[16,2048]{1,0:T(8,128)(2,1)S(1)}, u32[]{:S(2)}, u32[]{:S(2)}) collective-permute-start(bf16[16,2048]{1,0:T(8,128)(2,1)S(1)} %get-tuple-element.36), channel_id=1, source_target_pairs={{0,8},{2,10},{4,12},{6,14},{1,9},{3,11},{5,13},{7,15},{8,0},{10,2}... | collective-permute-start | bytes 196616 | tf_op jit(solution)/shard_map/ppermute | solution.py:52
  15.5 4.3 %collective-permute-start.5 = (bf16[8,2048]{1,0:T(8,128)(2,1)S(1)}, bf16[8,2048]{1,0:T(8,128)(2,1)S(1)}, u32[]{:S(2)}, u32[]{:S(2)}) collective-permute-start(bf16[8,2048]{1,0:T(8,128)(2,1)S(1)} %get-tuple-element.39.own_ref), channel_id=1, source_target_pairs={{0,1},{2,3},{4,5},{6,7},{1,0},{3,2},{5,4},{7,6},{8,9},{10,11},{12,... | collective-permute-start | bytes 98312 | tf_op jit(solution)/shard_map/ppermute | solution.py:52
  19.8 5.2 %collective-permute-start.6 = (bf16[64,2048]{1,0:T(8,128)(2,1)S(1)}, bf16[64,2048]{1,0:T(8,128)(2,1)S(1)}, u32[]{:S(2)}, u32[]{:S(2)}) collective-permute-start(bf16[64,2048]{1,0:T(8,128)(2,1)S(1)} %pad_maximum_fusion.3), channel_id=1, source_target_pairs={{0,64},{2,6},{4,68},{6,2},{1,65},{3,7},{5,69},{7,3},{8,72},{10,14}... | collective-permute-start | bytes 786440 | tf_op jit(solution)/shard_map/ppermute | solution.py:52
  21.0 9.5 %collective-permute-start.9 = (bf16[64,2048]{1,0:T(8,128)(2,1)S(1)}, bf16[64,2048]{1,0:T(8,128)(2,1)S(1)}, u32[]{:S(2)}, u32[]{:S(2)}) collective-permute-start(bf16[64,2048]{1,0:T(8,128)(2,1)S(1)} %pad_maximum_fusion.3), channel_id=1, source_target_pairs={{0,192},{2,7},{4,196},{6,3},{1,193},{3,6},{5,197},{7,2},{8,200},{1... | collective-permute-start | bytes 786440 | tf_op jit(solution)/shard_map/ppermute | solution.py:52
  22.8 7.3 %collective-permute-start.8 = (bf16[64,2048]{1,0:T(8,128)(2,1)S(1)}, bf16[64,2048]{1,0:T(8,128)(2,1)S(1)}, u32[]{:S(2)}, u32[]{:S(2)}) collective-permute-start(bf16[64,2048]{1,0:T(8,128)(2,1)S(1)} %pad_maximum_fusion.3), channel_id=1, source_target_pairs={{0,128},{2,3},{4,132},{6,7},{1,129},{3,2},{5,133},{7,6},{8,136},{1... | collective-permute-start | bytes 786440 | tf_op jit(solution)/shard_map/ppermute | solution.py:52
  25.0 14.6 %collective-permute-start.11 = (bf16[128,2048]{1,0:T(8,128)(2,1)S(1)}, bf16[128,2048]{1,0:T(8,128)(2,1)S(1)}, u32[]{:S(2)}, u32[]{:S(2)}) collective-permute-start(bf16[128,2048]{1,0:T(8,128)(2,1)S(1)} %constant_dynamic-update-slice_fusion.top.refs_0_), channel_id=1, source_target_pairs={{0,5},{2,194},{4,1},{6,198},{1,4},{3,195},{5,0},{7,199},{8,13},{10... | collective-permute-start | bytes 1572872 | tf_op jit(solution)/shard_map/ppermute | solution.py:52
  27.9 11.8 %collective-permute-start.7 = (bf16[128,2048]{1,0:T(8,128)(2,1)S(1)}, bf16[128,2048]{1,0:T(8,128)(2,1)S(1)}, u32[]{:S(2)}, u32[]{:S(2)}) collective-permute-start(bf16[128,2048]{1,0:T(8,128)(2,1)S(1)} %constant_dynamic-update-slice_fusion.top.refs_0_), channel_id=1, source_target_pairs={{0,4},{2,66},{4,0},{6,70},{1,5},{3,67},{5,1},{7,71},{8,12},{10,74}... | collective-permute-start | bytes 1572872 | tf_op jit(solution)/shard_map/ppermute | solution.py:52
  30.6 15.0 %collective-permute-start.12 = (bf16[128,2048]{1,0:T(8,128)(2,1)S(1)}, bf16[128,2048]{1,0:T(8,128)(2,1)S(1)}, u32[]{:S(2)}, u32[]{:S(2)}) collective-permute-start(bf16[128,2048]{1,0:T(8,128)(2,1)S(1)} %constant_dynamic-update-slice_fusion.2.bottom.refs_1_), channel_id=1, source_target_pairs={{0,5},{2,194},{4,1},{6,198},{1,4},{3,195},{5,0},{7,199},{8,13},{10... | collective-permute-start | bytes 1572872 | tf_op jit(solution)/shard_map/ppermute | solution.py:52
  33.4 12.2 %collective-permute-start.10 = (bf16[128,2048]{1,0:T(8,128)(2,1)S(1)}, bf16[128,2048]{1,0:T(8,128)(2,1)S(1)}, u32[]{:S(2)}, u32[]{:S(2)}) collective-permute-start(bf16[128,2048]{1,0:T(8,128)(2,1)S(1)} %constant_dynamic-update-slice_fusion.2.bottom.refs_1_), channel_id=1, source_target_pairs={{0,4},{2,66},{4,0},{6,70},{1,5},{3,67},{5,1},{7,71},{8,12},{10,74}... | collective-permute-start | bytes 1572872 | tf_op jit(solution)/shard_map/ppermute | solution.py:52
  45.7 8.4 %collective-permute-start.15 = (bf16[256,2048]{1,0:T(8,128)(2,1)S(1)}, bf16[256,2048]{1,0:T(8,128)(2,1)S(1)}, u32[]{:S(2)}, u32[]{:S(2)}) collective-permute-start(bf16[256,2048]{1,0:T(8,128)(2,1)S(1)} %pad_maximum_fusion.2), channel_id=1, source_target_pairs={{0,2},{2,0},{4,6},{6,4},{1,3},{3,1},{5,7},{7,5},{8,10},{10,8},{12,... | collective-permute-start | bytes 3145736 | tf_op jit(solution)/shard_map/ppermute | solution.py:52
  50.1 3.9 %collective-permute-start.14 = (bf16[256,2048]{1,0:T(8,128)(2,1)S(1)}, bf16[256,2048]{1,0:T(8,128)(2,1)S(1)}, u32[]{:S(2)}, u32[]{:S(2)}) collective-permute-start(bf16[256,2048]{1,0:T(8,128)(2,1)S(1)} %pad_maximum_fusion), channel_id=1, source_target_pairs={{0,2},{2,0},{4,6},{6,4},{1,3},{3,1},{5,7},{7,5},{8,10},{10,8},{12,... | collective-permute-start | bytes 3145736 | tf_op jit(solution)/shard_map/ppermute | solution.py:52
  50.2 7.2 %collective-permute-start.13 = (bf16[256,2048]{1,0:T(8,128)(2,1)S(1)}, bf16[256,2048]{1,0:T(8,128)(2,1)S(1)}, u32[]{:S(2)}, u32[]{:S(2)}) collective-permute-start(bf16[256,2048]{1,0:T(8,128)(2,1)S(1)} %pad_maximum_fusion.1), channel_id=1, source_target_pairs={{0,2},{2,0},{4,6},{6,4},{1,3},{3,1},{5,7},{7,5},{8,10},{10,8},{12,... | collective-permute-start | bytes 3145736 | tf_op jit(solution)/shard_map/ppermute | solution.py:52
  50.7 9.0 %collective-permute-start.16 = (bf16[128,2048]{1,0:T(8,128)(2,1)S(1)}, bf16[128,2048]{1,0:T(8,128)(2,1)S(1)}, u32[]{:S(2)}, u32[]{:S(2)}) collective-permute-start(bf16[128,2048]{1,0:T(8,128)(2,1)S(1)} %collective-permute-done.11.refs_2_), channel_id=1, source_target_pairs={{0,4},{2,66},{4,0},{6,70},{1,5},{3,67},{5,1},{7,71},{8,12},{10,74}... | collective-permute-start | bytes 1572872 | tf_op jit(solution)/shard_map/ppermute | solution.py:52
  50.7 9.5 %collective-permute-start.17 = (bf16[128,2048]{1,0:T(8,128)(2,1)S(1)}, bf16[128,2048]{1,0:T(8,128)(2,1)S(1)}, u32[]{:S(2)}, u32[]{:S(2)}) collective-permute-start(bf16[128,2048]{1,0:T(8,128)(2,1)S(1)} %collective-permute-done.10.refs_1_), channel_id=1, source_target_pairs={{0,5},{2,194},{4,1},{6,198},{1,4},{3,195},{5,0},{7,199},{8,13},{10... | collective-permute-start | bytes 1572872 | tf_op jit(solution)/shard_map/ppermute | solution.py:52
  60.2 3.9 %collective-permute-start.18 = (bf16[128,2048]{1,0:T(8,128)(2,1)S(1)}, bf16[128,2048]{1,0:T(8,128)(2,1)S(1)}, u32[]{:S(2)}, u32[]{:S(2)}) collective-permute-start(bf16[128,2048]{1,0:T(8,128)(2,1)S(1)} %collective-permute-done.16.refs_2_), channel_id=1, source_target_pairs={{0,2},{2,0},{4,6},{6,4},{1,3},{3,1},{5,7},{7,5},{8,10},{10,8},{12,... | collective-permute-start | bytes 1572872 | tf_op jit(solution)/shard_map/ppermute | solution.py:52
  61.4 2.7 %collective-permute-start.19 = (bf16[128,2048]{1,0:T(8,128)(2,1)S(1)}, bf16[128,2048]{1,0:T(8,128)(2,1)S(1)}, u32[]{:S(2)}, u32[]{:S(2)}) collective-permute-start(bf16[128,2048]{1,0:T(8,128)(2,1)S(1)} %collective-permute-done.17.refs_3_), channel_id=1, source_target_pairs={{0,2},{2,0},{4,6},{6,4},{1,3},{3,1},{5,7},{7,5},{8,10},{10,8},{12,... | collective-permute-start | bytes 1572872 | tf_op jit(solution)/shard_map/ppermute | solution.py:52
